TPU v7x, 128 devices: a whole 4x4x4 slice. The times are simulated.
128 devices in a mesh: along: 16 (over z, x), cross: 8 (over y, core).
Axes of the slice: x: 4, y: 4, z: 4, core: 2. Of those that a mesh axis runs over, the one named last changes fastest.
Arguments:
- offsets: float32 [2, 64, 128, 128], P(None, 'along', 'cross'), may hold values from 0 to 1
- velocity: float32 [2, 64, 128, 128], P(None, 'along', 'cross'), may hold values from -6 to 6
- particle_mass: float32 [64, 128, 128], P('along', 'cross'), may hold values from 0.5 to 2
- neighbours: int32 [64, 128, 9], P('along', 'cross'), may hold values from -1 to 8, as said below
- owner_device: int32 [16, 8, 8192, 1], P('along', 'cross'), may hold values from 0 to 127; in each aligned block of 8192 rows (0 to 8191, 8192 to 16383, ..., all dimensions but the last counted through in order) at most 192 rows name the same one
- target_cell: int32 [16, 8, 8192], P('along', 'cross'), may hold values from 0 to 65535
- surface: float32 [3, 2048, 4096], P(None, 'along', 'cross'), may hold values from -6 to 6
- water_depth: float32 [2048, 4096], P('along', 'cross'), may hold values from 0.5 to 2
Outputs:
- grid_state: float32 [3, 2048, 4096], P(None, 'along', 'cross')
- density: float32 [64, 128, 128], P('along', 'cross')
- feedback: float32 [3, 64, 128, 128], P(None, 'along', 'cross')
Inputs may be any that keep to these rules, and one draw needn't show every extreme that they name: `owner_device`: in the rows of one device, at most 192 particles name one owner device (numbered as along index times 8 plus cross index), a bound that some block reaches. `neighbours`: slot 0 holds 4, the tile itself; the other slots hold distinct window positions or -1 for padding.
All inputs are finite; a program needn't handle non-finite values.
Results may differ from a plain program's by a relative error of at most 0.0003.
Values sent between devices are 32-bit elements; how exact they have to be, the bound alone decides.
A program may use at most 64 MiB of HBM per device.

v0:
```python
import jax
import jax.numpy as jnp
from jax import lax
from jax.sharding import PartitionSpec as P

SUBSTEPS = 4


courant = 0.4
kernel_width = 1.0


def padded_2(cells, sides, width):
    for axis, dim in sides:
        count = lax.axis_size(axis)
        ends = count - 1
        head = lax.slice_in_dim(cells, 0, width, axis=dim)
        tail = lax.slice_in_dim(cells, cells.shape[dim] - width, cells.shape[dim], axis=dim)
        cells = jnp.concatenate(
            [
                lax.ppermute(tail, axis, [(i, (i + 1) % count) for i in range(ends)]),
                cells,
                lax.ppermute(head, axis, [((i + 1) % count, i) for i in range(ends)]),
            ],
            axis=dim,
        )
    return cells


def tile_sums(window_rows, present_row):
    columns = window_rows.shape[2] - 2
    own_row = window_rows[:, 1, 1 : columns + 1, :]
    totals = jnp.zeros((3, columns, window_rows.shape[3]), jnp.float32)
    for window in range(9):
        row_shift = window // 3
        col_shift = window % 3
        nearby = window_rows[:, row_shift, col_shift : col_shift + columns, :]
        delta_x = own_row[0][:, :, None] - nearby[0][:, None, :] - (row_shift - 1.0)
        delta_y = own_row[1][:, :, None] - nearby[1][:, None, :] - (col_shift - 1.0)
        weights = jnp.exp(-(delta_x * delta_x + delta_y * delta_y) / kernel_width)
        weights = weights * present_row[:, window][:, None, None]
        carried = jnp.stack([nearby[4], nearby[4] * nearby[2], nearby[4] * nearby[3]])
        totals = totals + jnp.einsum(
            "tab,ktb->kta", weights, carried, precision=lax.Precision.HIGHEST
        )
    return totals


def particle_pass(padded, neighbours):
    rows = padded.shape[1] - 2
    present = jnp.any(neighbours[..., :, None] == jnp.arange(9, dtype=jnp.int32), axis=-2).astype(
        jnp.float32
    )

    def one_row(row_index):
        window_rows = lax.dynamic_slice_in_dim(padded, row_index, 3, 1)
        present_row = lax.dynamic_index_in_dim(present, row_index, 0, keepdims=False)
        return tile_sums(window_rows, present_row)

    return lax.map(one_row, jnp.arange(rows, dtype=jnp.int32))


def lax_friedrichs(state_pad, depth_pad):
    height = state_pad[0]
    speed_x = state_pad[1]
    speed_y = state_pad[2]
    flux_x = depth_pad * speed_x
    flux_y = depth_pad * speed_y

    def average(quantity):
        return 0.25 * (
            quantity[2:, 1:-1] + quantity[:-2, 1:-1] + quantity[1:-1, 2:] + quantity[1:-1, :-2]
        )

    next_height = average(height) - 0.5 * courant * (
        flux_x[2:, 1:-1] - flux_x[:-2, 1:-1] + flux_y[1:-1, 2:] - flux_y[1:-1, :-2]
    )
    next_speed_x = average(speed_x) - 0.5 * courant * (height[2:, 1:-1] - height[:-2, 1:-1])
    next_speed_y = average(speed_y) - 0.5 * courant * (height[1:-1, 2:] - height[1:-1, :-2])
    return jnp.stack([next_height, next_speed_x, next_speed_y])


def slot_ranks(destination, devices):
    particles = destination.shape[0]
    block = 128
    groups = particles // block
    onehot = (
        destination.reshape(groups, block)[:, :, None] == jnp.arange(devices, dtype=jnp.int32)
    ).astype(jnp.float32)
    lower = (jnp.arange(block)[:, None] > jnp.arange(block)[None, :]).astype(jnp.float32)
    earlier = jnp.einsum("ij,bjd->bid", lower, onehot, precision=lax.Precision.HIGHEST)
    counts = jnp.sum(onehot, axis=1)
    before = jnp.cumsum(counts, axis=0) - counts
    ranks = jnp.sum(onehot * (earlier + before[:, None, :]), axis=2)
    return ranks.reshape(-1).astype(jnp.int32)


def shards(
    offsets, velocity, particle_mass, neighbours, owner_device, target_cell, surface, water_depth
):
    tiles_along = offsets.shape[1]
    tiles_cross = offsets.shape[2]
    tile_size = offsets.shape[3]
    cells_along = surface.shape[1]
    cells_cross = surface.shape[2]
    cell_count = cells_along * cells_cross
    along_count = lax.axis_size("along")
    cross_count = lax.axis_size("cross")
    devices = along_count * cross_count
    stacked = jnp.concatenate([offsets, velocity, particle_mass[None]], axis=0)
    padded = padded_2(stacked, (("along", 1), ("cross", 2)), 1)
    totals = particle_pass(padded, neighbours)
    mass_sum = totals[:, 0]
    density = mass_sum / tile_size
    volume = particle_mass / density
    smooth_x = totals[:, 1] / mass_sum
    smooth_y = totals[:, 2] / mass_sum
    sources = jnp.stack([volume, volume * smooth_x, volume * smooth_y]).reshape(3, -1)
    destination = owner_device.reshape(-1)
    particles = destination.shape[0]
    capacity = 3 * particles // devices
    slot_total = devices * capacity
    slot_index = destination * capacity + slot_ranks(destination, devices)
    payload = jnp.concatenate([target_cell.reshape(1, -1).astype(jnp.float32), sources], axis=0)
    send_index = (
        jnp.arange(4, dtype=jnp.int32)[:, None] * slot_total + slot_index[None, :]
    ).reshape(-1)
    outgoing = jnp.zeros((4 * slot_total,), jnp.float32).at[send_index].set(payload.reshape(-1))
    outgoing = outgoing.reshape(4, devices, capacity)
    incoming = lax.all_to_all(
        outgoing, ("along", "cross"), split_axis=1, concat_axis=1, tiled=True
    ).reshape(4, -1)
    cells_in = incoming[0].astype(jnp.int32)
    cell_index = (jnp.arange(3, dtype=jnp.int32)[:, None] * cell_count + cells_in[None, :]).reshape(
        -1
    )
    grid_source = (
        jnp.zeros((3 * cell_count,), jnp.float32).at[cell_index].add(incoming[1:].reshape(-1))
    )
    grid_source = grid_source.reshape(3, cells_along, cells_cross)
    depth_pad = padded_2(water_depth, (("along", 0), ("cross", 1)), 1)
    water_state = surface
    for substep in range(SUBSTEPS):
        state_pad = padded_2(water_state, (("along", 1), ("cross", 2)), 1)
        water_state = lax_friedrichs(state_pad, depth_pad) + grid_source
    looked = water_state.reshape(-1)[cell_index].reshape(3, devices, capacity)
    returned = lax.all_to_all(
        looked, ("along", "cross"), split_axis=1, concat_axis=1, tiled=True
    ).reshape(-1)
    back_index = (
        jnp.arange(3, dtype=jnp.int32)[:, None] * slot_total + slot_index[None, :]
    ).reshape(-1)
    feedback = returned[back_index].reshape(3, tiles_along, tiles_cross, tile_size)
    return (water_state, density, feedback)


def solution(mesh):
    in_specs = (
        P(None, "along", "cross", None),
        P(None, "along", "cross", None),
        P("along", "cross", None),
        P("along", "cross", None),
        P("along", "cross", None, None),
        P("along", "cross", None),
        P(None, "along", "cross"),
        P("along", "cross"),
    )
    out_specs = (
        P(None, "along", "cross"),
        P("along", "cross", None),
        P(None, "along", "cross", None),
    )
    return jax.shard_map(shards, mesh=mesh, in_specs=in_specs, out_specs=out_specs, check_vma=False)
```

profile of v0, /device:TPU:1, one launch (start us, length us, event | category | flops | bytes accessed | tf_op | source)
XLA Modules:
  0.0 1516.4 jit_solution(8460796752312169972)
XLA Ops:
  1.4 3.9 collective-permute-start.8
  7.5 4.0 collective-permute-start
  13.6 4.0 collective-permute-start.4
  21.5 2.4 fusion.225
  25.9 5.2 collective-permute-start.2
  33.1 3.6 collective-permute-start.6
  40.0 3.6 collective-permute-start.10
  45.8 2.9 collective-permute-done.11
  48.8 92.7 %while.13 = (s32[]{:T(128)}, f32[4,3,16,128]{3,2,0,1:T(8,128)S(1)}, s32[4]{0:T(128)S(1)}, f32[5,6,18,128]{3,2,1,0:T(8,128)S(1)}, f32[4,16,9]{1,0,2:T(4,128)S(1)}...) while((s32[]{:T(128)}, f32[4,3,16,128]{3,2,0,1:T(8,128)S(1)}, ...), condition=%wide.region_5.6_spmd, body=%wide.region_4.5_spmd.sunk | while | flops 104792080 | bytes 2199840 | solution.py:60
  53.1 2.1 fusion.338
  55.2 2.1 convolution_add_fusion.15
  57.3 2.1 convolution_add_fusion.16
  59.4 2.1 convolution_add_fusion.17
  61.5 2.1 convolution_add_fusion.18
  63.6 2.1 convolution_add_fusion.19
  65.7 2.1 convolution_add_fusion.20
  67.8 2.1 convolution_add_fusion.21
  69.9 2.1 fusion.339
  76.2 2.1 fusion.338
  78.3 2.1 convolution_add_fusion.15
  80.4 2.1 convolution_add_fusion.16
  82.5 2.1 convolution_add_fusion.17
  84.6 2.1 convolution_add_fusion.18
  86.7 2.1 convolution_add_fusion.19
  88.8 2.1 convolution_add_fusion.20
  90.9 2.1 convolution_add_fusion.21
  93.0 2.1 fusion.339
  99.3 2.1 fusion.338
  101.4 2.1 convolution_add_fusion.15
  103.5 2.1 convolution_add_fusion.16
  105.6 2.1 convolution_add_fusion.17
  107.7 2.1 convolution_add_fusion.18
  109.8 2.1 convolution_add_fusion.19
  111.9 2.1 convolution_add_fusion.20
  114.0 2.1 convolution_add_fusion.21
  116.1 2.1 fusion.339
  122.4 2.1 fusion.338
  124.4 2.1 convolution_add_fusion.15
  126.6 2.1 convolution_add_fusion.16
  128.7 2.1 convolution_add_fusion.17
  130.8 2.1 convolution_add_fusion.18
  132.9 2.1 convolution_add_fusion.19
  135.0 2.1 convolution_add_fusion.20
  137.1 2.1 convolution_add_fusion.21
  139.2 2.1 fusion.339
  142.3 120.2 %scatter_custom_fusion = f32[98304]{0:T(1024)S(1)} fusion(s32[32768]{0:T(1024)S(1)} %bitcast.311, f32[32768]{0:T(1024)S(1)} %bitcast.312, f32[]{:T(128)} %constant.81.clone.1), kind=kCustom, calls=%fused_computation.420 | custom fusion | bytes 393220 | tf_op jit(solution)/shard_map/scatter | solution.py:128
  263.8 14.8 all-to-all-start
  281.2 11.0 all-to-all-done
  293.9 451.7 %scatter_custom_fusion.1 = f32[196608]{0:T(1024)S(1)} fusion(s32[73728]{0:T(1024)S(1)} %bitcast.295, f32[73728]{0:T(1024)S(1)} %reshape.839, f32[]{:T(128)} %constant.81.clone.1), kind=kCustom, calls=%fused_computation.320 | custom fusion | flops 73728 | bytes 786436 | tf_op jit(solution)/shard_map/scatter-add | solution.py:138
  746.0 21.0 %collective-permute-start.12 = (f32[3,1,512]{2,1,0:T(1,128)S(1)}, f32[3,1,512]{2,1,0:T(1,128)S(1)}, u32[]{:S(2)}, u32[]{:S(2)}) collective-permute-start(f32[3,1,512]{2,1,0:T(1,128)S(1)} %get-tuple-element.229), channel_id=1, source_target_pairs={{0,8},{8,16},{16,24},{24,32},{32,40},{40,48},{48,56},{56,64},{64,7... | collective-permute-start | bytes 18440 | tf_op jit(solution)/shard_map/ppermute | solution.py:21
  768.3 3.1 collective-permute-done.13
  771.5 19.6 %collective-permute-start.14 = (f32[3,130,1]{2,1,0:T(8,128)S(1)}, f32[3,130,1]{2,1,0:T(8,128)S(1)}, u32[]{:S(2)}, u32[]{:S(2)}) collective-permute-start(f32[3,130,1]{2,1,0:T(8,128)S(1)} %get-tuple-element.219), channel_id=1, source_target_pairs={{0,1},{1,2},{2,3},{3,4},{4,5},{5,6},{6,7},{8,9},{9,10},{10,11},{11... | collective-permute-start | bytes 4688 | tf_op jit(solution)/shard_map/ppermute | solution.py:21
  793.9 4.4 collective-permute-done.15
  803.3 3.1 collective-permute-done.17
  806.5 3.2 collective-permute-start.18
  812.4 4.4 collective-permute-done.19
  818.8 3.4 collective-permute-start.20
  823.7 3.2 collective-permute-done.21
  827.0 3.2 collective-permute-start.22
  832.7 4.7 collective-permute-done.23
  840.5 408.0 %gather_fusion = f32[73728]{0:T(1024)S(1)} fusion(f32[196608]{0:T(1024)S(1)} %add.530, s32[73728]{0:T(1024)S(1)} %broadcast_clamp_fusion), kind=kCustom, calls=%fused_computation | custom fusion | bytes 884736 | tf_op jit(solution)/shard_map/gather | solution.py:146
  1249.7 12.2 all-to-all-start.1
  1262.0 13.5 all-to-all-done.1
  1275.8 240.6 %gather_fusion.1 = f32[24576]{0:T(1024)} fusion(f32[73728]{0:T(1024)S(1)} %reshape.809, s32[24576]{0:T(1024)S(1)} %broadcast_clamp_fusion.1), kind=kCustom, calls=%fused_computation.1 | custom fusion | bytes 294912 | tf_op jit(solution)/shard_map/gather | solution.py:153
  (175 shorter events, 50.5 us)
Async XLA Ops:
  1.4 37.8 %collective-permute-start.8 = (f32[5,1,16,128]{3,2,1,0:T(8,128)S(1)}, f32[5,1,16,128]{3,2,1,0:T(8,128)S(1)}, u32[]{:S(2)}, u32[]{:S(2)}) collective-permute-start(f32[5,1,16,128]{3,2,1,0:T(8,128)S(1)} %get-tuple-element.247), channel_id=1, source_target_pairs={{0,8},{8,16},{16,24},{24,32},{32,40},{40,48},{48,56},{56,64},{64,7... | collective-permute-start | bytes 122888 | tf_op jit(solution)/shard_map/ppermute | solution.py:21
  5.4 33.9 %collective-permute-start.9 = (f32[5,1,16,128]{3,2,1,0:T(8,128)S(1)}, f32[5,1,16,128]{3,2,1,0:T(8,128)S(1)}, u32[]{:S(2)}, u32[]{:S(2)}) collective-permute-start(f32[5,1,16,128]{3,2,1,0:T(8,128)S(1)} %get-tuple-element.248), channel_id=1, source_target_pairs={{8,0},{16,8},{24,16},{32,24},{40,32},{48,40},{56,48},{64,56},{72,6... | collective-permute-start | bytes 122888 | tf_op jit(solution)/shard_map/ppermute | solution.py:23
  7.5 16.9 %collective-permute-start = (f32[3,1,512]{2,1,0:T(1,128)S(1)}, f32[3,1,512]{2,1,0:T(1,128)S(1)}, u32[]{:S(2)}, u32[]{:S(2)}) collective-permute-start(f32[3,1,512]{2,1,0:T(1,128)S(1)} %get-tuple-element.231), channel_id=1, source_target_pairs={{0,8},{8,16},{16,24},{24,32},{32,40},{40,48},{48,56},{56,64},{64,7... | collective-permute-start | bytes 18440 | tf_op jit(solution)/shard_map/ppermute | solution.py:21
  11.5 14.2 collective-permute-start.1
  13.6 17.5 %collective-permute-start.4 = (f32[1,512]{1,0:T(1,128)S(1)}, f32[1,512]{1,0:T(1,128)S(1)}, u32[]{:S(2)}, u32[]{:S(2)}) collective-permute-start(f32[1,512]{1,0:T(1,128)S(1)} %get-tuple-element.243), channel_id=1, source_target_pairs={{0,8},{8,16},{16,24},{24,32},{32,40},{40,48},{48,56},{56,64},{64,7... | collective-permute-start | bytes 6152 | tf_op jit(solution)/shard_map/ppermute | solution.py:21
  21.5 4.2 copy-start.1
  23.9 9.0 copy-start
  24.4 8.6 collective-permute-start.5
  25.9 10.9 collective-permute-start.2
  31.0 7.6 collective-permute-start.3
  33.1 12.5 collective-permute-start.6
  36.7 8.9 collective-permute-start.7
  39.1 0.8 copy-start.4
  39.1 0.9 copy-start.5
  39.1 0.9 copy-start.6
  40.0 5.8 collective-permute-start.10
  43.7 5.0 collective-permute-start.11
  263.8 28.4 %all-to-all-start = ((f32[4,128,192]{2,0,1:T(4,128)}), f32[4,128,192]{2,0,1:T(4,128)S(1)}, u32[]{:S(2)}, u32[]{:S(2)}) async-start(f32[4,128,192]{2,0,1:T(4,128)} %copy.75), calls=%async_computation | async-start | bytes 1048576 | tf_op jit(solution)/shard_map/all_to_all | solution.py:130
  293.9 451.9 %copy-start.2 = (f32[1,128,512]{2,1,0:T(8,128)S(1)}, f32[1,128,512]{2,1,0:T(8,128)}, u32[]{:S(2)}) copy-start(f32[1,128,512]{2,1,0:T(8,128)} %get-tuple-element.240) | copy-start | bytes 786436
  293.9 451.9 %copy-start.3 = (f32[1,128,512]{2,1,0:T(8,128)S(1)}, f32[1,128,512]{2,1,0:T(8,128)}, u32[]{:S(2)}) copy-start(f32[1,128,512]{2,1,0:T(8,128)} %fusion.262) | copy-start | bytes 786436
  746.0 22.3 %collective-permute-start.12 = (f32[3,1,512]{2,1,0:T(1,128)S(1)}, f32[3,1,512]{2,1,0:T(1,128)S(1)}, u32[]{:S(2)}, u32[]{:S(2)}) collective-permute-start(f32[3,1,512]{2,1,0:T(1,128)S(1)} %get-tuple-element.229), channel_id=1, source_target_pairs={{0,8},{8,16},{16,24},{24,32},{32,40},{40,48},{48,56},{56,64},{64,7... | collective-permute-start | bytes 18440 | tf_op jit(solution)/shard_map/ppermute | solution.py:21
  767.0 4.4 collective-permute-start.13
  771.5 22.3 %collective-permute-start.14 = (f32[3,130,1]{2,1,0:T(8,128)S(1)}, f32[3,130,1]{2,1,0:T(8,128)S(1)}, u32[]{:S(2)}, u32[]{:S(2)}) collective-permute-start(f32[3,130,1]{2,1,0:T(8,128)S(1)} %get-tuple-element.219), channel_id=1, source_target_pairs={{0,1},{1,2},{2,3},{3,4},{4,5},{5,6},{6,7},{8,9},{9,10},{10,11},{11... | collective-permute-start | bytes 4688 | tf_op jit(solution)/shard_map/ppermute | solution.py:21
  791.1 7.1 collective-permute-start.15
  800.3 3.0 collective-permute-start.16
  801.9 4.4 collective-permute-start.17
  806.5 5.9 collective-permute-start.18
  809.6 7.1 collective-permute-start.19
  818.8 4.9 collective-permute-start.20
  822.2 4.7 collective-permute-start.21
  827.0 5.6 collective-permute-start.22
  830.2 7.1 collective-permute-start.23
  1249.7 25.8 %all-to-all-start.1 = ((f32[3,128,192]{2,0,1:T(4,128)}), f32[3,128,192]{2,0,1:T(4,128)S(1)}, u32[]{:S(2)}, u32[]{:S(2)}) async-start(f32[3,128,192]{2,0,1:T(4,128)} %copy.77), calls=%async_computation.1 | async-start | bytes 1048576 | tf_op jit(solution)/shard_map/all_to_all | solution.py:147
where the time goes:
time: 1520 us
  local copies, waits for them, and re-layouts  778 us (51%)
  other arithmetic  470 us (31%)
  starting transfers between devices  123 us (8%)
  matrix products  78.2 us (5%)
  waiting for transfers between devices  52 us (3%)
    scatter-add x1, other arithmetic, shards(): jnp.zeros((3 * cell_count,), jnp.float32).at[cell_index]  452 us
    gather x1, local copies, waits for them, and re-layouts, shards(): looked = water_state.reshape(-1)[cell_index].reshape(3, devices, capacity)  408 us
    gather x1, local copies, waits for them, and re-layouts, shards(): returned[back_index].reshape(3, tiles_along, tiles_cross, tile_size)  241 us
    scatter x1, local copies, waits for them, and re-layouts, shards(): jnp.zeros((4 * slot_total,), jnp.float32).at[send_index]  120 us
    ppermute x12, starting transfers between devices, padded_2(): lax.ppermute(tail, axis, [(i, (i + 1) % count) for i in range(ends)])  76.4 us
    dot_general x36, matrix products, tile_sums(): jnp.einsum('tab,ktb->kta', weights, carried, precision=lax.Precision.HIGH...  75.8 us
  transfers between devices with their start and end apart: 26, of which 12 were waited for; matrix products, arithmetic and copies ran while one was open for 1% of the time, Pallas kernels for 0%

commit v1 on v0

v1 whole, which is shorter than its diff:
```python
import math

import jax
import jax.numpy as jnp
from jax import lax
from jax.experimental import pallas as pl
from jax.experimental.pallas import tpu as pltpu
from jax.sharding import PartitionSpec as P

SUBSTEPS = 4
KAPPA = math.sqrt(math.log2(math.e))
F32 = jnp.float32
BF16 = jnp.bfloat16
NN = (((1,), (0,)), ((), ()))
NT = (((1,), (1,)), ((), ()))
VMEM_LIMIT = 56 * 1024 * 1024

courant = 0.4


def dot(a, b, dims):
    return lax.dot_general(a, b, dims, preferred_element_type=F32)


def split2(x):
    hi = x.astype(BF16).astype(F32)
    return hi, x - hi


def iota(shape, dim):
    return lax.broadcasted_iota(jnp.int32, shape, dim)


def cross_rows(x, y, pattern, scale):
    q = iota((16, 128), 0)
    v = jnp.where(q < 6, jnp.broadcast_to(x, (16, 128)), jnp.broadcast_to(y, (16, 128)))
    hi, rest = split2(v)
    mid, low = split2(rest)
    out = jnp.zeros((16, 128), F32)
    for r, p in enumerate(pattern * 2):
        out = jnp.where(q == r, (hi, mid, low)[p], out)
    return (out * scale).astype(BF16)


def window_sums(pad_ref, present_ref, sums_ref, cols_ref):
    rows_pad, cols_pad = pad_ref.shape[1], pad_ref.shape[2]
    rows, cols = rows_pad - 2, cols_pad - 2

    def features(g, carry):
        i = g // cols_pad
        j = g - i * cols_pad
        x = pad_ref[0, i, pl.ds(j, 1), :] * KAPPA
        y = pad_ref[1, i, pl.ds(j, 1), :] * KAPPA
        feats = cross_rows(x, y, [0, 1, 0, 1, 2, 0], 2.0)
        cols_ref[g, :, 0:16] = feats.astype(F32).T.astype(BF16)
        return carry

    lax.fori_loop(0, rows_pad * cols_pad, features, 0)
    q16 = iota((16, 128), 0)
    kind = jnp.where(q16 >= 3, q16 - 3, q16)

    def tile(t, carry):
        i = t // cols
        j = t - i * cols
        x = pad_ref[0, i + 1, pl.ds(j + 1, 1), :] * KAPPA
        y = pad_ref[1, i + 1, pl.ds(j + 1, 1), :] * KAPPA
        own = cross_rows(x, y, [0, 0, 1, 1, 0, 2], 1.0)
        acc = jnp.zeros((16, 128), F32)
        for w in range(9):
            di, dj = w // 3, w % 3
            sx, sy = di - 1.0, dj - 1.0
            bi = i + di
            bj = j + dj
            weights = jnp.exp2(dot(cols_ref[bi * cols_pad + bj, :, 0:16], own, NN))
            hi = weights.astype(BF16)
            lo = (weights - hi.astype(F32)).astype(BF16)
            bx = pad_ref[0, bi, pl.ds(bj, 1), :] * KAPPA
            by = pad_ref[1, bi, pl.ds(bj, 1), :] * KAPPA
            vx = pad_ref[2, bi, pl.ds(bj, 1), :]
            vy = pad_ref[3, bi, pl.ds(bj, 1), :]
            mass = pad_ref[4, bi, pl.ds(bj, 1), :]
            b_part = mass * jnp.exp2(-2.0 * KAPPA * (sx * bx + sy * by) - bx * bx - by * by)
            rows16 = jnp.broadcast_to(b_part, (16, 128)) * jnp.where(
                kind == 0, 1.0, jnp.where(kind == 1, vx, vy)
            )
            c_hi, c_lo = split2(rows16)
            carried = jnp.where(q16 < 3, c_hi, jnp.where(q16 < 6, c_lo, 0.0)).astype(BF16)
            out = dot(
                jnp.concatenate([carried, carried], 1), jnp.concatenate([hi, lo], 0), NN
            )
            a_part = jnp.exp2(
                2.0 * KAPPA * (sx * x + sy * y)
                - x * x
                - y * y
                - KAPPA * KAPPA * (sx * sx + sy * sy)
            )
            acc = acc + out * (a_part * present_ref[t * 9 + w])
        for k in range(3):
            sums_ref[k, pl.ds(t, 1), :] = acc[k : k + 1] + acc[k + 3 : k + 4]
        return carry

    lax.fori_loop(0, rows * cols, tile, 0)


def pack(dest_ref, vals_ref, rank_ref, send_ref, left_ref, slots_ref, acc_ref):
    groups = dest_ref.shape[0] // 8
    d_iota = iota((128, 128), 0)
    before = jnp.concatenate(
        [
            (iota((128, 128), 0) < iota((128, 128), 1)).astype(F32),
            jnp.ones((128, 128), F32),
        ],
        1,
    ).astype(BF16)
    p_iota = iota((192, 128), 0).astype(F32)
    acc_ref[...] = jnp.zeros_like(acc_ref)

    def group(g, running):
        dest8 = dest_ref[pl.ds(g * 8, 8), :]
        vals8 = [split2(vals_ref[k, pl.ds(g * 8, 8), :]) for k in range(4)]
        ranks = []
        for r in range(8):
            hit = d_iota == jnp.broadcast_to(dest8[r : r + 1], (128, 128))
            counts = dot(jnp.where(hit, 1.0, 0.0).astype(BF16), before, NN)
            rank = jnp.sum(
                jnp.where(hit, counts[:, :128] + running, 0.0), axis=0, keepdims=True
            )
            running = running + counts[:, 128:]
            ranks.append(rank)
            lanes = slice(r * 128, r * 128 + 128)
            slots_ref[:, lanes] = jnp.where(
                p_iota == jnp.broadcast_to(rank, (192, 128)), 1.0, 0.0
            ).astype(BF16)
            for part in range(2):
                for k in range(4):
                    v = jnp.broadcast_to(vals8[k][part][r : r + 1], (128, 128))
                    at = (part * 4 + k) * 128
                    left_ref[at : at + 128, lanes] = jnp.where(hit, v, 0.0).astype(BF16)
        rank_ref[pl.ds(g * 8, 8), :] = jnp.concatenate(ranks, 0)
        acc_ref[:, 0:192] += dot(left_ref[...], slots_ref[...], NT)
        return running

    lax.fori_loop(0, groups, group, jnp.zeros((128, 128), F32))
    tails = []
    for k in range(4):
        send_ref[k] = acc_ref[k * 128 : k * 128 + 128, 0:128] + acc_ref[
            512 + k * 128 : 640 + k * 128, 0:128
        ]
        tails.append(
            acc_ref[k * 128 : k * 128 + 128, 128:256]
            + acc_ref[512 + k * 128 : 640 + k * 128, 128:256]
        )
    low_half = iota((128, 128), 1) < 64
    for h in range(2):
        send_ref[4 + h] = jnp.where(
            low_half, tails[2 * h], pltpu.roll(tails[2 * h + 1], 64, 1)
        )


def particles_kernel(
    pad_ref, present_ref, dest_ref, cell_ref,
    dens_ref, rank_ref, send_ref,
    sums_ref, cols_ref, vals_ref, left_ref, slots_ref, acc_ref,
):
    window_sums(pad_ref, present_ref, sums_ref, cols_ref)
    rows, cols = pad_ref.shape[1] - 2, pad_ref.shape[2] - 2
    for i in range(rows):
        at = slice(i * cols, (i + 1) * cols)
        s0 = sums_ref[0, at, :]
        density = s0 / 128.0
        dens_ref[at, :] = density
        volume = pad_ref[4, i + 1, 1 : cols + 1, :] / density
        vals_ref[0, at, :] = cell_ref[at, :].astype(F32)
        vals_ref[1, at, :] = volume
        vals_ref[2, at, :] = volume * (sums_ref[1, at, :] / s0)
        vals_ref[3, at, :] = volume * (sums_ref[2, at, :] / s0)
    pack(dest_ref, vals_ref, rank_ref, send_ref, left_ref, slots_ref, acc_ref)


def vmem():
    return pl.BlockSpec(memory_space=pltpu.VMEM)


def particles_call(pad, present, dest, cell):
    return pl.pallas_call(
        particles_kernel,
        out_shape=(
            jax.ShapeDtypeStruct((64, 128), F32),
            jax.ShapeDtypeStruct((64, 128), F32),
            jax.ShapeDtypeStruct((6, 128, 128), F32),
        ),
        in_specs=[vmem(), pl.BlockSpec(memory_space=pltpu.SMEM), vmem(), vmem()],
        out_specs=(vmem(), vmem(), vmem()),
        scratch_shapes=[
            pltpu.VMEM((3, 64, 128), F32),
            pltpu.VMEM((pad.shape[1] * pad.shape[2], 128, 128), BF16),
            pltpu.VMEM((4, 64, 128), F32),
            pltpu.VMEM((1024, 1024), BF16),
            pltpu.VMEM((192, 1024), BF16),
            pltpu.VMEM((1024, 256), F32),
        ],
        compiler_params=pltpu.CompilerParams(vmem_limit_bytes=VMEM_LIMIT),
        name="particles",
    )(pad, present, dest, cell)


def unfold(got_ref, out_ref, kinds):
    low_half = iota((64, 128), 1) < 64
    for k in range(kinds):
        out_ref[k, 0:128, :] = got_ref[k]
        row = got_ref[kinds + k // 2]
        first, second = row[0:64], row[64:128]
        if k % 2 == 0:
            out_ref[k, 128:192, :] = jnp.where(low_half, first, pltpu.roll(second, 64, 1))
        else:
            out_ref[k, 128:192, :] = jnp.where(low_half, pltpu.roll(first, 64, 1), second)


ROWS_STEP = 8


def row_and_column(cell):
    row = jnp.floor(cell * (1.0 / 512.0))
    return row, cell - row * 512.0


def deposit_kernel(got_ref, out_ref, slots_ref, left_ref, right_ref, acc_ref):
    unfold(got_ref, slots_ref, 4)
    acc_ref[...] = jnp.zeros_like(acc_ref)
    r_iota = iota((128, 128), 0).astype(F32)
    c_iota = iota((512, 128), 0).astype(F32)

    def step(g, carry):
        at = pl.ds(g * ROWS_STEP, ROWS_STEP)
        row8, col8 = row_and_column(slots_ref[0, at, :])
        vals8 = [split2(slots_ref[1 + k, at, :]) for k in range(3)]
        for r in range(ROWS_STEP):
            lanes = slice(r * 128, r * 128 + 128)
            hit = r_iota == jnp.broadcast_to(row8[r : r + 1], (128, 128))
            for part in range(2):
                for k in range(3):
                    v = jnp.broadcast_to(vals8[k][part][r : r + 1], (128, 128))
                    base = (part * 3 + k) * 128
                    left_ref[base : base + 128, lanes] = jnp.where(hit, v, 0.0).astype(BF16)
            right_ref[:, lanes] = jnp.where(
                c_iota == jnp.broadcast_to(col8[r : r + 1], (512, 128)), 1.0, 0.0
            ).astype(BF16)
        acc_ref[...] += dot(left_ref[...], right_ref[...], NT)
        return carry

    lax.fori_loop(0, 192 // ROWS_STEP, step, 0)
    for k in range(3):
        out_ref[k] = acc_ref[k * 128 : k * 128 + 128, :] + acc_ref[384 + k * 128 : 512 + k * 128, :]


def deposit_call(got):
    width = ROWS_STEP * 128
    return pl.pallas_call(
        deposit_kernel,
        out_shape=jax.ShapeDtypeStruct((3, 128, 512), F32),
        in_specs=[vmem()],
        out_specs=vmem(),
        scratch_shapes=[
            pltpu.VMEM((4, 192, 128), F32),
            pltpu.VMEM((768, width), BF16),
            pltpu.VMEM((512, width), BF16),
            pltpu.VMEM((768, 512), F32),
        ],
        compiler_params=pltpu.CompilerParams(vmem_limit_bytes=VMEM_LIMIT),
        name="deposit",
    )(got)


def lookup_kernel(got_ref, state_ref, back_ref, cells_ref, table_ref, found_ref):
    cells_ref[0:128, :] = got_ref[0]
    low_half = iota((64, 128), 1) < 64
    tail = got_ref[4]
    cells_ref[128:192, :] = jnp.where(low_half, tail[0:64], pltpu.roll(tail[64:128], 64, 1))
    for k in range(3):
        hi, lo = split2(state_ref[k])
        table_ref[k * 128 : k * 128 + 128, 0:512] = hi.astype(BF16)
        table_ref[k * 128 : k * 128 + 128, 512:1024] = lo.astype(BF16)
    r_iota = iota((128, 128), 0).astype(F32)
    c_iota = iota((512, 128), 0).astype(F32)

    def step(g, carry):
        at = pl.ds(g * 8, 8)
        row8, col8 = row_and_column(cells_ref[at, :])
        found = [[], [], []]
        for pair in range(4):
            right = jnp.concatenate(
                [
                    jnp.where(
                        c_iota == jnp.broadcast_to(col8[r : r + 1], (512, 128)), 1.0, 0.0
                    ).astype(BF16)
                    for r in (2 * pair, 2 * pair + 1)
                ],
                1,
            )
            got = dot(table_ref[...], jnp.concatenate([right, right], 0), NN)
            for k in range(3):
                for h in range(2):
                    r = 2 * pair + h
                    hit = r_iota == jnp.broadcast_to(row8[r : r + 1], (128, 128))
                    part = got[k * 128 : k * 128 + 128, h * 128 : h * 128 + 128]
                    found[k].append(jnp.sum(jnp.where(hit, part, 0.0), axis=0, keepdims=True))
        for k in range(3):
            found_ref[k, at, :] = jnp.concatenate(found[k], 0)
        return carry

    lax.fori_loop(0, 24, step, 0)
    tails = [found_ref[k, 128:192, :] for k in range(3)]
    for k in range(3):
        back_ref[k] = found_ref[k, 0:128, :]
    turned = [pltpu.roll(t, 64, 1) for t in tails]
    back_ref[3, 0:64, :] = jnp.where(low_half, tails[0], turned[1])
    back_ref[3, 64:128, :] = jnp.where(low_half, turned[0], tails[1])
    back_ref[4, 0:64, :] = tails[2]
    back_ref[4, 64:128, :] = turned[2]


def lookup_call(got, state):
    return pl.pallas_call(
        lookup_kernel,
        out_shape=jax.ShapeDtypeStruct((5, 128, 128), F32),
        in_specs=[vmem(), vmem()],
        out_specs=vmem(),
        scratch_shapes=[
            pltpu.VMEM((192, 128), F32),
            pltpu.VMEM((384, 1024), BF16),
            pltpu.VMEM((3, 192, 128), F32),
        ],
        compiler_params=pltpu.CompilerParams(vmem_limit_bytes=VMEM_LIMIT),
        name="lookup",
    )(got, state)


def unpack_kernel(back_ref, dest_ref, rank_ref, out_ref, table_ref):
    turned = pltpu.roll(back_ref[3], 64, 1)
    tails = [back_ref[3], turned, back_ref[4]]
    for k in range(3):
        for part, piece in enumerate(split2(back_ref[k])):
            table_ref[k * 128 : k * 128 + 128, part * 192 : part * 192 + 128] = piece.astype(BF16)
        for part, piece in enumerate(split2(tails[k])):
            table_ref[
                k * 128 : k * 128 + 128, part * 192 + 128 : part * 192 + 192
            ] = piece[:, 0:64].astype(BF16)
    d_iota = iota((128, 128), 0)
    p_iota = iota((192, 128), 0).astype(F32)

    def step(g, carry):
        at = pl.ds(g * 8, 8)
        dest8 = dest_ref[at, :]
        rank8 = rank_ref[at, :]
        found = [[], [], []]
        for pair in range(4):
            slots = jnp.concatenate(
                [
                    jnp.where(
                        p_iota == jnp.broadcast_to(rank8[r : r + 1], (192, 128)), 1.0, 0.0
                    ).astype(BF16)
                    for r in (2 * pair, 2 * pair + 1)
                ],
                1,
            )
            got = dot(table_ref[...], jnp.concatenate([slots, slots], 0), NN)
            for k in range(3):
                for h in range(2):
                    r = 2 * pair + h
                    hit = d_iota == jnp.broadcast_to(dest8[r : r + 1], (128, 128))
                    part = got[k * 128 : k * 128 + 128, h * 128 : h * 128 + 128]
                    found[k].append(jnp.sum(jnp.where(hit, part, 0.0), axis=0, keepdims=True))
        for k in range(3):
            out_ref[k, at, :] = jnp.concatenate(found[k], 0)
        return carry

    lax.fori_loop(0, dest_ref.shape[0] // 8, step, 0)


def unpack_call(back, dest, rank):
    return pl.pallas_call(
        unpack_kernel,
        out_shape=jax.ShapeDtypeStruct((3, 64, 128), F32),
        in_specs=[vmem(), vmem(), vmem()],
        out_specs=vmem(),
        scratch_shapes=[pltpu.VMEM((384, 384), BF16)],
        compiler_params=pltpu.CompilerParams(vmem_limit_bytes=VMEM_LIMIT),
        name="unpack",
    )(back, dest, rank)


def padded_2(cells, sides, width):
    for axis, dim in sides:
        count = lax.axis_size(axis)
        ends = count - 1
        head = lax.slice_in_dim(cells, 0, width, axis=dim)
        tail = lax.slice_in_dim(cells, cells.shape[dim] - width, cells.shape[dim], axis=dim)
        cells = jnp.concatenate(
            [
                lax.ppermute(tail, axis, [(i, (i + 1) % count) for i in range(ends)]),
                cells,
                lax.ppermute(head, axis, [((i + 1) % count, i) for i in range(ends)]),
            ],
            axis=dim,
        )
    return cells


def lax_friedrichs(state_pad, depth_pad):
    height = state_pad[0]
    speed_x = state_pad[1]
    speed_y = state_pad[2]
    flux_x = depth_pad * speed_x
    flux_y = depth_pad * speed_y

    def average(quantity):
        return 0.25 * (
            quantity[2:, 1:-1] + quantity[:-2, 1:-1] + quantity[1:-1, 2:] + quantity[1:-1, :-2]
        )

    next_height = average(height) - 0.5 * courant * (
        flux_x[2:, 1:-1] - flux_x[:-2, 1:-1] + flux_y[1:-1, 2:] - flux_y[1:-1, :-2]
    )
    next_speed_x = average(speed_x) - 0.5 * courant * (height[2:, 1:-1] - height[:-2, 1:-1])
    next_speed_y = average(speed_y) - 0.5 * courant * (height[1:-1, 2:] - height[1:-1, :-2])
    return jnp.stack([next_height, next_speed_x, next_speed_y])


def shards(
    offsets, velocity, particle_mass, neighbours, owner_device, target_cell, surface, water_depth
):
    stacked = jnp.concatenate([offsets, velocity, particle_mass[None]], axis=0)
    padded = padded_2(stacked, (("along", 1), ("cross", 2)), 1)
    present = jnp.any(
        neighbours[..., :, None] == jnp.arange(9, dtype=jnp.int32), axis=-2
    ).astype(F32)
    dest = owner_device.reshape(64, 128)
    cell = target_cell.reshape(64, 128)
    density, rank, send = particles_call(padded, present.reshape(-1), dest, cell)
    got = lax.all_to_all(send, ("along", "cross"), split_axis=1, concat_axis=1, tiled=True)
    grid_source = deposit_call(got)
    depth_pad = padded_2(water_depth, (("along", 0), ("cross", 1)), 1)
    water_state = surface
    for substep in range(SUBSTEPS):
        state_pad = padded_2(water_state, (("along", 1), ("cross", 2)), 1)
        water_state = lax_friedrichs(state_pad, depth_pad) + grid_source
    back = lookup_call(got, water_state)
    back = lax.all_to_all(back, ("along", "cross"), split_axis=1, concat_axis=1, tiled=True)
    feedback = unpack_call(back, dest, rank)
    return (
        water_state,
        density.reshape(particle_mass.shape),
        feedback.reshape((3,) + particle_mass.shape),
    )


def solution(mesh):
    in_specs = (
        P(None, "along", "cross", None),
        P(None, "along", "cross", None),
        P("along", "cross", None),
        P("along", "cross", None),
        P("along", "cross", None, None),
        P("along", "cross", None),
        P(None, "along", "cross"),
        P("along", "cross"),
    )
    out_specs = (
        P(None, "along", "cross"),
        P("along", "cross", None),
        P(None, "along", "cross", None),
    )
    return jax.shard_map(shards, mesh=mesh, in_specs=in_specs, out_specs=out_specs, check_vma=False)
```

time: 1520 us -> 280 us (0.18)
  local copies, waits for them, and re-layouts: 778 us -> 8.72 us
  other arithmetic: 470 us -> 13 us
  Pallas kernels: 0 us -> 115 us
  matrix products: 78.2 us -> 0 us
  starting transfers between devices: 123 us -> 77.9 us
  blocking collectives: 0 us -> 22.6 us
    gather x2 -> x0, local copies, waits for them, and re-layouts: 649 us -> none  [the longest x1 408 us: shards(): looked = water_state.reshape(-1)[cell_index].reshape(3, devices, capacity)]
    scatter-add x1 -> x0, other arithmetic: 452 us -> none  [shards(): jnp.zeros((3 * cell_count,), jnp.float32).at[cell_index]]
    scatter x1 -> x0, local copies, waits for them, and re-layouts: 120 us -> none  [shards(): jnp.zeros((4 * slot_total,), jnp.float32).at[send_index]]
    pallas_call x0 -> x4, Pallas kernels: none -> 115 us  [the longest x1 51.1 us: particles_call(): pl.pallas_call(particles_kernel, out_shape=(jax.ShapeDtypeStruct((64, 128...]
    dot_general x37 -> x0, matrix products: 78.2 us -> none  [the longest x36 75.8 us: tile_sums(): jnp.einsum('tab,ktb->kta', weights, carried, precision=lax.Precision.HIGH...]
    ppermute x12, starting transfers between devices: 76.4 us -> 43.3 us  [padded_2(): lax.ppermute(tail, axis, [(i, (i + 1) % count) for i in range(ends)])]
    all_to_all x0 -> x1, blocking collectives: none -> 22.6 us  [shards(): lax.all_to_all(back, ('along', 'cross'), split_axis=1, concat_axis=1, til...]
  transfers between devices with their start and end apart: 26 -> 25, of which waited for: 12 -> 11; matrix products, arithmetic and copies ran while one was open for 1% -> 2% of each run, Pallas kernels for 0% -> 0%
where the time goes in v1:
time: 280 us; the launch traced here: 278 us
  Pallas kernels  115 us (41%)
  starting transfers between devices  77.9 us (28%)
  waiting for transfers between devices  40 us (14%)
  blocking collectives  22.6 us (8%)
  other arithmetic  13 us (5%)
  local copies, waits for them, and re-layouts  8.72 us (3%)
    pallas_call x1, Pallas kernels, particles_call(): pl.pallas_call(particles_kernel, out_shape=(jax.ShapeDtypeStruct((64, 128...  51.1 us
    ppermute x12, starting transfers between devices, padded_2(): lax.ppermute(tail, axis, [(i, (i + 1) % count) for i in range(ends)])  43.3 us
    pallas_call x1, Pallas kernels, deposit_call(): pl.pallas_call(deposit_kernel, out_shape=jax.ShapeDtypeStruct((3, 128, 51...  30.1 us
    pallas_call x1, Pallas kernels, lookup_call(): pl.pallas_call(lookup_kernel, out_shape=jax.ShapeDtypeStruct((5, 128, 128...  27 us
    ppermute x12, waiting for transfers between devices, padded_2(): lax.ppermute(head, axis, [((i + 1) % count, i) for i in range(ends)])  25.6 us
    all_to_all x1, blocking collectives, shards(): lax.all_to_all(back, ('along', 'cross'), split_axis=1, concat_axis=1, til...  22.6 us
    ppermute x12, starting transfers between devices, padded_2(): lax.ppermute(head, axis, [((i + 1) % count, i) for i in range(ends)])  19.8 us
    all_to_all x1, starting transfers between devices, shards(): lax.all_to_all(send, ('along', 'cross'), split_axis=1, concat_axis=1, til...  14.9 us
  transfers between devices with their start and end apart: 25, of which 11 were waited for; matrix products, arithmetic and copies ran while one was open for 2% of the time, Pallas kernels for 0%

profile of v1, /device:TPU:1, one launch (start us, length us, event | category | flops | bytes accessed | tf_op | source)
XLA Modules:
  0.0 278.3 jit_solution(1744774974440710167)
XLA Ops:
  0.6 0.8 fusion.48
  1.5 3.9 %collective-permute-start = (f32[3,1,512]{2,1,0:T(1,128)S(1)}, f32[3,1,512]{2,1,0:T(1,128)S(1)}, u32[]{:S(2)}, u32[]{:S(2)}) collective-permute-start(f32[3,1,512]{2,1,0:T(1,128)S(1)} %get-tuple-element.43), channel_id=1, source_target_pairs={{0,8},{8,16},{16,24},{24,32},{32,40},{40,48},{48,56},{56,64},{64,7... | collective-permute-start | bytes 18440 | tf_op jit(solution)/shard_map/ppermute | solution.py:400
  5.4 1.3 collective-permute-start.1
  6.7 0.7 fusion.49
  7.5 4.0 %collective-permute-start.4 = (f32[1,512]{1,0:T(1,128)S(1)}, f32[1,512]{1,0:T(1,128)S(1)}, u32[]{:S(2)}, u32[]{:S(2)}) collective-permute-start(f32[1,512]{1,0:T(1,128)S(1)} %get-tuple-element.55), channel_id=1, source_target_pairs={{0,8},{8,16},{16,24},{24,32},{32,40},{40,48},{48,56},{56,64},{64,7... | collective-permute-start | bytes 6152 | tf_op jit(solution)/shard_map/ppermute | solution.py:400
  11.5 1.3 collective-permute-start.5
  12.8 0.8 pad_maximum_fusion.23
  13.6 4.0 %collective-permute-start.8 = (f32[5,1,16,128]{3,2,1,0:T(8,128)S(1)}, f32[5,1,16,128]{3,2,1,0:T(8,128)S(1)}, u32[]{:S(2)}, u32[]{:S(2)}) collective-permute-start(f32[5,1,16,128]{3,2,1,0:T(8,128)S(1)} %get-tuple-element.59), channel_id=1, source_target_pairs={{0,8},{8,16},{16,24},{24,32},{32,40},{40,48},{48,56},{56,64},{64,7... | collective-permute-start | bytes 122888 | tf_op jit(solution)/shard_map/ppermute | solution.py:400
  17.7 0.7 reshape.27.present_ref
  18.5 1.4 collective-permute-start.9
  19.9 1.2 pad_maximum_fusion.17
  21.1 5.2 %collective-permute-start.2 = (f32[3,130,1]{2,1,0:T(8,128)S(1)}, f32[3,130,1]{2,1,0:T(8,128)S(1)}, u32[]{:S(2)}, u32[]{:S(2)}) collective-permute-start(f32[3,130,1]{2,1,0:T(8,128)S(1)} %get-tuple-element.35), channel_id=1, source_target_pairs={{0,1},{1,2},{2,3},{3,4},{4,5},{5,6},{6,7},{8,9},{9,10},{10,11},{11... | collective-permute-start | bytes 4688 | tf_op jit(solution)/shard_map/ppermute | solution.py:400
  26.3 1.9 collective-permute-start.3
  28.3 3.6 %collective-permute-start.6 = (f32[130,1]{1,0:T(8,128)S(1)}, f32[130,1]{1,0:T(8,128)S(1)}, u32[]{:S(2)}, u32[]{:S(2)}) collective-permute-start(f32[130,1]{1,0:T(8,128)S(1)} %get-tuple-element.53), channel_id=1, source_target_pairs={{0,1},{1,2},{2,3},{3,4},{4,5},{5,6},{6,7},{8,9},{9,10},{10,11},{11... | collective-permute-start | bytes 1568 | tf_op jit(solution)/shard_map/ppermute | solution.py:400
  32.0 1.9 collective-permute-start.7
  33.9 0.4 pad_maximum_fusion
  34.5 0.7 copy-done.3
  35.3 3.6 %collective-permute-start.10 = (f32[5,6,1,128]{3,2,1,0:T(1,128)S(1)}, f32[5,6,1,128]{3,2,1,0:T(1,128)S(1)}, u32[]{:S(2)}, u32[]{:S(2)}) collective-permute-start(f32[5,6,1,128]{3,2,1,0:T(1,128)S(1)} %get-tuple-element.57), channel_id=1, source_target_pairs={{0,1},{1,2},{2,3},{3,4},{4,5},{5,6},{6,7},{8,9},{9,10},{10,11},{11... | collective-permute-start | bytes 46088 | tf_op jit(solution)/shard_map/ppermute | solution.py:400
  38.9 1.9 collective-permute-start.11
  41.1 2.9 %collective-permute-done.11 = f32[5,6,1,128]{3,2,1,0:T(1,128)S(1)} collective-permute-done((f32[5,6,1,128]{3,2,1,0:T(1,128)S(1)}, f32[5,6,1,128]{3,2,1,0:T(1,128)S(1)}, u32[]{:S(2)}, u32[]{:S(2)}) %collective-permute-start.11) | collective-permute-done | bytes 15392 | tf_op jit(solution)/shard_map/ppermute | solution.py:402
  44.0 0.8 pad_maximum_fusion.4.pad_ref
  44.8 51.1 %particles.1 = (f32[64,128]{1,0:T(8,128)}, f32[64,128]{1,0:T(8,128)}, f32[6,128,128]{2,1,0:T(8,128)}) custom-call(f32[5,6,18,128]{3,2,1,0:T(8,128)} %pad_maximum_fusion.4.pad_ref, f32[576]{0:T(1024)} %reshape.27.present_ref, s32[64,128]{1,0:T(8,128)} %bitcast.72, s32[64,128]{1,0:T(8,128)} %bitcast.75), custom_call_target="tpu_custom_call" | custom-call | tf_op jit(solution)/shard_map/particles/pallas_call | solution.py:185
  95.9 2.0 copy.20
  97.9 14.9 %all-to-all-start = ((f32[6,128,128]{2,0,1:T(8,128)}), f32[6,128,128]{2,0,1:T(8,128)S(1)}, u32[]{:S(2)}, u32[]{:S(2)}) async-start(f32[6,128,128]{2,0,1:T(8,128)} %copy.20), calls=%async_computation | async-start | bytes 1048576 | tf_op jit(solution)/shard_map/all_to_all | solution.py:440
  112.8 0.4 fusion.32
  113.2 0.7 fusion.35
  113.9 12.4 %all-to-all-done = f32[6,128,128]{2,0,1:T(8,128)S(1)} async-done(((f32[6,128,128]{2,0,1:T(8,128)}), f32[6,128,128]{2,0,1:T(8,128)S(1)}, u32[]{:S(2)}, u32[]{:S(2)}) %all-to-all-start) | async-done | bytes 393248 | tf_op jit(solution)/shard_map/all_to_all | solution.py:440
  126.3 0.8 copy.21.got_ref
  127.1 30.1 %deposit.1 = f32[3,128,512]{2,1,0:T(8,128)} custom-call(f32[6,128,128]{2,1,0:T(8,128)} %copy.21.got_ref), custom_call_target="tpu_custom_call" | custom-call | tf_op jit(solution)/shard_map/deposit/pallas_call | solution.py:258
  157.2 1.3 maximum_add_fusion
  158.6 2.2 collective-permute-start.12
  160.7 1.3 collective-permute-start.13
  162.0 3.1 %collective-permute-done.13 = f32[3,1,512]{2,1,0:T(1,128)S(1)} collective-permute-done((f32[3,1,512]{2,1,0:T(1,128)S(1)}, f32[3,1,512]{2,1,0:T(1,128)S(1)}, u32[]{:S(2)}, u32[]{:S(2)}) %collective-permute-start.13) | collective-permute-done | bytes 6176 | tf_op jit(solution)/shard_map/ppermute | solution.py:402
  165.2 3.7 %collective-permute-start.14 = (f32[3,130,1]{2,1,0:T(8,128)S(1)}, f32[3,130,1]{2,1,0:T(8,128)S(1)}, u32[]{:S(2)}, u32[]{:S(2)}) collective-permute-start(f32[3,130,1]{2,1,0:T(8,128)S(1)} %get-tuple-element.33), channel_id=1, source_target_pairs={{0,1},{1,2},{2,3},{3,4},{4,5},{5,6},{6,7},{8,9},{9,10},{10,11},{11... | collective-permute-start | bytes 4688 | tf_op jit(solution)/shard_map/ppermute | solution.py:400
  168.9 2.1 collective-permute-start.15
  171.1 0.6 collective-permute-done.14
  171.7 4.4 %collective-permute-done.15 = f32[3,130,1]{2,1,0:T(8,128)S(1)} collective-permute-done((f32[3,130,1]{2,1,0:T(8,128)S(1)}, f32[3,130,1]{2,1,0:T(8,128)S(1)}, u32[]{:S(2)}, u32[]{:S(2)}) %collective-permute-start.15) | collective-permute-done | bytes 1592 | tf_op jit(solution)/shard_map/ppermute | solution.py:402
  176.1 0.4 pad_maximum_fusion.1
  176.6 0.4 fusion.23
  177.2 0.7 fusion.26
  178.5 2.9 %collective-permute-start.16 = (f32[3,1,512]{2,1,0:T(1,128)S(1)}, f32[3,1,512]{2,1,0:T(1,128)S(1)}, u32[]{:S(2)}, u32[]{:S(2)}) collective-permute-start(f32[3,1,512]{2,1,0:T(1,128)S(1)} %get-tuple-element.39), channel_id=1, source_target_pairs={{0,8},{8,16},{16,24},{24,32},{32,40},{40,48},{48,56},{56,64},{64,7... | collective-permute-start | bytes 18440 | tf_op jit(solution)/shard_map/ppermute | solution.py:400
  181.4 1.3 collective-permute-start.17
  182.7 3.1 %collective-permute-done.17 = f32[3,1,512]{2,1,0:T(1,128)S(1)} collective-permute-done((f32[3,1,512]{2,1,0:T(1,128)S(1)}, f32[3,1,512]{2,1,0:T(1,128)S(1)}, u32[]{:S(2)}, u32[]{:S(2)}) %collective-permute-start.17) | collective-permute-done | bytes 6176 | tf_op jit(solution)/shard_map/ppermute | solution.py:402
  185.9 3.2 %collective-permute-start.18 = (f32[3,130,1]{2,1,0:T(8,128)S(1)}, f32[3,130,1]{2,1,0:T(8,128)S(1)}, u32[]{:S(2)}, u32[]{:S(2)}) collective-permute-start(f32[3,130,1]{2,1,0:T(8,128)S(1)} %get-tuple-element.31), channel_id=1, source_target_pairs={{0,1},{1,2},{2,3},{3,4},{4,5},{5,6},{6,7},{8,9},{9,10},{10,11},{11... | collective-permute-start | bytes 4688 | tf_op jit(solution)/shard_map/ppermute | solution.py:400
  189.1 2.1 collective-permute-start.19
  191.3 0.6 collective-permute-done.18
  191.9 4.4 %collective-permute-done.19 = f32[3,130,1]{2,1,0:T(8,128)S(1)} collective-permute-done((f32[3,130,1]{2,1,0:T(8,128)S(1)}, f32[3,130,1]{2,1,0:T(8,128)S(1)}, u32[]{:S(2)}, u32[]{:S(2)}) %collective-permute-start.19) | collective-permute-done | bytes 1592 | tf_op jit(solution)/shard_map/ppermute | solution.py:402
  196.3 0.4 pad_maximum_fusion.2
  197.4 0.7 fusion.17
  198.3 4.1 %collective-permute-start.20 = (f32[3,1,512]{2,1,0:T(1,128)S(1)}, f32[3,1,512]{2,1,0:T(1,128)S(1)}, u32[]{:S(2)}, u32[]{:S(2)}) collective-permute-start(f32[3,1,512]{2,1,0:T(1,128)S(1)} %get-tuple-element.37), channel_id=1, source_target_pairs={{0,8},{8,16},{16,24},{24,32},{32,40},{40,48},{48,56},{56,64},{64,7... | collective-permute-start | bytes 18440 | tf_op jit(solution)/shard_map/ppermute | solution.py:400
  202.4 1.3 collective-permute-start.21
  203.7 3.3 %collective-permute-done.21 = f32[3,1,512]{2,1,0:T(1,128)S(1)} collective-permute-done((f32[3,1,512]{2,1,0:T(1,128)S(1)}, f32[3,1,512]{2,1,0:T(1,128)S(1)}, u32[]{:S(2)}, u32[]{:S(2)}) %collective-permute-start.21) | collective-permute-done | bytes 6176 | tf_op jit(solution)/shard_map/ppermute | solution.py:402
  207.2 2.9 %collective-permute-start.22 = (f32[3,130,1]{2,1,0:T(8,128)S(1)}, f32[3,130,1]{2,1,0:T(8,128)S(1)}, u32[]{:S(2)}, u32[]{:S(2)}) collective-permute-start(f32[3,130,1]{2,1,0:T(8,128)S(1)} %get-tuple-element.29), channel_id=1, source_target_pairs={{0,1},{1,2},{2,3},{3,4},{4,5},{5,6},{6,7},{8,9},{9,10},{10,11},{11... | collective-permute-start | bytes 4688 | tf_op jit(solution)/shard_map/ppermute | solution.py:400
  210.1 1.9 collective-permute-start.23
  212.0 0.8 collective-permute-done.22
  212.8 4.4 %collective-permute-done.23 = f32[3,130,1]{2,1,0:T(8,128)S(1)} collective-permute-done((f32[3,130,1]{2,1,0:T(8,128)S(1)}, f32[3,130,1]{2,1,0:T(8,128)S(1)}, u32[]{:S(2)}, u32[]{:S(2)}) %collective-permute-start.23) | collective-permute-done | bytes 1592 | tf_op jit(solution)/shard_map/ppermute | solution.py:402
  217.2 0.4 pad_maximum_fusion.3
  218.3 0.7 fusion.8
  219.1 1.0 maximum_add_fusion.3.state_ref
  220.1 27.0 %lookup.1 = f32[5,128,128]{2,1,0:T(8,128)} custom-call(f32[6,128,128]{2,1,0:T(8,128)} %copy.21.got_ref, f32[3,128,512]{2,1,0:T(8,128)} %maximum_add_fusion.3.state_ref), custom_call_target="tpu_custom_call" | custom-call | tf_op jit(solution)/shard_map/lookup/pallas_call | solution.py:323
  247.1 1.2 copy.23
  248.3 22.6 %all_to_all.10 = f32[5,128,128]{2,0,1:T(8,128)S(1)} all-to-all(f32[5,128,128]{2,0,1:T(8,128)S(1)} %copy.23), channel_id=1, replica_groups=mesh['along'=16,'cross'=8] {'along','cross'}, dimensions={1} | all-to-all | bytes 655360 | tf_op jit(solution)/shard_map/all_to_all | solution.py:448
  270.9 0.8 copy.24.back_ref
  271.6 6.6 %unpack.1 = f32[3,64,128]{2,1,0:T(8,128)} custom-call(f32[5,128,128]{2,1,0:T(8,128)} %copy.24.back_ref, s32[64,128]{1,0:T(8,128)} %bitcast.73, f32[64,128]{1,0:T(8,128)} %get-tuple-element.8.rank_ref), custom_call_target="tpu_custom_call" | custom-call | tf_op jit(solution)/shard_map/unpack/pallas_call | solution.py:381
  (50 shorter events, 3.4 us)
Async XLA Ops:
  0.6 12.1 %copy-start.5 = (f32[4,16,128]{2,1,0:T(8,128)S(1)}, f32[4,16,128]{2,1,0:T(8,128)}, u32[]{:S(2)}) copy-start(f32[4,16,128]{2,1,0:T(8,128)} %param.10) | copy-start | bytes 98308
  1.5 17.0 %collective-permute-start = (f32[3,1,512]{2,1,0:T(1,128)S(1)}, f32[3,1,512]{2,1,0:T(1,128)S(1)}, u32[]{:S(2)}, u32[]{:S(2)}) collective-permute-start(f32[3,1,512]{2,1,0:T(1,128)S(1)} %get-tuple-element.43), channel_id=1, source_target_pairs={{0,8},{8,16},{16,24},{24,32},{32,40},{40,48},{48,56},{56,64},{64,7... | collective-permute-start | bytes 18440 | tf_op jit(solution)/shard_map/ppermute | solution.py:400
  5.4 14.5 %collective-permute-start.1 = (f32[3,1,512]{2,1,0:T(1,128)S(1)}, f32[3,1,512]{2,1,0:T(1,128)S(1)}, u32[]{:S(2)}, u32[]{:S(2)}) collective-permute-start(f32[3,1,512]{2,1,0:T(1,128)S(1)} %get-tuple-element.44), channel_id=1, source_target_pairs={{8,0},{16,8},{24,16},{32,24},{40,32},{48,40},{56,48},{64,56},{72,6... | collective-permute-start | bytes 18440 | tf_op jit(solution)/shard_map/ppermute | solution.py:402
  7.5 18.8 %collective-permute-start.4 = (f32[1,512]{1,0:T(1,128)S(1)}, f32[1,512]{1,0:T(1,128)S(1)}, u32[]{:S(2)}, u32[]{:S(2)}) collective-permute-start(f32[1,512]{1,0:T(1,128)S(1)} %get-tuple-element.55), channel_id=1, source_target_pairs={{0,8},{8,16},{16,24},{24,32},{32,40},{40,48},{48,56},{56,64},{64,7... | collective-permute-start | bytes 6152 | tf_op jit(solution)/shard_map/ppermute | solution.py:400
  11.5 16.7 %collective-permute-start.5 = (f32[1,512]{1,0:T(1,128)S(1)}, f32[1,512]{1,0:T(1,128)S(1)}, u32[]{:S(2)}, u32[]{:S(2)}) collective-permute-start(f32[1,512]{1,0:T(1,128)S(1)} %get-tuple-element.56), channel_id=1, source_target_pairs={{8,0},{16,8},{24,16},{32,24},{40,32},{48,40},{56,48},{64,56},{72,6... | collective-permute-start | bytes 6152 | tf_op jit(solution)/shard_map/ppermute | solution.py:402
  12.8 4.8 %copy-start.6 = (s32[4,16,9]{1,0,2:T(4,128)S(1)}, s32[4,16,9]{1,0,2:T(4,128)}, u32[]{:S(2)}) copy-start(s32[4,16,9]{1,0,2:T(4,128)} %param.11) | copy-start | bytes 6916
  13.6 20.9 %collective-permute-start.8 = (f32[5,1,16,128]{3,2,1,0:T(8,128)S(1)}, f32[5,1,16,128]{3,2,1,0:T(8,128)S(1)}, u32[]{:S(2)}, u32[]{:S(2)}) collective-permute-start(f32[5,1,16,128]{3,2,1,0:T(8,128)S(1)} %get-tuple-element.59), channel_id=1, source_target_pairs={{0,8},{8,16},{16,24},{24,32},{32,40},{40,48},{48,56},{56,64},{64,7... | collective-permute-start | bytes 122888 | tf_op jit(solution)/shard_map/ppermute | solution.py:400
  18.5 9.7 %copy-start.1 = (f32[128,512]{1,0:T(8,128)S(1)}, f32[128,512]{1,0:T(8,128)}, u32[]{:S(2)}) copy-start(f32[128,512]{1,0:T(8,128)} %param.15) | copy-start | bytes 786436
  18.5 15.4 %copy-start.2 = (f32[3,128,512]{2,1,0:T(8,128)S(1)}, f32[3,128,512]{2,1,0:T(8,128)}, u32[]{:S(2)}) copy-start(f32[3,128,512]{2,1,0:T(8,128)} %param.14) | copy-start | bytes 2359300
  18.5 16.0 %collective-permute-start.9 = (f32[5,1,16,128]{3,2,1,0:T(8,128)S(1)}, f32[5,1,16,128]{3,2,1,0:T(8,128)S(1)}, u32[]{:S(2)}, u32[]{:S(2)}) collective-permute-start(f32[5,1,16,128]{3,2,1,0:T(8,128)S(1)} %get-tuple-element.60), channel_id=1, source_target_pairs={{8,0},{16,8},{24,16},{32,24},{40,32},{48,40},{56,48},{64,56},{72,6... | collective-permute-start | bytes 122888 | tf_op jit(solution)/shard_map/ppermute | solution.py:402
  21.1 10.9 %collective-permute-start.2 = (f32[3,130,1]{2,1,0:T(8,128)S(1)}, f32[3,130,1]{2,1,0:T(8,128)S(1)}, u32[]{:S(2)}, u32[]{:S(2)}) collective-permute-start(f32[3,130,1]{2,1,0:T(8,128)S(1)} %get-tuple-element.35), channel_id=1, source_target_pairs={{0,1},{1,2},{2,3},{3,4},{4,5},{5,6},{6,7},{8,9},{9,10},{10,11},{11... | collective-permute-start | bytes 4688 | tf_op jit(solution)/shard_map/ppermute | solution.py:400
  26.3 7.6 %collective-permute-start.3 = (f32[3,130,1]{2,1,0:T(8,128)S(1)}, f32[3,130,1]{2,1,0:T(8,128)S(1)}, u32[]{:S(2)}, u32[]{:S(2)}) collective-permute-start(f32[3,130,1]{2,1,0:T(8,128)S(1)} %get-tuple-element.36), channel_id=1, source_target_pairs={{1,0},{2,1},{3,2},{4,3},{5,4},{6,5},{7,6},{9,8},{10,9},{11,10},{12... | collective-permute-start | bytes 4688 | tf_op jit(solution)/shard_map/ppermute | solution.py:402
  28.3 12.5 %collective-permute-start.6 = (f32[130,1]{1,0:T(8,128)S(1)}, f32[130,1]{1,0:T(8,128)S(1)}, u32[]{:S(2)}, u32[]{:S(2)}) collective-permute-start(f32[130,1]{1,0:T(8,128)S(1)} %get-tuple-element.53), channel_id=1, source_target_pairs={{0,1},{1,2},{2,3},{3,4},{4,5},{5,6},{6,7},{8,9},{9,10},{10,11},{11... | collective-permute-start | bytes 1568 | tf_op jit(solution)/shard_map/ppermute | solution.py:400
  32.0 8.9 %collective-permute-start.7 = (f32[130,1]{1,0:T(8,128)S(1)}, f32[130,1]{1,0:T(8,128)S(1)}, u32[]{:S(2)}, u32[]{:S(2)}) collective-permute-start(f32[130,1]{1,0:T(8,128)S(1)} %get-tuple-element.54), channel_id=1, source_target_pairs={{1,0},{2,1},{3,2},{4,3},{5,4},{6,5},{7,6},{9,8},{10,9},{11,10},{12... | collective-permute-start | bytes 1568 | tf_op jit(solution)/shard_map/ppermute | solution.py:402
  34.4 0.8 copy-start.3
  34.4 0.9 copy-start.4
  35.3 5.8 %collective-permute-start.10 = (f32[5,6,1,128]{3,2,1,0:T(1,128)S(1)}, f32[5,6,1,128]{3,2,1,0:T(1,128)S(1)}, u32[]{:S(2)}, u32[]{:S(2)}) collective-permute-start(f32[5,6,1,128]{3,2,1,0:T(1,128)S(1)} %get-tuple-element.57), channel_id=1, source_target_pairs={{0,1},{1,2},{2,3},{3,4},{4,5},{5,6},{6,7},{8,9},{9,10},{10,11},{11... | collective-permute-start | bytes 46088 | tf_op jit(solution)/shard_map/ppermute | solution.py:400
  38.9 5.0 %collective-permute-start.11 = (f32[5,6,1,128]{3,2,1,0:T(1,128)S(1)}, f32[5,6,1,128]{3,2,1,0:T(1,128)S(1)}, u32[]{:S(2)}, u32[]{:S(2)}) collective-permute-start(f32[5,6,1,128]{3,2,1,0:T(1,128)S(1)} %get-tuple-element.58), channel_id=1, source_target_pairs={{1,0},{2,1},{3,2},{4,3},{5,4},{6,5},{7,6},{9,8},{10,9},{11,10},{12... | collective-permute-start | bytes 46088 | tf_op jit(solution)/shard_map/ppermute | solution.py:402
  97.9 28.4 %all-to-all-start = ((f32[6,128,128]{2,0,1:T(8,128)}), f32[6,128,128]{2,0,1:T(8,128)S(1)}, u32[]{:S(2)}, u32[]{:S(2)}) async-start(f32[6,128,128]{2,0,1:T(8,128)} %copy.20), calls=%async_computation | async-start | bytes 1048576 | tf_op jit(solution)/shard_map/all_to_all | solution.py:440
  158.6 3.5 %collective-permute-start.12 = (f32[3,1,512]{2,1,0:T(1,128)S(1)}, f32[3,1,512]{2,1,0:T(1,128)S(1)}, u32[]{:S(2)}, u32[]{:S(2)}) collective-permute-start(f32[3,1,512]{2,1,0:T(1,128)S(1)} %get-tuple-element.41), channel_id=1, source_target_pairs={{0,8},{8,16},{16,24},{24,32},{32,40},{40,48},{48,56},{56,64},{64,7... | collective-permute-start | bytes 18440 | tf_op jit(solution)/shard_map/ppermute | solution.py:400
  160.7 4.4 %collective-permute-start.13 = (f32[3,1,512]{2,1,0:T(1,128)S(1)}, f32[3,1,512]{2,1,0:T(1,128)S(1)}, u32[]{:S(2)}, u32[]{:S(2)}) collective-permute-start(f32[3,1,512]{2,1,0:T(1,128)S(1)} %get-tuple-element.42), channel_id=1, source_target_pairs={{8,0},{16,8},{24,16},{32,24},{40,32},{48,40},{56,48},{64,56},{72,6... | collective-permute-start | bytes 18440 | tf_op jit(solution)/shard_map/ppermute | solution.py:402
  165.2 6.4 %collective-permute-start.14 = (f32[3,130,1]{2,1,0:T(8,128)S(1)}, f32[3,130,1]{2,1,0:T(8,128)S(1)}, u32[]{:S(2)}, u32[]{:S(2)}) collective-permute-start(f32[3,130,1]{2,1,0:T(8,128)S(1)} %get-tuple-element.33), channel_id=1, source_target_pairs={{0,1},{1,2},{2,3},{3,4},{4,5},{5,6},{6,7},{8,9},{9,10},{10,11},{11... | collective-permute-start | bytes 4688 | tf_op jit(solution)/shard_map/ppermute | solution.py:400
  168.9 7.1 %collective-permute-start.15 = (f32[3,130,1]{2,1,0:T(8,128)S(1)}, f32[3,130,1]{2,1,0:T(8,128)S(1)}, u32[]{:S(2)}, u32[]{:S(2)}) collective-permute-start(f32[3,130,1]{2,1,0:T(8,128)S(1)} %get-tuple-element.34), channel_id=1, source_target_pairs={{1,0},{2,1},{3,2},{4,3},{5,4},{6,5},{7,6},{9,8},{10,9},{11,10},{12... | collective-permute-start | bytes 4688 | tf_op jit(solution)/shard_map/ppermute | solution.py:402
  177.2 1.1 copy-start
  178.5 4.2 %collective-permute-start.16 = (f32[3,1,512]{2,1,0:T(1,128)S(1)}, f32[3,1,512]{2,1,0:T(1,128)S(1)}, u32[]{:S(2)}, u32[]{:S(2)}) collective-permute-start(f32[3,1,512]{2,1,0:T(1,128)S(1)} %get-tuple-element.39), channel_id=1, source_target_pairs={{0,8},{8,16},{16,24},{24,32},{32,40},{40,48},{48,56},{56,64},{64,7... | collective-permute-start | bytes 18440 | tf_op jit(solution)/shard_map/ppermute | solution.py:400
  181.4 4.4 %collective-permute-start.17 = (f32[3,1,512]{2,1,0:T(1,128)S(1)}, f32[3,1,512]{2,1,0:T(1,128)S(1)}, u32[]{:S(2)}, u32[]{:S(2)}) collective-permute-start(f32[3,1,512]{2,1,0:T(1,128)S(1)} %get-tuple-element.40), channel_id=1, source_target_pairs={{8,0},{16,8},{24,16},{32,24},{40,32},{48,40},{56,48},{64,56},{72,6... | collective-permute-start | bytes 18440 | tf_op jit(solution)/shard_map/ppermute | solution.py:402
  185.9 6.0 %collective-permute-start.18 = (f32[3,130,1]{2,1,0:T(8,128)S(1)}, f32[3,130,1]{2,1,0:T(8,128)S(1)}, u32[]{:S(2)}, u32[]{:S(2)}) collective-permute-start(f32[3,130,1]{2,1,0:T(8,128)S(1)} %get-tuple-element.31), channel_id=1, source_target_pairs={{0,1},{1,2},{2,3},{3,4},{4,5},{5,6},{6,7},{8,9},{9,10},{10,11},{11... | collective-permute-start | bytes 4688 | tf_op jit(solution)/shard_map/ppermute | solution.py:400
  189.1 7.1 %collective-permute-start.19 = (f32[3,130,1]{2,1,0:T(8,128)S(1)}, f32[3,130,1]{2,1,0:T(8,128)S(1)}, u32[]{:S(2)}, u32[]{:S(2)}) collective-permute-start(f32[3,130,1]{2,1,0:T(8,128)S(1)} %get-tuple-element.32), channel_id=1, source_target_pairs={{1,0},{2,1},{3,2},{4,3},{5,4},{6,5},{7,6},{9,8},{10,9},{11,10},{12... | collective-permute-start | bytes 4688 | tf_op jit(solution)/shard_map/ppermute | solution.py:402
  198.3 5.4 %collective-permute-start.20 = (f32[3,1,512]{2,1,0:T(1,128)S(1)}, f32[3,1,512]{2,1,0:T(1,128)S(1)}, u32[]{:S(2)}, u32[]{:S(2)}) collective-permute-start(f32[3,1,512]{2,1,0:T(1,128)S(1)} %get-tuple-element.37), channel_id=1, source_target_pairs={{0,8},{8,16},{16,24},{24,32},{32,40},{40,48},{48,56},{56,64},{64,7... | collective-permute-start | bytes 18440 | tf_op jit(solution)/shard_map/ppermute | solution.py:400
  202.4 4.7 %collective-permute-start.21 = (f32[3,1,512]{2,1,0:T(1,128)S(1)}, f32[3,1,512]{2,1,0:T(1,128)S(1)}, u32[]{:S(2)}, u32[]{:S(2)}) collective-permute-start(f32[3,1,512]{2,1,0:T(1,128)S(1)} %get-tuple-element.38), channel_id=1, source_target_pairs={{8,0},{16,8},{24,16},{32,24},{40,32},{48,40},{56,48},{64,56},{72,6... | collective-permute-start | bytes 18440 | tf_op jit(solution)/shard_map/ppermute | solution.py:402
  207.2 5.6 %collective-permute-start.22 = (f32[3,130,1]{2,1,0:T(8,128)S(1)}, f32[3,130,1]{2,1,0:T(8,128)S(1)}, u32[]{:S(2)}, u32[]{:S(2)}) collective-permute-start(f32[3,130,1]{2,1,0:T(8,128)S(1)} %get-tuple-element.29), channel_id=1, source_target_pairs={{0,1},{1,2},{2,3},{3,4},{4,5},{5,6},{6,7},{8,9},{9,10},{10,11},{11... | collective-permute-start | bytes 4688 | tf_op jit(solution)/shard_map/ppermute | solution.py:400
  210.1 7.1 %collective-permute-start.23 = (f32[3,130,1]{2,1,0:T(8,128)S(1)}, f32[3,130,1]{2,1,0:T(8,128)S(1)}, u32[]{:S(2)}, u32[]{:S(2)}) collective-permute-start(f32[3,130,1]{2,1,0:T(8,128)S(1)} %get-tuple-element.30), channel_id=1, source_target_pairs={{1,0},{2,1},{3,2},{4,3},{5,4},{6,5},{7,6},{9,8},{10,9},{11,10},{12... | collective-permute-start | bytes 4688 | tf_op jit(solution)/shard_map/ppermute | solution.py:402

commit v2 on v1

--- a/solution.py
+++ b/solution.py
@@ -143,7 +143,7 @@
     lax.fori_loop(0, groups, group, jnp.zeros((128, 128), F32))
     tails = []
     for k in range(4):
-        send_ref[k] = acc_ref[k * 128 : k * 128 + 128, 0:128] + acc_ref[
+        send_ref[pl.ds(k, 128, stride=8), :] = acc_ref[k * 128 : k * 128 + 128, 0:128] + acc_ref[
             512 + k * 128 : 640 + k * 128, 0:128
         ]
         tails.append(
@@ -151,8 +151,10 @@
             + acc_ref[512 + k * 128 : 640 + k * 128, 128:256]
         )
     low_half = iota((128, 128), 1) < 64
+    for k in range(6, 8):
+        send_ref[pl.ds(k, 128, stride=8), :] = jnp.zeros((128, 128), F32)
     for h in range(2):
-        send_ref[4 + h] = jnp.where(
+        send_ref[pl.ds(4 + h, 128, stride=8), :] = jnp.where(
             low_half, tails[2 * h], pltpu.roll(tails[2 * h + 1], 64, 1)
         )
 
@@ -187,7 +189,7 @@
         out_shape=(
             jax.ShapeDtypeStruct((64, 128), F32),
             jax.ShapeDtypeStruct((64, 128), F32),
-            jax.ShapeDtypeStruct((6, 128, 128), F32),
+            jax.ShapeDtypeStruct((1024, 128), F32),
         ),
         in_specs=[vmem(), pl.BlockSpec(memory_space=pltpu.SMEM), vmem(), vmem()],
         out_specs=(vmem(), vmem(), vmem()),
@@ -207,8 +209,8 @@
 def unfold(got_ref, out_ref, kinds):
     low_half = iota((64, 128), 1) < 64
     for k in range(kinds):
-        out_ref[k, 0:128, :] = got_ref[k]
-        row = got_ref[kinds + k // 2]
+        out_ref[k, 0:128, :] = got_ref[pl.ds(k, 128, stride=8), :]
+        row = got_ref[pl.ds(kinds + k // 2, 128, stride=8), :]
         first, second = row[0:64], row[64:128]
         if k % 2 == 0:
             out_ref[k, 128:192, :] = jnp.where(low_half, first, pltpu.roll(second, 64, 1))
@@ -272,9 +274,9 @@
 
 
 def lookup_kernel(got_ref, state_ref, back_ref, cells_ref, table_ref, found_ref):
-    cells_ref[0:128, :] = got_ref[0]
+    cells_ref[0:128, :] = got_ref[pl.ds(0, 128, stride=8), :]
     low_half = iota((64, 128), 1) < 64
-    tail = got_ref[4]
+    tail = got_ref[pl.ds(4, 128, stride=8), :]
     cells_ref[128:192, :] = jnp.where(low_half, tail[0:64], pltpu.roll(tail[64:128], 64, 1))
     for k in range(3):
         hi, lo = split2(state_ref[k])
@@ -311,18 +313,20 @@
     lax.fori_loop(0, 24, step, 0)
     tails = [found_ref[k, 128:192, :] for k in range(3)]
     for k in range(3):
-        back_ref[k] = found_ref[k, 0:128, :]
+        back_ref[pl.ds(k, 128, stride=8), :] = found_ref[k, 0:128, :]
     turned = [pltpu.roll(t, 64, 1) for t in tails]
-    back_ref[3, 0:64, :] = jnp.where(low_half, tails[0], turned[1])
-    back_ref[3, 64:128, :] = jnp.where(low_half, turned[0], tails[1])
-    back_ref[4, 0:64, :] = tails[2]
-    back_ref[4, 64:128, :] = turned[2]
+    back_ref[pl.ds(3, 64, stride=8), :] = jnp.where(low_half, tails[0], turned[1])
+    back_ref[pl.ds(515, 64, stride=8), :] = jnp.where(low_half, turned[0], tails[1])
+    back_ref[pl.ds(4, 64, stride=8), :] = tails[2]
+    back_ref[pl.ds(516, 64, stride=8), :] = turned[2]
+    for k in range(5, 8):
+        back_ref[pl.ds(k, 128, stride=8), :] = jnp.zeros((128, 128), F32)
 
 
 def lookup_call(got, state):
     return pl.pallas_call(
         lookup_kernel,
-        out_shape=jax.ShapeDtypeStruct((5, 128, 128), F32),
+        out_shape=jax.ShapeDtypeStruct((1024, 128), F32),
         in_specs=[vmem(), vmem()],
         out_specs=vmem(),
         scratch_shapes=[
@@ -336,10 +340,10 @@
 
 
 def unpack_kernel(back_ref, dest_ref, rank_ref, out_ref, table_ref):
-    turned = pltpu.roll(back_ref[3], 64, 1)
-    tails = [back_ref[3], turned, back_ref[4]]
+    tail = back_ref[pl.ds(3, 128, stride=8), :]
+    tails = [tail, pltpu.roll(tail, 64, 1), back_ref[pl.ds(4, 128, stride=8), :]]
     for k in range(3):
-        for part, piece in enumerate(split2(back_ref[k])):
+        for part, piece in enumerate(split2(back_ref[pl.ds(k, 128, stride=8), :])):
             table_ref[k * 128 : k * 128 + 128, part * 192 : part * 192 + 128] = piece.astype(BF16)
         for part, piece in enumerate(split2(tails[k])):
             table_ref[
@@ -389,63 +393,380 @@
     )(back, dest, rank)
 
 
-def padded_2(cells, sides, width):
-    for axis, dim in sides:
-        count = lax.axis_size(axis)
-        ends = count - 1
-        head = lax.slice_in_dim(cells, 0, width, axis=dim)
-        tail = lax.slice_in_dim(cells, cells.shape[dim] - width, cells.shape[dim], axis=dim)
-        cells = jnp.concatenate(
-            [
-                lax.ppermute(tail, axis, [(i, (i + 1) % count) for i in range(ends)]),
-                cells,
-                lax.ppermute(head, axis, [((i + 1) % count, i) for i in range(ends)]),
-            ],
-            axis=dim,
+MESH = pl.DeviceIdType.MESH
+AROUND = [(-1, 0), (1, 0), (0, -1), (0, 1), (-1, -1), (-1, 1), (1, -1), (1, 1)]
+
+
+def my_place():
+    return lax.axis_index("along"), lax.axis_index("cross")
+
+
+def sizes():
+    return lax.axis_size("along"), lax.axis_size("cross")
+
+
+def at_step(step):
+    (a, c), (na, nc) = my_place(), sizes()
+    return lax.rem(a + step[0] + na, na), lax.rem(c + step[1] + nc, nc)
+
+
+def greet_around():
+    barrier = pltpu.get_barrier_semaphore()
+    for step in AROUND:
+        pl.semaphore_signal(barrier, inc=1, device_id=at_step(step), device_id_type=MESH)
+    pl.semaphore_wait(barrier, len(AROUND))
+
+
+def rim_copies(out_refs, in_refs, send_sem, recv_sem):
+    copies = []
+    for n, step in enumerate(AROUND):
+        opposite = AROUND.index((-step[0], -step[1]))
+        copies.append(
+            pltpu.make_async_remote_copy(
+                src_ref=out_refs[n],
+                dst_ref=in_refs[opposite],
+                send_sem=send_sem.at[n],
+                recv_sem=recv_sem.at[opposite],
+                device_id=at_step(step),
+                device_id_type=MESH,
+            )
         )
-    return cells
-
-
-def lax_friedrichs(state_pad, depth_pad):
-    height = state_pad[0]
-    speed_x = state_pad[1]
-    speed_y = state_pad[2]
-    flux_x = depth_pad * speed_x
-    flux_y = depth_pad * speed_y
-
-    def average(quantity):
-        return 0.25 * (
-            quantity[2:, 1:-1] + quantity[:-2, 1:-1] + quantity[1:-1, 2:] + quantity[1:-1, :-2]
+    return copies
+
+
+DEEP = 4
+SIDE_PARTICLES = 24
+
+
+def column_strip(fields, right):
+    lanes = iota((fields[0].shape[0], 128), 1)
+    out = jnp.zeros((fields[0].shape[0], 128), F32)
+    for f, field in enumerate(fields):
+        turn = DEEP * f + (DEEP if right else 0)
+        moved = pltpu.roll(field, turn, 1) if turn else field
+        out = jnp.where((lanes >= DEEP * f) & (lanes < DEEP * f + DEEP), moved, out)
+    return out
+
+
+def write_rims(out_refs, base, fields):
+    top, bottom = slice(0, 8), slice(120, 128)
+    for n, rows in ((0, top), (1, bottom)):
+        for f, field in enumerate(fields):
+            for b in range(4):
+                at = base[n] + (f * 4 + b) * 8
+                out_refs[n][at : at + 8, :] = field(rows, slice(b * 128, b * 128 + 128))
+    for right in range(2):
+        lanes = slice(384, 512) if right else slice(0, 128)
+        strip = column_strip([field(slice(0, 128), lanes) for field in fields], right == 1)
+        at = base[2 + right]
+        out_refs[2 + right][at : at + 128, :] = strip
+        out_refs[4 + right][base[4] : base[4] + 8, :] = strip[0:8]
+        out_refs[6 + right][base[4] : base[4] + 8, :] = strip[120:128]
+
+
+def rims_kernel(
+    off_ref, vel_ref, mass_ref, surface_ref, depth_ref,
+    pad_ref, up_ref, down_ref, left_ref, right_ref, c0_ref, c1_ref, c2_ref, c3_ref,
+    o0, o1, o2, o3, o4, o5, o6, o7, i0, i1, i2, i3, i4, i5, i6, i7, send_sem, recv_sem,
+):
+    outs = [o0, o1, o2, o3, o4, o5, o6, o7]
+    ins = [i0, i1, i2, i3, i4, i5, i6, i7]
+    rows, cols = mass_ref.shape[0], mass_ref.shape[1]
+    particle = [
+        (off_ref, 0), (off_ref, 1), (vel_ref, 0), (vel_ref, 1), (mass_ref, None),
+    ]
+
+    def tiles(f, i, j):
+        ref, part = particle[f]
+        return ref[i, j, :] if part is None else ref[part, i, j, :]
+
+    everything = slice(0, cols)
+    for f in range(5):
+        outs[0][f * cols : (f + 1) * cols, :] = tiles(f, 0, everything)
+        outs[1][f * cols : (f + 1) * cols, :] = tiles(f, rows - 1, everything)
+        for side, j in ((0, slice(0, 1)), (1, slice(cols - 1, cols))):
+            for i in range(rows):
+                outs[2 + side][f * rows + i : f * rows + i + 1, :] = tiles(f, i, j)
+            outs[4 + side][f : f + 1, :] = tiles(f, 0, j)
+            outs[6 + side][f : f + 1, :] = tiles(f, rows - 1, j)
+    for side in range(2):
+        outs[2 + side][5 * rows :SIDE_PARTICLES, :] = jnp.zeros((SIDE_PARTICLES - 5 * rows, 128), F32)
+        outs[4 + side][5:8, :] = jnp.zeros((3, 128), F32)
+        outs[6 + side][5:8, :] = jnp.zeros((3, 128), F32)
+    fields = [
+        lambda r, c: surface_ref[0, r, c],
+        lambda r, c: surface_ref[1, r, c],
+        lambda r, c: surface_ref[2, r, c],
+        lambda r, c: depth_ref[r, c],
+    ]
+    write_rims(outs, [5 * cols, 5 * cols, SIDE_PARTICLES, SIDE_PARTICLES, 8], fields)
+    greet_around()
+    copies = rim_copies(outs, ins, send_sem, recv_sem)
+    for copy in copies:
+        copy.start()
+    for f in range(5):
+        for i in range(rows):
+            pad_ref[f, i + 1, 1 : cols + 1, :] = tiles(f, i, everything)
+    for copy in copies:
+        copy.wait()
+    (a, c), (na, nc) = my_place(), sizes()
+    inside = [a > 0, a < na - 1, c > 0, c < nc - 1]
+
+    def kept(f, value, *tests):
+        if f < 4:
+            return value
+        for test in tests:
+            value = jnp.where(test, value, 0.0)
+        return value
+
+    for f in range(5):
+        pad_ref[f, 0, 1 : cols + 1, :] = kept(f, ins[0][f * cols : (f + 1) * cols, :], inside[0])
+        pad_ref[f, rows + 1, 1 : cols + 1, :] = kept(f, ins[1][f * cols : (f + 1) * cols, :], inside[1])
+        for side, j in ((0, 0), (1, cols + 1)):
+            for i in range(rows):
+                pad_ref[f, i + 1, j : j + 1, :] = kept(
+                    f, ins[2 + side][f * rows + i : f * rows + i + 1, :], inside[2 + side]
+                )
+            pad_ref[f, 0, j : j + 1, :] = kept(f, ins[4 + side][f : f + 1, :], inside[0], inside[2 + side])
+            pad_ref[f, rows + 1, j : j + 1, :] = kept(f, ins[6 + side][f : f + 1, :], inside[1], inside[2 + side])
+    up_ref[...] = ins[0][5 * cols : 5 * cols + 128, :]
+    down_ref[...] = ins[1][5 * cols : 5 * cols + 128, :]
+    left_ref[...] = ins[2][SIDE_PARTICLES : SIDE_PARTICLES + 128, :]
+    right_ref[...] = ins[3][SIDE_PARTICLES : SIDE_PARTICLES + 128, :]
+    for n, ref in enumerate((c0_ref, c1_ref, c2_ref, c3_ref)):
+        ref[...] = ins[4 + n][8:16, :]
+
+
+def rims_call(offsets, velocity, mass, surface, depth):
+    rows, cols = mass.shape[0], mass.shape[1]
+    tall, wide, corner = 5 * cols + 128, SIDE_PARTICLES + 128, 16
+    heights = [tall, tall, wide, wide, corner, corner, corner, corner]
+    buffers = [pltpu.VMEM((h, 128), F32) for h in heights]
+    return pl.pallas_call(
+        rims_kernel,
+        out_shape=(
+            jax.ShapeDtypeStruct((5, rows + 2, cols + 2, 128), F32),
+            *[jax.ShapeDtypeStruct((128, 128), F32)] * 4,
+            *[jax.ShapeDtypeStruct((8, 128), F32)] * 4,
+        ),
+        in_specs=[vmem()] * 5,
+        out_specs=tuple([vmem()] * 9),
+        scratch_shapes=[
+            *buffers,
+            *buffers,
+            pltpu.SemaphoreType.DMA((8,)),
+            pltpu.SemaphoreType.DMA((8,)),
+        ],
+        compiler_params=pltpu.CompilerParams(
+            vmem_limit_bytes=VMEM_LIMIT, collective_id=0, has_side_effects=True
+        ),
+        name="rims",
+    )(offsets, velocity, mass, surface, depth)
+
+
+def exchange_kernel(out_ref, in_ref, send_sem, recv_sem):
+    (a, c), (na, nc) = my_place(), sizes()
+    count = na * nc
+    me = a * nc + c
+
+    def block(ref, n):
+        return ref.at[pl.ds(pl.multiple_of(n * 8, 8), 8), :]
+
+    def start(step, carry):
+        to = lax.rem(me + step, count)
+        pltpu.make_async_remote_copy(
+            src_ref=block(out_ref, to),
+            dst_ref=block(in_ref, me),
+            send_sem=send_sem,
+            recv_sem=recv_sem,
+            device_id=(lax.div(to, nc), lax.rem(to, nc)),
+            device_id_type=MESH,
+        ).start()
+        return carry
+
+    lax.fori_loop(1, count, start, 0)
+    own = pl.ds(pl.multiple_of(me * 8, 8), 8)
+    in_ref[own, :] = out_ref[own, :]
+    most = (count - 1) * 8
+    pltpu.make_async_copy(out_ref.at[0:most, :], out_ref.at[0:most, :], send_sem).wait()
+    pltpu.make_async_copy(in_ref.at[0:most, :], in_ref.at[0:most, :], recv_sem).wait()
+
+
+def exchange_call(blocks, name):
+    return pl.pallas_call(
+        exchange_kernel,
+        out_shape=jax.ShapeDtypeStruct(blocks.shape, F32),
+        in_specs=[vmem()],
+        out_specs=vmem(),
+        scratch_shapes=[pltpu.SemaphoreType.DMA, pltpu.SemaphoreType.DMA],
+        compiler_params=pltpu.CompilerParams(
+            vmem_limit_bytes=VMEM_LIMIT, has_side_effects=True
+        ),
+        name=name,
+    )(blocks)
+
+
+TALL = 160
+BROAD = 768
+FIRST = 16
+
+
+def place_rims(wide_ref, index, f, refs, bases):
+    up, down, left, right, *corners = refs
+    for b in range(4):
+        lanes = slice(128 + b * 128, 256 + b * 128)
+        at = (f * 4 + b) * 8
+        wide_ref[index, FIRST - 8 : FIRST, lanes] = up[bases[0] + at : bases[0] + at + 8, :]
+        wide_ref[index, FIRST + 128 : FIRST + 136, lanes] = down[bases[0] + at : bases[0] + at + 8, :]
+    for side in range(2):
+        lanes = slice(0, 128) if side == 0 else slice(BROAD - 128, BROAD)
+        turn = (128 - DEEP - DEEP * f) % 128 if side == 0 else (128 - DEEP * f) % 128
+        for rows, ref, base in (
+            (slice(FIRST, FIRST + 128), (left, right)[side], bases[1]),
+            (slice(FIRST - 8, FIRST), corners[side], bases[2]),
+            (slice(FIRST + 128, FIRST + 136), corners[2 + side], bases[2]),
+        ):
+            value = ref[base : base + rows.stop - rows.start, :]
+            wide_ref[index, rows, lanes] = pltpu.roll(value, turn, 1) if turn else value
+
+
+def water_step(old_ref, new_ref, depth_ref, source_ref, with_source):
+    (a, c), (na, nc) = my_place(), sizes()
+    cols = iota((8, BROAD), 1) + (c * 512 - 128)
+    cols_in = (cols >= 0) & (cols < nc * 512)
+
+    def rows8(rb, carry):
+        start = pl.multiple_of(rb * 8, 8)
+        three = pl.ds(pl.multiple_of(rb * 8 - 8, 8), 24)
+        h3, u3, v3 = [old_ref[f, three, :] for f in range(3)]
+        fu3 = depth_ref[0, three, :] * u3
+        h, u, v = h3[8:16], u3[8:16], v3[8:16]
+        fv = depth_ref[0, pl.ds(start, 8), :] * v
+
+        def left(x):
+            return pltpu.roll(x, 1, 1)
+
+        def right(x):
+            return pltpu.roll(x, BROAD - 1, 1)
+
+        def average(x3, x_left, x_right):
+            return 0.25 * (x3[9:17] + x3[7:15] + x_right + x_left)
+
+        hl, hr = left(h), right(h)
+        next_h = average(h3, hl, hr) - 0.5 * courant * (
+            fu3[9:17] - fu3[7:15] + right(fv) - left(fv)
         )
-
-    next_height = average(height) - 0.5 * courant * (
-        flux_x[2:, 1:-1] - flux_x[:-2, 1:-1] + flux_y[1:-1, 2:] - flux_y[1:-1, :-2]
-    )
-    next_speed_x = average(speed_x) - 0.5 * courant * (height[2:, 1:-1] - height[:-2, 1:-1])
-    next_speed_y = average(speed_y) - 0.5 * courant * (height[1:-1, 2:] - height[1:-1, :-2])
-    return jnp.stack([next_height, next_speed_x, next_speed_y])
+        next_u = average(u3, left(u), right(u)) - 0.5 * courant * (h3[9:17] - h3[7:15])
+        next_v = average(v3, left(v), right(v)) - 0.5 * courant * (hr - hl)
+        rows = iota((8, BROAD), 0) + (a * 128 - FIRST + start)
+        inside = cols_in & (rows >= 0) & (rows < na * 128)
+        for f, value in enumerate((next_h, next_u, next_v)):
+            if with_source:
+                value = value + source_ref[f, pl.ds(start, 8), :]
+            new_ref[f, pl.ds(start, 8), :] = jnp.where(inside, value, 0.0)
+        return carry
+
+    lax.fori_loop(1, 19, rows8, 0)
+
+
+def mask_state(ref):
+    (a, c), (na, nc) = my_place(), sizes()
+    cols = iota((8, BROAD), 1) + (c * 512 - 128)
+    cols_in = (cols >= 0) & (cols < nc * 512)
+
+    def rows8(rb, carry):
+        at = pl.ds(pl.multiple_of(rb * 8, 8), 8)
+        rows = iota((8, BROAD), 0) + (a * 128 - FIRST + rb * 8)
+        inside = cols_in & (rows >= 0) & (rows < na * 128)
+        for f in range(3):
+            ref[f, at, :] = jnp.where(inside, ref[f, at, :], 0.0)
+        return carry
+
+    lax.fori_loop(1, 19, rows8, 0)
+
+
+def water_kernel(
+    source_ref, surface_ref, depth_ref,
+    up_ref, down_ref, left_ref, right_ref, c0_ref, c1_ref, c2_ref, c3_ref,
+    state_ref,
+    even, odd, deep, wide_source,
+    o0, o1, o2, o3, o4, o5, o6, o7, i0, i1, i2, i3, i4, i5, i6, i7, send_sem, recv_sem,
+):
+    outs = [o0, o1, o2, o3, o4, o5, o6, o7]
+    ins = [i0, i1, i2, i3, i4, i5, i6, i7]
+    write_rims(outs, [0, 0, 0, 0, 0], [
+        lambda r, c: source_ref[0, r, c],
+        lambda r, c: source_ref[1, r, c],
+        lambda r, c: source_ref[2, r, c],
+    ])
+    greet_around()
+    copies = rim_copies(outs, ins, send_sem, recv_sem)
+    for copy in copies:
+        copy.start()
+    rims = [up_ref, down_ref, left_ref, right_ref, c0_ref, c1_ref, c2_ref, c3_ref]
+    own_rows, own_lanes = slice(FIRST, FIRST + 128), slice(128, 640)
+    for ref in (even, odd, deep):
+        for f in range(ref.shape[0]):
+            ref[f, 0:8, :] = jnp.zeros((8, BROAD), F32)
+            ref[f, TALL - 8 : TALL, :] = jnp.zeros((8, BROAD), F32)
+    for f in range(3):
+        even[f, own_rows, own_lanes] = surface_ref[f]
+        place_rims(even, f, f, rims, [0, 0, 0])
+    deep[0, own_rows, own_lanes] = depth_ref[...]
+    place_rims(deep, 0, 3, rims, [0, 0, 0])
+    mask_state(even)
+    for f in range(3):
+        wide_source[f, own_rows, own_lanes] = source_ref[f]
+    for copy in copies:
+        copy.wait()
+    for f in range(3):
+        place_rims(wide_source, f, f, ins, [0, 0, 0])
+    for step in range(SUBSTEPS):
+        old, new = (even, odd) if step % 2 == 0 else (odd, even)
+        water_step(old, new, deep, wide_source, True)
+    for f in range(3):
+        state_ref[f] = even[f, own_rows, own_lanes]
+
+
+def water_call(source, surface, depth, rims):
+    heights = [96, 96, 128, 128, 8, 8, 8, 8]
+    buffers = [pltpu.VMEM((h, 128), F32) for h in heights]
+    return pl.pallas_call(
+        water_kernel,
+        out_shape=jax.ShapeDtypeStruct((3, 128, 512), F32),
+        in_specs=[vmem()] * 11,
+        out_specs=vmem(),
+        scratch_shapes=[
+            pltpu.VMEM((3, TALL, BROAD), F32),
+            pltpu.VMEM((3, TALL, BROAD), F32),
+            pltpu.VMEM((1, TALL, BROAD), F32),
+            pltpu.VMEM((3, TALL, BROAD), F32),
+            *buffers,
+            *buffers,
+            pltpu.SemaphoreType.DMA((8,)),
+            pltpu.SemaphoreType.DMA((8,)),
+        ],
+        compiler_params=pltpu.CompilerParams(
+            vmem_limit_bytes=VMEM_LIMIT, collective_id=1, has_side_effects=True
+        ),
+        name="water",
+    )(source, surface, depth, *rims)
 
 
 def shards(
     offsets, velocity, particle_mass, neighbours, owner_device, target_cell, surface, water_depth
 ):
-    stacked = jnp.concatenate([offsets, velocity, particle_mass[None]], axis=0)
-    padded = padded_2(stacked, (("along", 1), ("cross", 2)), 1)
+    padded, *rims = rims_call(offsets, velocity, particle_mass, surface, water_depth)
     present = jnp.any(
         neighbours[..., :, None] == jnp.arange(9, dtype=jnp.int32), axis=-2
     ).astype(F32)
     dest = owner_device.reshape(64, 128)
     cell = target_cell.reshape(64, 128)
     density, rank, send = particles_call(padded, present.reshape(-1), dest, cell)
-    got = lax.all_to_all(send, ("along", "cross"), split_axis=1, concat_axis=1, tiled=True)
+    got = exchange_call(send, "send_sources")
     grid_source = deposit_call(got)
-    depth_pad = padded_2(water_depth, (("along", 0), ("cross", 1)), 1)
-    water_state = surface
-    for substep in range(SUBSTEPS):
-        state_pad = padded_2(water_state, (("along", 1), ("cross", 2)), 1)
-        water_state = lax_friedrichs(state_pad, depth_pad) + grid_source
-    back = lookup_call(got, water_state)
-    back = lax.all_to_all(back, ("along", "cross"), split_axis=1, concat_axis=1, tiled=True)
+    water_state = water_call(grid_source, surface, water_depth, rims)
+    back = exchange_call(lookup_call(got, water_state), "send_back")
     feedback = unpack_call(back, dest, rank)
     return (
         water_state,

time: 280 us -> 197 us (0.70)
  Pallas kernels: 115 us -> 193 us
  starting transfers between devices: 77.9 us -> 0 us
  waiting for transfers between devices: 40 us -> 0 us
  blocking collectives: 22.6 us -> 0 us
  other arithmetic: 13 us -> 0.8 us
  local copies, waits for them, and re-layouts: 8.72 us -> 1.71 us
    pallas_call x1 -> x5, Pallas kernels: 27 us -> 105 us  [the longest x2 40.5 us: exchange_call(): pl.pallas_call(exchange_kernel, out_shape=jax.ShapeDtypeStruct(blocks.sha...]
    ppermute x24 -> x0, starting transfers between devices: 63.1 us -> none  [the longest x12 43.3 us: padded_2(): lax.ppermute(tail, axis, [(i, (i + 1) % count) for i in range(ends)])]
    ppermute x24 -> x0, waiting for transfers between devices: 27.6 us -> none  [the longest x12 25.6 us: padded_2(): lax.ppermute(head, axis, [((i + 1) % count, i) for i in range(ends)])]
    all_to_all x1 -> x0, blocking collectives: 22.6 us -> none  [shards(): lax.all_to_all(back, ('along', 'cross'), split_axis=1, concat_axis=1, til...]
    all_to_all x1 -> x0, starting transfers between devices: 14.9 us -> none  [shards(): lax.all_to_all(send, ('along', 'cross'), split_axis=1, concat_axis=1, til...]
    all_to_all x1 -> x0, waiting for transfers between devices: 12.4 us -> none  [shards(): lax.all_to_all(send, ('along', 'cross'), split_axis=1, concat_axis=1, til...]
    another operation x8 -> x0, other arithmetic: 4.53 us -> none  [lax_friedrichs(): return jnp.stack([next_height, next_speed_x, next_speed_y])]
    pallas_call x2 -> x0, local copies, waits for them, and re-layouts: 3.2 us -> none  [the longest x1 2.03 us: particles_call(): pl.pallas_call(particles_kernel, out_shape=(jax.ShapeDtypeStruct((64, 128...]
  transfers between devices with their start and end apart: 25 -> 0, of which waited for: 11 -> 0; matrix products, arithmetic and copies ran while one was open for 2% -> 0% of each run, Pallas kernels for 0% -> 0%
where the time goes in v2:
time: 197 us; the launch traced here: 196 us
  Pallas kernels  193 us (98%)
    pallas_call x1, Pallas kernels, particles_call(): pl.pallas_call(particles_kernel, out_shape=(jax.ShapeDtypeStruct((64, 128...  51.3 us
    pallas_call x2, Pallas kernels, exchange_call(): pl.pallas_call(exchange_kernel, out_shape=jax.ShapeDtypeStruct(blocks.sha...  40.5 us
    pallas_call x1, Pallas kernels, deposit_call(): pl.pallas_call(deposit_kernel, out_shape=jax.ShapeDtypeStruct((3, 128, 51...  30.2 us
    pallas_call x1, Pallas kernels, lookup_call(): pl.pallas_call(lookup_kernel, out_shape=jax.ShapeDtypeStruct((1024, 128),...  27.1 us
    pallas_call x1, Pallas kernels, water_call(): pl.pallas_call(water_kernel, out_shape=jax.ShapeDtypeStruct((3, 128, 512)...  21.8 us
    pallas_call x1, Pallas kernels, rims_call(): pl.pallas_call(rims_kernel, out_shape=(jax.ShapeDtypeStruct((5, rows + 2,...  15.4 us
    pallas_call x1, Pallas kernels, unpack_call(): pl.pallas_call(unpack_kernel, out_shape=jax.ShapeDtypeStruct((3, 64, 128)...  6.7 us

profile of v2, /device:TPU:1, one launch (start us, length us, event | category | flops | bytes accessed | tf_op | source)
XLA Modules:
  0.0 196.2 jit_solution(15707115269134339696)
XLA Ops:
  0.6 0.8 fusion
  1.4 0.1 copy.13
  1.5 0.7 reshape.27.present_ref
  2.3 15.4 %rims.1 = (f32[5,6,18,128]{3,2,1,0:T(8,128)}, f32[128,128]{1,0:T(8,128)}, f32[128,128]{1,0:T(8,128)}, f32[128,128]{1,0:T(8,128)}, f32[128,128]{1,0:T(8,128)}, /*...) custom-call(f32[2,4,16,128]{3,2,1,0:T(8,128)} %off_ref.1, f32[2,4,16,128]{3,2,1,0:T(8,128)} %vel_ref.1, ...), custom_call_target="tpu_custom_call" | custom-call | tf_op jit(solution)/shard_map/rims/pallas_call | solution.py:545
  17.7 51.3 %particles.1 = (f32[64,128]{1,0:T(8,128)}, f32[64,128]{1,0:T(8,128)}, f32[1024,128]{1,0:T(8,128)}) custom-call(f32[5,6,18,128]{3,2,1,0:T(8,128)} %get-tuple-element.15.pad_ref, f32[576]{0:T(1024)} %reshape.27.present_ref, s32[64,128]{1,0:T(8,128)} %bitcast.4, s32[64,128]{1,0:T(8,128)} %bitcast.7), custom_call_target="tpu_custom_call" | custom-call | tf_op jit(solution)/shard_map/particles/pallas_call | solution.py:187
  69.0 21.0 %send_sources.1.got_ref = f32[1024,128]{1,0:T(8,128)} custom-call(f32[1024,128]{1,0:T(8,128)} %get-tuple-element.16.out_ref), custom_call_target="tpu_custom_call" | custom-call | tf_op jit(solution)/shard_map/send_sources/pallas_call | solution.py:596
  90.0 30.2 %deposit.1.source_ref = f32[3,128,512]{2,1,0:T(8,128)} custom-call(f32[1024,128]{1,0:T(8,128)} %send_sources.1.got_ref), custom_call_target="tpu_custom_call" | custom-call | tf_op jit(solution)/shard_map/deposit/pallas_call | solution.py:260
  120.2 21.8 %water.1.state_ref = f32[3,128,512]{2,1,0:T(8,128)} custom-call(f32[3,128,512]{2,1,0:T(8,128)} %deposit.1.source_ref, f32[3,128,512]{2,1,0:T(8,128)} %surface_ref.3, f32[128,512]{1,0:T(8,128)} %depth_ref.3, f32[128,128]{1,0:T(8,128)} %get-tuple-element.17.up_ref, f32[128,128]{1,0:T(8,128)} %get-tuple-element.18.down_ref, ...), custom_call_target="tpu_custom_call" | custom-call | tf_op jit(solution)/shard_map/water/pallas_call | solution.py:734
  142.0 27.1 %lookup.1.out_ref = f32[1024,128]{1,0:T(8,128)} custom-call(f32[1024,128]{1,0:T(8,128)} %send_sources.1.got_ref, f32[3,128,512]{2,1,0:T(8,128)} %water.1.state_ref), custom_call_target="tpu_custom_call" | custom-call | tf_op jit(solution)/shard_map/lookup/pallas_call | solution.py:327
  169.1 0.0 copy-start
  169.1 19.5 %send_back.1.back_ref = f32[1024,128]{1,0:T(8,128)} custom-call(f32[1024,128]{1,0:T(8,128)} %lookup.1.out_ref), custom_call_target="tpu_custom_call" | custom-call | tf_op jit(solution)/shard_map/send_back/pallas_call | solution.py:596
  188.7 6.7 %unpack.1 = f32[3,64,128]{2,1,0:T(8,128)} custom-call(f32[1024,128]{1,0:T(8,128)} %send_back.1.back_ref, s32[64,128]{1,0:T(8,128)} %bitcast.5, f32[64,128]{1,0:T(8,128)} %get-tuple-element.26.rank_ref), custom_call_target="tpu_custom_call" | custom-call | tf_op jit(solution)/shard_map/unpack/pallas_call | solution.py:385
  195.4 0.0 copy-done
  195.4 0.9 copy.15
  (1 shorter events, 0.0 us)
Async XLA Ops:
  169.1 26.2 %copy-start = (f32[3,128,512]{2,1,0:T(8,128)S(1)}, f32[3,128,512]{2,1,0:T(8,128)}, u32[]{:S(2)}) copy-start(f32[3,128,512]{2,1,0:T(8,128)} %water.1.state_ref) | copy-start | bytes 2359300

commit v3 on v0

v3 whole, which is shorter than its diff:
```python
import math

import jax
import jax.numpy as jnp
from jax import lax
from jax.experimental import pallas as pl
from jax.experimental.pallas import tpu as pltpu
from jax.sharding import PartitionSpec as P

SUBSTEPS = 4
KAPPA = math.sqrt(math.log2(math.e))
F32 = jnp.float32
BF16 = jnp.bfloat16
NN = (((1,), (0,)), ((), ()))
NT = (((1,), (1,)), ((), ()))
VMEM_LIMIT = 56 * 1024 * 1024

courant = 0.4


def dot(a, b, dims):
    return lax.dot_general(a, b, dims, preferred_element_type=F32)


def split2(x):
    hi = x.astype(BF16).astype(F32)
    return hi, x - hi


def iota(shape, dim):
    return lax.broadcasted_iota(jnp.int32, shape, dim)


def window_sums(pad_ref, present_ref, sums_ref):
    rows, cols = pad_ref.shape[1] - 2, pad_ref.shape[2] - 2

    def tile(t, carry):
        i = t // cols
        j = t - i * cols
        x = pad_ref[0, i + 1, pl.ds(j + 1, 1), :] * KAPPA
        y = pad_ref[1, i + 1, pl.ds(j + 1, 1), :] * KAPPA
        x_col = jnp.broadcast_to(x, (128, 128)).T
        y_col = jnp.broadcast_to(y, (128, 128)).T
        window = []
        for w in range(9):
            bi, bj = i + w // 3, j + w % 3
            bx = (pad_ref[0, bi, pl.ds(bj, 1), :] + (w // 3 - 1.0)) * KAPPA
            by = (pad_ref[1, bi, pl.ds(bj, 1), :] + (w % 3 - 1.0)) * KAPPA
            c0 = pad_ref[4, bi, pl.ds(bj, 1), :] * jnp.exp2(-bx * bx - by * by)
            c0 = c0 * present_ref[t * 9 + w]
            c1 = c0 * pad_ref[2, bi, pl.ds(bj, 1), :]
            c2 = c0 * pad_ref[3, bi, pl.ds(bj, 1), :]
            window.append((2.0 * bx, 2.0 * by, c0, c1, c2))
        acc = [jnp.zeros((128, 128), F32)] * 3
        for bx, by, *carried in window:
            weights = jnp.exp2(x_col * bx + y_col * by)
            acc = [total + weights * c for total, c in zip(acc, carried)]
        scale = jnp.exp2(-x * x - y * y)
        for k in range(3):
            sums_ref[k, pl.ds(t, 1), :] = jnp.sum(acc[k].T, axis=0, keepdims=True) * scale
        return carry

    lax.fori_loop(0, rows * cols, tile, 0, unroll=4)


def pack(dest_ref, vals_ref, rank_ref, send_ref, left_ref, slots_ref, acc_ref):
    groups = dest_ref.shape[0] // 8
    d_iota = iota((128, 128), 0)
    before = jnp.concatenate(
        [
            (iota((128, 128), 0) < iota((128, 128), 1)).astype(F32),
            jnp.ones((128, 128), F32),
        ],
        1,
    ).astype(BF16)
    p_iota = iota((192, 128), 0).astype(F32)
    acc_ref[...] = jnp.zeros_like(acc_ref)

    def group(g, running):
        dest8 = dest_ref[pl.ds(g * 8, 8), :]
        vals8 = [split2(vals_ref[k, pl.ds(g * 8, 8), :]) for k in range(4)]
        ranks = []
        for r in range(8):
            hit = d_iota == jnp.broadcast_to(dest8[r : r + 1], (128, 128))
            counts = dot(jnp.where(hit, 1.0, 0.0).astype(BF16), before, NN)
            rank = jnp.sum(
                jnp.where(hit, counts[:, :128] + running, 0.0), axis=0, keepdims=True
            )
            running = running + counts[:, 128:]
            ranks.append(rank)
            lanes = slice(r * 128, r * 128 + 128)
            slots_ref[:, lanes] = jnp.where(
                p_iota == jnp.broadcast_to(rank, (192, 128)), 1.0, 0.0
            ).astype(BF16)
            for part in range(2):
                for k in range(4):
                    v = jnp.broadcast_to(vals8[k][part][r : r + 1], (128, 128))
                    at = (part * 4 + k) * 128
                    left_ref[at : at + 128, lanes] = jnp.where(hit, v, 0.0).astype(BF16)
        rank_ref[pl.ds(g * 8, 8), :] = jnp.concatenate(ranks, 0)
        acc_ref[:, 0:192] += dot(left_ref[...], slots_ref[...], NT)
        return running

    lax.fori_loop(0, groups, group, jnp.zeros((128, 128), F32))
    tails = []
    for k in range(4):
        send_ref[pl.ds(k, 128, stride=8), :] = acc_ref[k * 128 : k * 128 + 128, 0:128] + acc_ref[
            512 + k * 128 : 640 + k * 128, 0:128
        ]
        tails.append(
            acc_ref[k * 128 : k * 128 + 128, 128:256]
            + acc_ref[512 + k * 128 : 640 + k * 128, 128:256]
        )
    low_half = iota((128, 128), 1) < 64
    for k in range(6, 8):
        send_ref[pl.ds(k, 128, stride=8), :] = jnp.zeros((128, 128), F32)
    for h in range(2):
        send_ref[pl.ds(4 + h, 128, stride=8), :] = jnp.where(
            low_half, tails[2 * h], pltpu.roll(tails[2 * h + 1], 64, 1)
        )


def vmem():
    return pl.BlockSpec(memory_space=pltpu.VMEM)


MESH = pl.DeviceIdType.MESH
AROUND = [(-1, 0), (1, 0), (0, -1), (0, 1), (-1, -1), (-1, 1), (1, -1), (1, 1)]


def my_place():
    return lax.axis_index("along"), lax.axis_index("cross")


def sizes():
    return lax.axis_size("along"), lax.axis_size("cross")


def at_step(step):
    (a, c), (na, nc) = my_place(), sizes()
    return lax.rem(a + step[0] + na, na), lax.rem(c + step[1] + nc, nc)


def greet_around():
    barrier = pltpu.get_barrier_semaphore()
    for step in AROUND:
        pl.semaphore_signal(barrier, inc=1, device_id=at_step(step), device_id_type=MESH)
    pl.semaphore_wait(barrier, len(AROUND))


def rim_copies(out_refs, in_refs, send_sem, recv_sem):
    copies = []
    for n, step in enumerate(AROUND):
        opposite = AROUND.index((-step[0], -step[1]))
        copies.append(
            pltpu.make_async_remote_copy(
                src_ref=out_refs[n],
                dst_ref=in_refs[opposite],
                send_sem=send_sem.at[n],
                recv_sem=recv_sem.at[opposite],
                device_id=at_step(step),
                device_id_type=MESH,
            )
        )
    return copies


DEEP = 4
SIDE_PARTICLES = 24


def column_strip(fields, right):
    lanes = iota((fields[0].shape[0], 128), 1)
    out = jnp.zeros((fields[0].shape[0], 128), F32)
    for f, field in enumerate(fields):
        turn = DEEP * f + (DEEP if right else 0)
        moved = pltpu.roll(field, turn, 1) if turn else field
        out = jnp.where((lanes >= DEEP * f) & (lanes < DEEP * f + DEEP), moved, out)
    return out


def write_rims(out_refs, base, fields):
    top, bottom = slice(0, 8), slice(120, 128)
    for n, rows in ((0, top), (1, bottom)):
        for f, field in enumerate(fields):
            for b in range(4):
                at = base[n] + (f * 4 + b) * 8
                out_refs[n][at : at + 8, :] = field(rows, slice(b * 128, b * 128 + 128))
    for right in range(2):
        lanes = slice(384, 512) if right else slice(0, 128)
        strip = column_strip([field(slice(0, 128), lanes) for field in fields], right == 1)
        at = base[2 + right]
        out_refs[2 + right][at : at + 128, :] = strip
        out_refs[4 + right][base[4] : base[4] + 8, :] = strip[0:8]
        out_refs[6 + right][base[4] : base[4] + 8, :] = strip[120:128]


def rims_kernel(
    off_ref, vel_ref, mass_ref, surface_ref, depth_ref,
    pad_ref, up_ref, down_ref, left_ref, right_ref, c0_ref, c1_ref, c2_ref, c3_ref,
    o0, o1, o2, o3, o4, o5, o6, o7, i0, i1, i2, i3, i4, i5, i6, i7, send_sem, recv_sem,
):
    outs = [o0, o1, o2, o3, o4, o5, o6, o7]
    ins = [i0, i1, i2, i3, i4, i5, i6, i7]
    rows, cols = mass_ref.shape[0], mass_ref.shape[1]
    particle = [
        (off_ref, 0), (off_ref, 1), (vel_ref, 0), (vel_ref, 1), (mass_ref, None),
    ]

    def tiles(f, i, j):
        ref, part = particle[f]
        return ref[i, j, :] if part is None else ref[part, i, j, :]

    everything = slice(0, cols)
    for f in range(5):
        outs[0][f * cols : (f + 1) * cols, :] = tiles(f, 0, everything)
        outs[1][f * cols : (f + 1) * cols, :] = tiles(f, rows - 1, everything)
        for side, j in ((0, slice(0, 1)), (1, slice(cols - 1, cols))):
            for i in range(rows):
                outs[2 + side][f * rows + i : f * rows + i + 1, :] = tiles(f, i, j)
            outs[4 + side][f : f + 1, :] = tiles(f, 0, j)
            outs[6 + side][f : f + 1, :] = tiles(f, rows - 1, j)
    for side in range(2):
        outs[2 + side][5 * rows :SIDE_PARTICLES, :] = jnp.zeros((SIDE_PARTICLES - 5 * rows, 128), F32)
        outs[4 + side][5:8, :] = jnp.zeros((3, 128), F32)
        outs[6 + side][5:8, :] = jnp.zeros((3, 128), F32)
    fields = [
        lambda r, c: surface_ref[0, r, c],
        lambda r, c: surface_ref[1, r, c],
        lambda r, c: surface_ref[2, r, c],
        lambda r, c: depth_ref[r, c],
    ]
    write_rims(outs, [5 * cols, 5 * cols, SIDE_PARTICLES, SIDE_PARTICLES, 8], fields)
    greet_around()
    copies = rim_copies(outs, ins, send_sem, recv_sem)
    for copy in copies:
        copy.start()
    for f in range(5):
        for i in range(rows):
            pad_ref[f, i + 1, 1 : cols + 1, :] = tiles(f, i, everything)
    for copy in copies:
        copy.wait()
    (a, c), (na, nc) = my_place(), sizes()
    inside = [a > 0, a < na - 1, c > 0, c < nc - 1]

    def kept(f, value, *tests):
        if f < 4:
            return value
        for test in tests:
            value = jnp.where(test, value, 0.0)
        return value

    for f in range(5):
        pad_ref[f, 0, 1 : cols + 1, :] = kept(f, ins[0][f * cols : (f + 1) * cols, :], inside[0])
        pad_ref[f, rows + 1, 1 : cols + 1, :] = kept(f, ins[1][f * cols : (f + 1) * cols, :], inside[1])
        for side, j in ((0, 0), (1, cols + 1)):
            for i in range(rows):
                pad_ref[f, i + 1, j : j + 1, :] = kept(
                    f, ins[2 + side][f * rows + i : f * rows + i + 1, :], inside[2 + side]
                )
            pad_ref[f, 0, j : j + 1, :] = kept(f, ins[4 + side][f : f + 1, :], inside[0], inside[2 + side])
            pad_ref[f, rows + 1, j : j + 1, :] = kept(f, ins[6 + side][f : f + 1, :], inside[1], inside[2 + side])
    up_ref[...] = ins[0][5 * cols : 5 * cols + 128, :]
    down_ref[...] = ins[1][5 * cols : 5 * cols + 128, :]
    left_ref[...] = ins[2][SIDE_PARTICLES : SIDE_PARTICLES + 128, :]
    right_ref[...] = ins[3][SIDE_PARTICLES : SIDE_PARTICLES + 128, :]
    for n, ref in enumerate((c0_ref, c1_ref, c2_ref, c3_ref)):
        ref[...] = ins[4 + n][8:16, :]


def rims_call(offsets, velocity, mass, surface, depth):
    rows, cols = mass.shape[0], mass.shape[1]
    tall, wide, corner = 5 * cols + 128, SIDE_PARTICLES + 128, 16
    heights = [tall, tall, wide, wide, corner, corner, corner, corner]
    buffers = [pltpu.VMEM((h, 128), F32) for h in heights]
    return pl.pallas_call(
        rims_kernel,
        out_shape=(
            jax.ShapeDtypeStruct((5, rows + 2, cols + 2, 128), F32),
            *[jax.ShapeDtypeStruct((128, 128), F32)] * 4,
            *[jax.ShapeDtypeStruct((8, 128), F32)] * 4,
        ),
        in_specs=[vmem()] * 5,
        out_specs=tuple([vmem()] * 9),
        scratch_shapes=[
            *buffers,
            *buffers,
            pltpu.SemaphoreType.DMA((8,)),
            pltpu.SemaphoreType.DMA((8,)),
        ],
        compiler_params=pltpu.CompilerParams(
            vmem_limit_bytes=VMEM_LIMIT, collective_id=0, has_side_effects=True
        ),
        name="rims",
    )(offsets, velocity, mass, surface, depth)


def unpack(back_ref, dest_ref, rank_ref, out_ref, table_ref):
    tail = back_ref[pl.ds(3, 128, stride=8), :]
    tails = [tail, pltpu.roll(tail, 64, 1), back_ref[pl.ds(4, 128, stride=8), :]]
    for k in range(3):
        for part, piece in enumerate(split2(back_ref[pl.ds(k, 128, stride=8), :])):
            table_ref[k * 128 : k * 128 + 128, part * 192 : part * 192 + 128] = piece.astype(BF16)
        for part, piece in enumerate(split2(tails[k])):
            table_ref[
                k * 128 : k * 128 + 128, part * 192 + 128 : part * 192 + 192
            ] = piece[:, 0:64].astype(BF16)
    d_iota = iota((128, 128), 0)
    p_iota = iota((192, 128), 0).astype(F32)

    def step(g, carry):
        at = pl.ds(g * 8, 8)
        dest8 = dest_ref[at, :]
        rank8 = rank_ref[at, :]
        found = [[], [], []]
        for pair in range(4):
            slots = jnp.concatenate(
                [
                    jnp.where(
                        p_iota == jnp.broadcast_to(rank8[r : r + 1], (192, 128)), 1.0, 0.0
                    ).astype(BF16)
                    for r in (2 * pair, 2 * pair + 1)
                ],
                1,
            )
            got = dot(table_ref[...], jnp.concatenate([slots, slots], 0), NN)
            for k in range(3):
                for h in range(2):
                    r = 2 * pair + h
                    hit = d_iota == jnp.broadcast_to(dest8[r : r + 1], (128, 128))
                    part = got[k * 128 : k * 128 + 128, h * 128 : h * 128 + 128]
                    found[k].append(jnp.sum(jnp.where(hit, part, 0.0), axis=0, keepdims=True))
        for k in range(3):
            out_ref[k, at, :] = jnp.concatenate(found[k], 0)
        return carry

    lax.fori_loop(0, dest_ref.shape[0] // 8, step, 0)


GROUPS = 4
PER_GROUP = 32
STEP = 8


def row_and_column(cell):
    row = jnp.floor(cell * (1.0 / 512.0))
    return row, cell - row * 512.0


def unfold(got_ref, slots_ref, group):
    low_half = iota((16, 128), 1) < 64
    first_row = group * PER_GROUP * 8
    for k in range(4):
        slots_ref[k, 0:32, :] = got_ref[pl.ds(first_row + k, 32, stride=8), :]
        row = got_ref[pl.ds(first_row + 4 + k // 2, 32, stride=8), :]
        first, second = row[0:16], row[16:32]
        if k % 2 == 0:
            full = jnp.where(low_half, first, pltpu.roll(second, 64, 1))
        else:
            full = jnp.where(low_half, pltpu.roll(first, 64, 1), second)
        slots_ref[k, 32:48, :] = full


def deposit_group(group, slots_ref, cells_ref, left_ref, right_ref, acc_ref):
    r_iota = iota((128, 128), 0).astype(F32)
    c_iota = iota((512, 128), 0).astype(F32)
    cells_ref[pl.ds(pl.multiple_of(group * 48, 8), 48), :] = slots_ref[0]

    def step(g, carry):
        at = pl.ds(pl.multiple_of(g * STEP, STEP), STEP)
        row8, col8 = row_and_column(slots_ref[0, at, :])
        vals8 = [split2(slots_ref[1 + k, at, :]) for k in range(3)]
        for r in range(STEP):
            lanes = slice(r * 128, r * 128 + 128)
            hit = r_iota == jnp.broadcast_to(row8[r : r + 1], (128, 128))
            for part in range(2):
                for k in range(3):
                    v = jnp.broadcast_to(vals8[k][part][r : r + 1], (128, 128))
                    base = (part * 3 + k) * 128
                    left_ref[base : base + 128, lanes] = jnp.where(hit, v, 0.0).astype(BF16)
            right_ref[:, lanes] = jnp.where(
                c_iota == jnp.broadcast_to(col8[r : r + 1], (512, 128)), 1.0, 0.0
            ).astype(BF16)
        acc_ref[...] += dot(left_ref[...], right_ref[...], NT)
        return carry

    lax.fori_loop(0, 48 // STEP, step, 0)


def lookup_group(group, cells_ref, table_ref, found_ref, back_ref):
    r_iota = iota((128, 128), 0).astype(F32)
    c_iota = iota((512, 128), 0).astype(F32)

    def step(g, carry):
        at = pl.ds(pl.multiple_of(group * 48 + g * 8, 8), 8)
        row8, col8 = row_and_column(cells_ref[at, :])
        found = [[], [], []]
        for pair in range(4):
            right = jnp.concatenate(
                [
                    jnp.where(
                        c_iota == jnp.broadcast_to(col8[r : r + 1], (512, 128)), 1.0, 0.0
                    ).astype(BF16)
                    for r in (2 * pair, 2 * pair + 1)
                ],
                1,
            )
            got = dot(table_ref[...], jnp.concatenate([right, right], 0), NN)
            for k in range(3):
                for h in range(2):
                    r = 2 * pair + h
                    hit = r_iota == jnp.broadcast_to(row8[r : r + 1], (128, 128))
                    part = got[k * 128 : k * 128 + 128, h * 128 : h * 128 + 128]
                    found[k].append(jnp.sum(jnp.where(hit, part, 0.0), axis=0, keepdims=True))
        for k in range(3):
            found_ref[k, pl.ds(pl.multiple_of(g * 8, 8), 8), :] = jnp.concatenate(found[k], 0)
        return carry

    lax.fori_loop(0, 6, step, 0)
    low_half = iota((16, 128), 1) < 64
    first_row = group * PER_GROUP * 8
    tails = [found_ref[k, 32:48, :] for k in range(3)]
    turned = [pltpu.roll(t, 64, 1) for t in tails]
    for k in range(3):
        back_ref[pl.ds(first_row + k, 32, stride=8), :] = found_ref[k, 0:32, :]
    back_ref[pl.ds(first_row + 3, 16, stride=8), :] = jnp.where(low_half, tails[0], turned[1])
    back_ref[pl.ds(first_row + 131, 16, stride=8), :] = jnp.where(low_half, turned[0], tails[1])
    back_ref[pl.ds(first_row + 4, 16, stride=8), :] = tails[2]
    back_ref[pl.ds(first_row + 132, 16, stride=8), :] = turned[2]
    for k in range(5, 8):
        back_ref[pl.ds(first_row + k, 32, stride=8), :] = jnp.zeros((32, 128), F32)


TALL = 136
BROAD = 640


def place_rims(wide_ref, index, f, refs, bases):
    up, down, left, right, *corners = refs
    upper_half = iota((8, 128), 0) < 4
    for b in range(4):
        at = bases[0] + (f * 4 + b) * 8
        wide_ref[index, 128:136, b * 128 : b * 128 + 128] = jnp.where(
            upper_half, down[at : at + 8, :], up[at : at + 8, :]
        )
    to_left = (128 - DEEP - DEEP * f) % 128
    to_right = (128 - DEEP * f) % 128

    def strip(left_part, right_part):
        moved_left = pltpu.roll(left_part, to_left, 1) if to_left else left_part
        moved_right = pltpu.roll(right_part, to_right, 1) if to_right else right_part
        return jnp.where(iota(left_part.shape, 1) < 64, moved_right, moved_left)

    sides = slice(bases[1], bases[1] + 128)
    wide_ref[index, 0:128, 512:640] = strip(left[sides, :], right[sides, :])
    rows = slice(bases[2], bases[2] + 8)
    c = [
        jnp.where(upper_half, corners[2 + side][rows, :], corners[side][rows, :])
        for side in range(2)
    ]
    wide_ref[index, 128:136, 512:640] = strip(c[0], c[1])


def inside_grid(block):
    (a, c), (na, nc) = my_place(), sizes()
    cols = iota((8, BROAD), 1)
    cols = jnp.where(cols < 576, cols, cols - BROAD) + c * 512
    rows = iota((8, BROAD), 0) + block * 8
    rows = jnp.where(rows < 132, rows, rows - TALL) + a * 128
    return (cols >= 0) & (cols < nc * 512) & (rows >= 0) & (rows < na * 128)


def water_step(old_ref, new_ref, depth_ref, source_ref):
    blocks = TALL // 8
    sub = iota((8, BROAD), 0)

    def load(block):
        at = slice(block * 8, block * 8 + 8)
        h, u, v = [old_ref[f, at, :] for f in range(3)]
        fu = depth_ref[0, at, :] * u
        fields = (h, u, v, fu)
        return fields, [pltpu.roll(x, 1, 0) for x in fields], [pltpu.roll(x, 7, 0) for x in fields]

    def left(x):
        return pltpu.roll(x, 1, 1)

    def right(x):
        return pltpu.roll(x, BROAD - 1, 1)

    before, here = load(blocks - 1), load(0)
    for block in range(blocks):
        after = load((block + 1) % blocks)
        at = slice(block * 8, block * 8 + 8)
        (h, u, v, _), down, up = here
        h_w, u_w, v_w, fu_w = [jnp.where(sub == 0, p, q) for p, q in zip(before[1], down)]
        h_e, u_e, v_e, fu_e = [jnp.where(sub == 7, p, q) for p, q in zip(after[2], up)]
        fv = depth_ref[0, at, :] * v
        h_s, h_n = left(h), right(h)
        next_h = 0.25 * (h_e + h_w + h_n + h_s) - 0.5 * courant * (
            fu_e - fu_w + right(fv) - left(fv)
        )
        next_u = 0.25 * (u_e + u_w + right(u) + left(u)) - 0.5 * courant * (h_e - h_w)
        next_v = 0.25 * (v_e + v_w + right(v) + left(v)) - 0.5 * courant * (h_n - h_s)
        inside = inside_grid(block)
        for f, value in enumerate((next_h, next_u, next_v)):
            new_ref[f, at, :] = jnp.where(inside, value + source_ref[f, at, :], 0.0)
        before, here = here, after


def main_kernel(
    pad_ref, present_ref, dest_ref, cell_ref, surface_ref, depth_ref,
    up_ref, down_ref, left_in, right_in, c0_ref, c1_ref, c2_ref, c3_ref,
    dens_ref, state_ref, feed_ref,
    sums_ref, vals_ref, pleft_ref, pslots_ref, pacc_ref, rank_ref, send_ref, got_ref,
    slots_ref, cells_ref, left_ref, right_ref, acc_ref,
    even, odd, deep, wide_source,
    table_ref, found_ref, back_ref, back_got, utable_ref,
    o0, o1, o2, o3, o4, o5, o6, o7, i0, i1, i2, i3, i4, i5, i6, i7,
    rim_send, rim_recv, out_sem, in_sem, back_out_sem, back_in_sem,
):
    (a, c), (na, nc) = my_place(), sizes()
    count = na * nc
    me = a * nc + c

    def device(n):
        return (lax.div(n, nc), lax.rem(n, nc))

    def block(n):
        return pl.ds(pl.multiple_of(n * 8, 8), 8)

    barrier = pltpu.get_barrier_semaphore()

    def greet(step, carry):
        pl.semaphore_signal(
            barrier, inc=1, device_id=device(lax.rem(me + step, count)), device_id_type=MESH
        )
        return carry

    lax.fori_loop(1, count, greet, 0)

    window_sums(pad_ref, present_ref, sums_ref)
    rows, cols = pad_ref.shape[1] - 2, pad_ref.shape[2] - 2
    for i in range(rows):
        at = slice(i * cols, (i + 1) * cols)
        s0 = sums_ref[0, at, :]
        density = s0 / 128.0
        dens_ref[at, :] = density
        volume = pad_ref[4, i + 1, 1 : cols + 1, :] / density
        vals_ref[0, at, :] = cell_ref[at, :].astype(F32)
        vals_ref[1, at, :] = volume
        vals_ref[2, at, :] = volume * (sums_ref[1, at, :] / s0)
        vals_ref[3, at, :] = volume * (sums_ref[2, at, :] / s0)
    pack(dest_ref, vals_ref, rank_ref, send_ref, pleft_ref, pslots_ref, pacc_ref)

    pl.semaphore_wait(barrier, count - 1)

    def send_out(group):
        def start(step, carry):
            to = lax.rem(me + step, count)
            pltpu.make_async_remote_copy(
                src_ref=send_ref.at[block(to), :],
                dst_ref=got_ref.at[block(step), :],
                send_sem=out_sem,
                recv_sem=in_sem.at[group],
                device_id=device(to),
                device_id_type=MESH,
            ).start()
            return carry

        lax.fori_loop(max(1, group * PER_GROUP), (group + 1) * PER_GROUP, start, 0)

    for group in range(GROUPS):
        send_out(group)
    got_ref[0:8, :] = send_ref[block(me), :]

    rims = [up_ref, down_ref, left_in, right_in, c0_ref, c1_ref, c2_ref, c3_ref]
    for f in range(3):
        even[f, 0:128, 0:512] = surface_ref[f]
        place_rims(even, f, f, rims, [0, 0, 0])
    deep[0, 0:128, 0:512] = depth_ref[...]
    place_rims(deep, 0, 3, rims, [0, 0, 0])
    for b in range(TALL // 8):
        at = slice(b * 8, b * 8 + 8)
        for f in range(3):
            even[f, at, :] = jnp.where(inside_grid(b), even[f, at, :], 0.0)

    acc_ref[...] = jnp.zeros_like(acc_ref)
    for group in range(GROUPS):
        landed = got_ref.at[max(8, group * PER_GROUP * 8) : (group + 1) * PER_GROUP * 8, :]
        pltpu.make_async_copy(landed, landed, in_sem.at[group]).wait()
        unfold(got_ref, slots_ref, group)
        deposit_group(group, slots_ref, cells_ref, left_ref, right_ref, acc_ref)
    for k in range(3):
        wide_source[k, 0:128, 0:512] = (
            acc_ref[k * 128 : k * 128 + 128, :] + acc_ref[384 + k * 128 : 512 + k * 128, :]
        )

    outs = [o0, o1, o2, o3, o4, o5, o6, o7]
    ins = [i0, i1, i2, i3, i4, i5, i6, i7]
    write_rims(outs, [0, 0, 0, 0, 0], [
        lambda r, c: wide_source[0, r, c],
        lambda r, c: wide_source[1, r, c],
        lambda r, c: wide_source[2, r, c],
    ])
    copies = rim_copies(outs, ins, rim_send, rim_recv)
    for copy in copies:
        copy.start()
    for copy in copies:
        copy.wait()
    for f in range(3):
        place_rims(wide_source, f, f, ins, [0, 0, 0])

    def two_steps(n, carry):
        water_step(even, odd, deep, wide_source)
        water_step(odd, even, deep, wide_source)
        return carry

    lax.fori_loop(0, SUBSTEPS // 2, two_steps, 0)
    for k in range(3):
        value = even[k, 0:128, 0:512]
        state_ref[k] = value
        hi, lo = split2(value)
        table_ref[k * 128 : k * 128 + 128, 0:512] = hi.astype(BF16)
        table_ref[k * 128 : k * 128 + 128, 512:1024] = lo.astype(BF16)

    for group in range(GROUPS):
        lookup_group(group, cells_ref, table_ref, found_ref, back_ref)

        def start(step, carry):
            pltpu.make_async_remote_copy(
                src_ref=back_ref.at[block(step), :],
                dst_ref=back_got.at[block(me), :],
                send_sem=back_out_sem,
                recv_sem=back_in_sem,
                device_id=device(lax.rem(me - step + count, count)),
                device_id_type=MESH,
            ).start()
            return carry

        lax.fori_loop(max(1, group * PER_GROUP), (group + 1) * PER_GROUP, start, 0)
    back_got[block(me), :] = back_ref[0:8, :]
    others = (count - 1) * 8
    for ref, sem in (
        (back_got, back_in_sem),
        (send_ref, out_sem),
        (back_ref, back_out_sem),
    ):
        pltpu.make_async_copy(ref.at[0:others, :], ref.at[0:others, :], sem).wait()
    unpack(back_got, dest_ref, rank_ref, feed_ref, utable_ref)


def main_call(pad, present, dest, cell, surface, depth, rims):
    heights = [96, 96, 128, 128, 8, 8, 8, 8]
    buffers = [pltpu.VMEM((h, 128), F32) for h in heights]
    dma = pltpu.SemaphoreType.DMA
    return pl.pallas_call(
        main_kernel,
        out_shape=(
            jax.ShapeDtypeStruct((64, 128), F32),
            jax.ShapeDtypeStruct((3, 128, 512), F32),
            jax.ShapeDtypeStruct((3, 64, 128), F32),
        ),
        in_specs=[vmem(), pl.BlockSpec(memory_space=pltpu.SMEM)] + [vmem()] * 12,
        out_specs=(vmem(), vmem(), vmem()),
        scratch_shapes=[
            pltpu.VMEM((3, 64, 128), F32),
            pltpu.VMEM((4, 64, 128), F32),
            pltpu.VMEM((1024, 1024), BF16),
            pltpu.VMEM((192, 1024), BF16),
            pltpu.VMEM((1024, 256), F32),
            pltpu.VMEM((64, 128), F32),
            pltpu.VMEM((1024, 128), F32),
            pltpu.VMEM((1024, 128), F32),
            pltpu.VMEM((4, 48, 128), F32),
            pltpu.VMEM((192, 128), F32),
            pltpu.VMEM((768, STEP * 128), BF16),
            pltpu.VMEM((512, STEP * 128), BF16),
            pltpu.VMEM((768, 512), F32),
            pltpu.VMEM((3, TALL, BROAD), F32),
            pltpu.VMEM((3, TALL, BROAD), F32),
            pltpu.VMEM((1, TALL, BROAD), F32),
            pltpu.VMEM((3, TALL, BROAD), F32),
            pltpu.VMEM((384, 1024), BF16),
            pltpu.VMEM((3, 48, 128), F32),
            pltpu.VMEM((1024, 128), F32),
            pltpu.VMEM((1024, 128), F32),
            pltpu.VMEM((384, 384), BF16),
            *buffers,
            *buffers,
            dma((8,)),
            dma((8,)),
            dma,
            dma((GROUPS,)),
            dma,
            dma,
        ],
        compiler_params=pltpu.CompilerParams(
            vmem_limit_bytes=VMEM_LIMIT, collective_id=1, has_side_effects=True
        ),
        name="main",
    )(pad, present, dest, cell, surface, depth, *rims)


def shards(
    offsets, velocity, particle_mass, neighbours, owner_device, target_cell, surface, water_depth
):
    padded, *rims = rims_call(offsets, velocity, particle_mass, surface, water_depth)
    present = jnp.any(
        neighbours[..., :, None] == jnp.arange(9, dtype=jnp.int32), axis=-2
    ).astype(F32)
    density, water_state, feedback = main_call(
        padded,
        present.reshape(-1),
        owner_device.reshape(64, 128),
        target_cell.reshape(64, 128),
        surface,
        water_depth,
        rims,
    )
    return (
        water_state,
        density.reshape(particle_mass.shape),
        feedback.reshape((3,) + particle_mass.shape),
    )


def solution(mesh):
    in_specs = (
        P(None, "along", "cross", None),
        P(None, "along", "cross", None),
        P("along", "cross", None),
        P("along", "cross", None),
        P("along", "cross", None, None),
        P("along", "cross", None),
        P(None, "along", "cross"),
        P("along", "cross"),
    )
    out_specs = (
        P(None, "along", "cross"),
        P("along", "cross", None),
        P(None, "along", "cross", None),
    )
    return jax.shard_map(shards, mesh=mesh, in_specs=in_specs, out_specs=out_specs, check_vma=False)
```

time: 1520 us -> 137 us (0.09)
  local copies, waits for them, and re-layouts: 778 us -> 4.19 us
  other arithmetic: 470 us -> 0.8 us
  Pallas kernels: 0 us -> 131 us
  starting transfers between devices: 123 us -> 0 us
  matrix products: 78.2 us -> 0 us
  waiting for transfers between devices: 52 us -> 0 us
    gather x2 -> x0, local copies, waits for them, and re-layouts: 649 us -> none  [the longest x1 408 us: shards(): looked = water_state.reshape(-1)[cell_index].reshape(3, devices, capacity)]
    scatter-add x1 -> x0, other arithmetic: 452 us -> none  [shards(): jnp.zeros((3 * cell_count,), jnp.float32).at[cell_index]]
    pallas_call x0 -> x2, Pallas kernels: none -> 131 us  [the longest x1 115 us: main_call(): pl.pallas_call(main_kernel, out_shape=(jax.ShapeDtypeStruct((64, 128), F3...]
    scatter x1 -> x0, local copies, waits for them, and re-layouts: 120 us -> none  [shards(): jnp.zeros((4 * slot_total,), jnp.float32).at[send_index]]
    ppermute x24 -> x0, starting transfers between devices: 95.7 us -> none  [the longest x12 76.4 us: padded_2(): lax.ppermute(tail, axis, [(i, (i + 1) % count) for i in range(ends)])]
    dot_general x37 -> x0, matrix products: 78.2 us -> none  [the longest x36 75.8 us: tile_sums(): jnp.einsum('tab,ktb->kta', weights, carried, precision=lax.Precision.HIGH...]
    ppermute x24 -> x0, waiting for transfers between devices: 27.6 us -> none  [the longest x12 25.7 us: padded_2(): lax.ppermute(head, axis, [((i + 1) % count, i) for i in range(ends)])]
    all_to_all x2 -> x0, starting transfers between devices: 27.1 us -> none  [the longest x1 14.8 us: shards(): lax.all_to_all(outgoing, ('along', 'cross'), split_axis=1, concat_axis=1,...]
  transfers between devices with their start and end apart: 26 -> 0, of which waited for: 12 -> 0; matrix products, arithmetic and copies ran while one was open for 1% -> 0% of each run, Pallas kernels for 0% -> 0%
where the time goes in v3:
time: 137 us; the launch traced here: 136 us
  Pallas kernels  131 us (96%)
  local copies, waits for them, and re-layouts  4.19 us (3%)
    pallas_call x1, Pallas kernels, main_call(): pl.pallas_call(main_kernel, out_shape=(jax.ShapeDtypeStruct((64, 128), F3...  115 us
    pallas_call x1, Pallas kernels, rims_call(): pl.pallas_call(rims_kernel, out_shape=(jax.ShapeDtypeStruct((5, rows + 2,...  15.4 us
    unnamed x7, local copies, waits for them, and re-layouts  3.36 us

profile of v3, /device:TPU:1, one launch (start us, length us, event | category | flops | bytes accessed | tf_op | source)
XLA Modules:
  0.0 136.3 jit_solution(5481059787845378235)
XLA Ops:
  0.6 0.8 fusion
  1.4 0.1 copy.13
  1.5 0.7 reshape.27.present_ref
  2.3 15.4 %rims.1 = (f32[5,6,18,128]{3,2,1,0:T(8,128)}, f32[128,128]{1,0:T(8,128)}, f32[128,128]{1,0:T(8,128)}, f32[128,128]{1,0:T(8,128)}, f32[128,128]{1,0:T(8,128)}, /*...) custom-call(f32[2,4,16,128]{3,2,1,0:T(8,128)} %off_ref.1, f32[2,4,16,128]{3,2,1,0:T(8,128)} %vel_ref.1, ...), custom_call_target="tpu_custom_call" | custom-call | tf_op jit(solution)/shard_map/rims/pallas_call | solution.py:276
  17.7 115.2 %main.1 = (f32[64,128]{1,0:T(8,128)}, f32[3,128,512]{2,1,0:T(8,128)}, f32[3,64,128]{2,1,0:T(8,128)}) custom-call(f32[5,6,18,128]{3,2,1,0:T(8,128)} %get-tuple-element.15.pad_ref, f32[576]{0:T(1024)} %reshape.27.present_ref, s32[64,128]{1,0:T(8,128)} %bitcast.5, s32[64,128]{1,0:T(8,128)} %bitcast.6, f32[3,128,512]{2,1,0:T(8,128)} %surface_ref.3, ...), custom_call_target="tpu_custom_call" | custom-call | tf_op jit(solution)/shard_map/main/pallas_call | solution.py:656
  132.9 0.0 copy-start.1
  132.9 0.0 copy-start
  132.9 2.1 %copy.17 = f32[3,128,512]{2,1,0:T(8,128)} copy(f32[3,128,512]{2,1,0:T(8,128)} %get-tuple-element.30) | data formatting | bytes 1572864
  135.0 0.0 copy-done.1
  135.0 0.6 copy.18
  135.7 0.0 copy-done
  135.7 0.6 copy.19
  (1 shorter events, 0.0 us)
Async XLA Ops:
  132.9 2.1 %copy-start.1 = (f32[64,128]{1,0:T(8,128)S(1)}, f32[64,128]{1,0:T(8,128)}, u32[]{:S(2)}) copy-start(f32[64,128]{1,0:T(8,128)} %get-tuple-element.25) | copy-start | bytes 98308
  132.9 2.7 %copy-start = (f32[3,64,128]{2,1,0:T(8,128)S(1)}, f32[3,64,128]{2,1,0:T(8,128)}, u32[]{:S(2)}) copy-start(f32[3,64,128]{2,1,0:T(8,128)} %get-tuple-element.26) | copy-start | bytes 294916

commit v4 on v3

--- a/solution.py
+++ b/solution.py
@@ -11,6 +11,7 @@
 KAPPA = math.sqrt(math.log2(math.e))
 F32 = jnp.float32
 BF16 = jnp.bfloat16
+F8 = jnp.float8_e4m3fn
 NN = (((1,), (0,)), ((), ()))
 NT = (((1,), (1,)), ((), ()))
 VMEM_LIMIT = 56 * 1024 * 1024
@@ -27,27 +28,51 @@
     return hi, x - hi
 
 
+def split8(x):
+    t0 = x.astype(F8).astype(F32)
+    r = (x - t0) * 16.0
+    t1 = r.astype(F8).astype(F32)
+    return t0, t1, (r - t1) * 16.0
+
+
 def iota(shape, dim):
     return lax.broadcasted_iota(jnp.int32, shape, dim)
 
 
-def window_sums(pad_ref, present_ref, sums_ref):
+def window_sums(pad_ref, near_ref, dest_ref, sums_ref, rank_ref):
     rows, cols = pad_ref.shape[1] - 2, pad_ref.shape[2] - 2
-
-    def tile(t, carry):
+    d_iota = iota((128, 128), 0)
+    before = jnp.concatenate(
+        [
+            (iota((128, 128), 0) < iota((128, 128), 1)).astype(F32),
+            jnp.ones((128, 128), F32),
+        ],
+        1,
+    ).astype(BF16)
+
+    def tile(t, running):
+        hit = d_iota == jnp.broadcast_to(dest_ref[pl.ds(t, 1), :], (128, 128))
+        counts = dot(jnp.where(hit, 1.0, 0.0).astype(BF16), before, NN)
+        rank_ref[pl.ds(t, 1), :] = jnp.sum(
+            jnp.where(hit, counts[:, :128] + running, 0.0), axis=0, keepdims=True
+        )
+        running = running + counts[:, 128:]
         i = t // cols
         j = t - i * cols
         x = pad_ref[0, i + 1, pl.ds(j + 1, 1), :] * KAPPA
         y = pad_ref[1, i + 1, pl.ds(j + 1, 1), :] * KAPPA
         x_col = jnp.broadcast_to(x, (128, 128)).T
         y_col = jnp.broadcast_to(y, (128, 128)).T
+        listed = jnp.int32(0)
+        for slot in range(9):
+            listed = listed | lax.shift_left(jnp.int32(1), near_ref[slot, i, j] + 1)
         window = []
         for w in range(9):
             bi, bj = i + w // 3, j + w % 3
             bx = (pad_ref[0, bi, pl.ds(bj, 1), :] + (w // 3 - 1.0)) * KAPPA
             by = (pad_ref[1, bi, pl.ds(bj, 1), :] + (w % 3 - 1.0)) * KAPPA
             c0 = pad_ref[4, bi, pl.ds(bj, 1), :] * jnp.exp2(-bx * bx - by * by)
-            c0 = c0 * present_ref[t * 9 + w]
+            c0 = c0 * (lax.shift_right_logical(listed, w + 1) & 1).astype(F32)
             c1 = c0 * pad_ref[2, bi, pl.ds(bj, 1), :]
             c2 = c0 * pad_ref[3, bi, pl.ds(bj, 1), :]
             window.append((2.0 * bx, 2.0 * by, c0, c1, c2))
@@ -58,50 +83,37 @@
         scale = jnp.exp2(-x * x - y * y)
         for k in range(3):
             sums_ref[k, pl.ds(t, 1), :] = jnp.sum(acc[k].T, axis=0, keepdims=True) * scale
-        return carry
-
-    lax.fori_loop(0, rows * cols, tile, 0, unroll=4)
+        return running
+
+    lax.fori_loop(0, rows * cols, tile, jnp.zeros((128, 128), F32), unroll=4)
 
 
 def pack(dest_ref, vals_ref, rank_ref, send_ref, left_ref, slots_ref, acc_ref):
     groups = dest_ref.shape[0] // 8
     d_iota = iota((128, 128), 0)
-    before = jnp.concatenate(
-        [
-            (iota((128, 128), 0) < iota((128, 128), 1)).astype(F32),
-            jnp.ones((128, 128), F32),
-        ],
-        1,
-    ).astype(BF16)
     p_iota = iota((192, 128), 0).astype(F32)
     acc_ref[...] = jnp.zeros_like(acc_ref)
 
-    def group(g, running):
-        dest8 = dest_ref[pl.ds(g * 8, 8), :]
-        vals8 = [split2(vals_ref[k, pl.ds(g * 8, 8), :]) for k in range(4)]
-        ranks = []
+    def group(g, carry):
+        at = pl.ds(pl.multiple_of(g * 8, 8), 8)
+        dest8 = dest_ref[at, :]
+        rank8 = rank_ref[at, :]
+        vals8 = [split2(vals_ref[k, at, :]) for k in range(4)]
         for r in range(8):
             hit = d_iota == jnp.broadcast_to(dest8[r : r + 1], (128, 128))
-            counts = dot(jnp.where(hit, 1.0, 0.0).astype(BF16), before, NN)
-            rank = jnp.sum(
-                jnp.where(hit, counts[:, :128] + running, 0.0), axis=0, keepdims=True
-            )
-            running = running + counts[:, 128:]
-            ranks.append(rank)
             lanes = slice(r * 128, r * 128 + 128)
             slots_ref[:, lanes] = jnp.where(
-                p_iota == jnp.broadcast_to(rank, (192, 128)), 1.0, 0.0
+                p_iota == jnp.broadcast_to(rank8[r : r + 1], (192, 128)), 1.0, 0.0
             ).astype(BF16)
             for part in range(2):
                 for k in range(4):
                     v = jnp.broadcast_to(vals8[k][part][r : r + 1], (128, 128))
-                    at = (part * 4 + k) * 128
-                    left_ref[at : at + 128, lanes] = jnp.where(hit, v, 0.0).astype(BF16)
-        rank_ref[pl.ds(g * 8, 8), :] = jnp.concatenate(ranks, 0)
+                    base = (part * 4 + k) * 128
+                    left_ref[base : base + 128, lanes] = jnp.where(hit, v, 0.0).astype(BF16)
         acc_ref[:, 0:192] += dot(left_ref[...], slots_ref[...], NT)
-        return running
-
-    lax.fori_loop(0, groups, group, jnp.zeros((128, 128), F32))
+        return carry
+
+    lax.fori_loop(0, groups, group, 0)
     tails = []
     for k in range(4):
         send_ref[pl.ds(k, 128, stride=8), :] = acc_ref[k * 128 : k * 128 + 128, 0:128] + acc_ref[
@@ -139,13 +151,6 @@
 def at_step(step):
     (a, c), (na, nc) = my_place(), sizes()
     return lax.rem(a + step[0] + na, na), lax.rem(c + step[1] + nc, nc)
-
-
-def greet_around():
-    barrier = pltpu.get_barrier_semaphore()
-    for step in AROUND:
-        pl.semaphore_signal(barrier, inc=1, device_id=at_step(step), device_id_type=MESH)
-    pl.semaphore_wait(barrier, len(AROUND))
 
 
 def rim_copies(out_refs, in_refs, send_sem, recv_sem):
@@ -196,13 +201,15 @@
 
 
 def rims_kernel(
-    off_ref, vel_ref, mass_ref, surface_ref, depth_ref,
-    pad_ref, up_ref, down_ref, left_ref, right_ref, c0_ref, c1_ref, c2_ref, c3_ref,
+    off_ref, vel_ref, mass_ref, pad_ref,
     o0, o1, o2, o3, o4, o5, o6, o7, i0, i1, i2, i3, i4, i5, i6, i7, send_sem, recv_sem,
 ):
     outs = [o0, o1, o2, o3, o4, o5, o6, o7]
     ins = [i0, i1, i2, i3, i4, i5, i6, i7]
     rows, cols = mass_ref.shape[0], mass_ref.shape[1]
+    barrier = pltpu.get_barrier_semaphore()
+    for step in AROUND:
+        pl.semaphore_signal(barrier, inc=1, device_id=at_step(step), device_id_type=MESH)
     particle = [
         (off_ref, 0), (off_ref, 1), (vel_ref, 0), (vel_ref, 1), (mass_ref, None),
     ]
@@ -221,17 +228,12 @@
             outs[4 + side][f : f + 1, :] = tiles(f, 0, j)
             outs[6 + side][f : f + 1, :] = tiles(f, rows - 1, j)
     for side in range(2):
-        outs[2 + side][5 * rows :SIDE_PARTICLES, :] = jnp.zeros((SIDE_PARTICLES - 5 * rows, 128), F32)
+        outs[2 + side][5 * rows : SIDE_PARTICLES, :] = jnp.zeros(
+            (SIDE_PARTICLES - 5 * rows, 128), F32
+        )
         outs[4 + side][5:8, :] = jnp.zeros((3, 128), F32)
         outs[6 + side][5:8, :] = jnp.zeros((3, 128), F32)
-    fields = [
-        lambda r, c: surface_ref[0, r, c],
-        lambda r, c: surface_ref[1, r, c],
-        lambda r, c: surface_ref[2, r, c],
-        lambda r, c: depth_ref[r, c],
-    ]
-    write_rims(outs, [5 * cols, 5 * cols, SIDE_PARTICLES, SIDE_PARTICLES, 8], fields)
-    greet_around()
+    pl.semaphore_wait(barrier, len(AROUND))
     copies = rim_copies(outs, ins, send_sem, recv_sem)
     for copy in copies:
         copy.start()
@@ -252,36 +254,31 @@
 
     for f in range(5):
         pad_ref[f, 0, 1 : cols + 1, :] = kept(f, ins[0][f * cols : (f + 1) * cols, :], inside[0])
-        pad_ref[f, rows + 1, 1 : cols + 1, :] = kept(f, ins[1][f * cols : (f + 1) * cols, :], inside[1])
+        pad_ref[f, rows + 1, 1 : cols + 1, :] = kept(
+            f, ins[1][f * cols : (f + 1) * cols, :], inside[1]
+        )
         for side, j in ((0, 0), (1, cols + 1)):
             for i in range(rows):
                 pad_ref[f, i + 1, j : j + 1, :] = kept(
                     f, ins[2 + side][f * rows + i : f * rows + i + 1, :], inside[2 + side]
                 )
-            pad_ref[f, 0, j : j + 1, :] = kept(f, ins[4 + side][f : f + 1, :], inside[0], inside[2 + side])
-            pad_ref[f, rows + 1, j : j + 1, :] = kept(f, ins[6 + side][f : f + 1, :], inside[1], inside[2 + side])
-    up_ref[...] = ins[0][5 * cols : 5 * cols + 128, :]
-    down_ref[...] = ins[1][5 * cols : 5 * cols + 128, :]
-    left_ref[...] = ins[2][SIDE_PARTICLES : SIDE_PARTICLES + 128, :]
-    right_ref[...] = ins[3][SIDE_PARTICLES : SIDE_PARTICLES + 128, :]
-    for n, ref in enumerate((c0_ref, c1_ref, c2_ref, c3_ref)):
-        ref[...] = ins[4 + n][8:16, :]
-
-
-def rims_call(offsets, velocity, mass, surface, depth):
+            pad_ref[f, 0, j : j + 1, :] = kept(
+                f, ins[4 + side][f : f + 1, :], inside[0], inside[2 + side]
+            )
+            pad_ref[f, rows + 1, j : j + 1, :] = kept(
+                f, ins[6 + side][f : f + 1, :], inside[1], inside[2 + side]
+            )
+
+
+def rims_call(offsets, velocity, mass):
     rows, cols = mass.shape[0], mass.shape[1]
-    tall, wide, corner = 5 * cols + 128, SIDE_PARTICLES + 128, 16
-    heights = [tall, tall, wide, wide, corner, corner, corner, corner]
+    heights = [5 * cols] * 2 + [SIDE_PARTICLES] * 2 + [8] * 4
     buffers = [pltpu.VMEM((h, 128), F32) for h in heights]
     return pl.pallas_call(
         rims_kernel,
-        out_shape=(
-            jax.ShapeDtypeStruct((5, rows + 2, cols + 2, 128), F32),
-            *[jax.ShapeDtypeStruct((128, 128), F32)] * 4,
-            *[jax.ShapeDtypeStruct((8, 128), F32)] * 4,
-        ),
-        in_specs=[vmem()] * 5,
-        out_specs=tuple([vmem()] * 9),
+        out_shape=jax.ShapeDtypeStruct((5, rows + 2, cols + 2, 128), F32),
+        in_specs=[vmem()] * 3,
+        out_specs=vmem(),
         scratch_shapes=[
             *buffers,
             *buffers,
@@ -292,10 +289,18 @@
             vmem_limit_bytes=VMEM_LIMIT, collective_id=0, has_side_effects=True
         ),
         name="rims",
-    )(offsets, velocity, mass, surface, depth)
-
-
-def unpack(back_ref, dest_ref, rank_ref, out_ref, table_ref):
+    )(offsets, velocity, mass)
+
+
+def finish_kernel(
+    back_ref, dest_ref, rank_ref, state_in, dens_in, out_ref, state_ref, dens_ref, table_ref, sems
+):
+    copies = [
+        pltpu.make_async_copy(state_in, state_ref, sems.at[0]),
+        pltpu.make_async_copy(dens_in, dens_ref, sems.at[1]),
+    ]
+    for copy in copies:
+        copy.start()
     tail = back_ref[pl.ds(3, 128, stride=8), :]
     tails = [tail, pltpu.roll(tail, 64, 1), back_ref[pl.ds(4, 128, stride=8), :]]
     for k in range(3):
@@ -334,12 +339,31 @@
             out_ref[k, at, :] = jnp.concatenate(found[k], 0)
         return carry
 
-    lax.fori_loop(0, dest_ref.shape[0] // 8, step, 0)
+    lax.fori_loop(0, dest_ref.shape[0] // 8, step, 0, unroll=2)
+    for copy in copies:
+        copy.wait()
+
+
+def finish_call(back, dest, rank, state, density):
+    anywhere = pl.BlockSpec(memory_space=pl.ANY)
+    return pl.pallas_call(
+        finish_kernel,
+        out_shape=(
+            jax.ShapeDtypeStruct((3, 64, 128), F32),
+            jax.ShapeDtypeStruct(state.shape, F32),
+            jax.ShapeDtypeStruct(density.shape, F32),
+        ),
+        in_specs=[vmem(), vmem(), vmem(), anywhere, anywhere],
+        out_specs=(vmem(), anywhere, anywhere),
+        scratch_shapes=[pltpu.VMEM((384, 384), BF16), pltpu.SemaphoreType.DMA((2,))],
+        compiler_params=pltpu.CompilerParams(vmem_limit_bytes=VMEM_LIMIT),
+        name="finish",
+    )(back, dest, rank, state, density)
 
 
 GROUPS = 4
 PER_GROUP = 32
-STEP = 8
+STEP = 16
 
 
 def row_and_column(cell):
@@ -369,25 +393,40 @@
     def step(g, carry):
         at = pl.ds(pl.multiple_of(g * STEP, STEP), STEP)
         row8, col8 = row_and_column(slots_ref[0, at, :])
-        vals8 = [split2(slots_ref[1 + k, at, :]) for k in range(3)]
+        vals8 = [split8(slots_ref[1 + k, at, :] * 0.5) for k in range(3)]
         for r in range(STEP):
             lanes = slice(r * 128, r * 128 + 128)
             hit = r_iota == jnp.broadcast_to(row8[r : r + 1], (128, 128))
-            for part in range(2):
+            for part in range(3):
                 for k in range(3):
                     v = jnp.broadcast_to(vals8[k][part][r : r + 1], (128, 128))
                     base = (part * 3 + k) * 128
-                    left_ref[base : base + 128, lanes] = jnp.where(hit, v, 0.0).astype(BF16)
+                    left_ref[base : base + 128, lanes] = jnp.where(hit, v, 0.0).astype(F8)
             right_ref[:, lanes] = jnp.where(
                 c_iota == jnp.broadcast_to(col8[r : r + 1], (512, 128)), 1.0, 0.0
-            ).astype(BF16)
+            ).astype(F8)
         acc_ref[...] += dot(left_ref[...], right_ref[...], NT)
         return carry
 
     lax.fori_loop(0, 48 // STEP, step, 0)
 
 
-def lookup_group(group, cells_ref, table_ref, found_ref, back_ref):
+def deposit_sum(acc_ref, k):
+    t0, t1, t2 = [
+        acc_ref[(part * 3 + k) * 128 : (part * 3 + k) * 128 + 128, :] for part in range(3)
+    ]
+    return 2.0 * (t0 + (1.0 / 16.0) * t1 + (1.0 / 256.0) * t2)
+
+
+def lookup_table(state, k, table_ref):
+    most = jnp.max(jnp.max(jnp.abs(state), axis=0, keepdims=True), axis=1, keepdims=True)
+    most = jnp.maximum(most, 1e-30)
+    for part, term in enumerate(split8(state * (256.0 / most))):
+        table_ref[k * 128 : k * 128 + 128, part * 512 : part * 512 + 512] = term.astype(F8)
+    return most * (1.0 / 256.0)
+
+
+def lookup_group(group, cells_ref, table_ref, undo, found_ref, back_ref):
     r_iota = iota((128, 128), 0).astype(F32)
     c_iota = iota((512, 128), 0).astype(F32)
 
@@ -396,16 +435,13 @@
         row8, col8 = row_and_column(cells_ref[at, :])
         found = [[], [], []]
         for pair in range(4):
-            right = jnp.concatenate(
-                [
-                    jnp.where(
-                        c_iota == jnp.broadcast_to(col8[r : r + 1], (512, 128)), 1.0, 0.0
-                    ).astype(BF16)
-                    for r in (2 * pair, 2 * pair + 1)
-                ],
-                1,
-            )
-            got = dot(table_ref[...], jnp.concatenate([right, right], 0), NN)
+            rights = [[], [], []]
+            for r in (2 * pair, 2 * pair + 1):
+                column = c_iota == jnp.broadcast_to(col8[r : r + 1], (512, 128))
+                for part, share in enumerate((1.0, 1.0 / 16.0, 1.0 / 256.0)):
+                    rights[part].append(jnp.where(column, share, 0.0).astype(F8))
+            right = jnp.concatenate([jnp.concatenate(halves, 1) for halves in rights], 0)
+            got = dot(table_ref[...], right, NN)
             for k in range(3):
                 for h in range(2):
                     r = 2 * pair + h
@@ -413,7 +449,9 @@
                     part = got[k * 128 : k * 128 + 128, h * 128 : h * 128 + 128]
                     found[k].append(jnp.sum(jnp.where(hit, part, 0.0), axis=0, keepdims=True))
         for k in range(3):
-            found_ref[k, pl.ds(pl.multiple_of(g * 8, 8), 8), :] = jnp.concatenate(found[k], 0)
+            found_ref[k, pl.ds(pl.multiple_of(g * 8, 8), 8), :] = (
+                jnp.concatenate(found[k], 0) * undo[k]
+            )
         return carry
 
     lax.fori_loop(0, 6, step, 0)
@@ -508,15 +546,16 @@
 
 
 def main_kernel(
-    pad_ref, present_ref, dest_ref, cell_ref, surface_ref, depth_ref,
-    up_ref, down_ref, left_in, right_in, c0_ref, c1_ref, c2_ref, c3_ref,
-    dens_ref, state_ref, feed_ref,
-    sums_ref, vals_ref, pleft_ref, pslots_ref, pacc_ref, rank_ref, send_ref, got_ref,
+    pad_ref, near_ref, dest_ref, cell_ref, surface_ref, depth_ref,
+    dens_ref, rank_ref, state_ref, back_got,
+    sums_ref, vals_ref, pleft_ref, pslots_ref, pacc_ref, send_ref, got_ref,
     slots_ref, cells_ref, left_ref, right_ref, acc_ref,
     even, odd, deep, wide_source,
-    table_ref, found_ref, back_ref, back_got, utable_ref,
+    table_ref, found_ref, back_ref,
     o0, o1, o2, o3, o4, o5, o6, o7, i0, i1, i2, i3, i4, i5, i6, i7,
-    rim_send, rim_recv, out_sem, in_sem, back_out_sem, back_in_sem,
+    q0, q1, q2, q3, q4, q5, q6, q7, g0, g1, g2, g3, g4, g5, g6, g7,
+    rim_send, rim_recv, first_send, first_recv,
+    out_sem, in_sem, back_out_sem, back_in_sem, state_sem,
 ):
     (a, c), (na, nc) = my_place(), sizes()
     count = na * nc
@@ -538,7 +577,7 @@
 
     lax.fori_loop(1, count, greet, 0)
 
-    window_sums(pad_ref, present_ref, sums_ref)
+    window_sums(pad_ref, near_ref, dest_ref, sums_ref, rank_ref)
     rows, cols = pad_ref.shape[1] - 2, pad_ref.shape[2] - 2
     for i in range(rows):
         at = slice(i * cols, (i + 1) * cols)
@@ -573,27 +612,38 @@
         send_out(group)
     got_ref[0:8, :] = send_ref[block(me), :]
 
-    rims = [up_ref, down_ref, left_in, right_in, c0_ref, c1_ref, c2_ref, c3_ref]
+    first_outs = [q0, q1, q2, q3, q4, q5, q6, q7]
+    first_ins = [g0, g1, g2, g3, g4, g5, g6, g7]
+    write_rims(first_outs, [0, 0, 0, 0, 0], [
+        lambda r, c: surface_ref[0, r, c],
+        lambda r, c: surface_ref[1, r, c],
+        lambda r, c: surface_ref[2, r, c],
+        lambda r, c: depth_ref[r, c],
+    ])
+    copies = rim_copies(first_outs, first_ins, first_send, first_recv)
+    for copy in copies:
+        copy.start()
     for f in range(3):
         even[f, 0:128, 0:512] = surface_ref[f]
-        place_rims(even, f, f, rims, [0, 0, 0])
     deep[0, 0:128, 0:512] = depth_ref[...]
-    place_rims(deep, 0, 3, rims, [0, 0, 0])
+    acc_ref[...] = jnp.zeros_like(acc_ref)
+    for copy in copies:
+        copy.wait()
+    for f in range(3):
+        place_rims(even, f, f, first_ins, [0, 0, 0])
+    place_rims(deep, 0, 3, first_ins, [0, 0, 0])
     for b in range(TALL // 8):
         at = slice(b * 8, b * 8 + 8)
         for f in range(3):
             even[f, at, :] = jnp.where(inside_grid(b), even[f, at, :], 0.0)
 
-    acc_ref[...] = jnp.zeros_like(acc_ref)
     for group in range(GROUPS):
         landed = got_ref.at[max(8, group * PER_GROUP * 8) : (group + 1) * PER_GROUP * 8, :]
         pltpu.make_async_copy(landed, landed, in_sem.at[group]).wait()
         unfold(got_ref, slots_ref, group)
         deposit_group(group, slots_ref, cells_ref, left_ref, right_ref, acc_ref)
     for k in range(3):
-        wide_source[k, 0:128, 0:512] = (
-            acc_ref[k * 128 : k * 128 + 128, :] + acc_ref[384 + k * 128 : 512 + k * 128, :]
-        )
+        wide_source[k, 0:128, 0:512] = deposit_sum(acc_ref, k)
 
     outs = [o0, o1, o2, o3, o4, o5, o6, o7]
     ins = [i0, i1, i2, i3, i4, i5, i6, i7]
@@ -616,15 +666,12 @@
         return carry
 
     lax.fori_loop(0, SUBSTEPS // 2, two_steps, 0)
-    for k in range(3):
-        value = even[k, 0:128, 0:512]
-        state_ref[k] = value
-        hi, lo = split2(value)
-        table_ref[k * 128 : k * 128 + 128, 0:512] = hi.astype(BF16)
-        table_ref[k * 128 : k * 128 + 128, 512:1024] = lo.astype(BF16)
+    keep = pltpu.make_async_copy(even.at[:, 0:128, 0:512], state_ref, state_sem)
+    keep.start()
+    undo = [lookup_table(even[k, 0:128, 0:512], k, table_ref) for k in range(3)]
 
     for group in range(GROUPS):
-        lookup_group(group, cells_ref, table_ref, found_ref, back_ref)
+        lookup_group(group, cells_ref, table_ref, undo, found_ref, back_ref)
 
         def start(step, carry):
             pltpu.make_async_remote_copy(
@@ -646,51 +693,56 @@
         (back_ref, back_out_sem),
     ):
         pltpu.make_async_copy(ref.at[0:others, :], ref.at[0:others, :], sem).wait()
-    unpack(back_got, dest_ref, rank_ref, feed_ref, utable_ref)
-
-
-def main_call(pad, present, dest, cell, surface, depth, rims):
-    heights = [96, 96, 128, 128, 8, 8, 8, 8]
-    buffers = [pltpu.VMEM((h, 128), F32) for h in heights]
+    keep.wait()
+
+
+def main_call(pad, near, dest, cell, surface, depth):
+    def buffers(heights):
+        return [pltpu.VMEM((h, 128), F32) for h in heights + [8, 8, 8, 8]]
+
     dma = pltpu.SemaphoreType.DMA
+    anywhere = pl.BlockSpec(memory_space=pl.ANY)
     return pl.pallas_call(
         main_kernel,
         out_shape=(
             jax.ShapeDtypeStruct((64, 128), F32),
+            jax.ShapeDtypeStruct((64, 128), F32),
             jax.ShapeDtypeStruct((3, 128, 512), F32),
-            jax.ShapeDtypeStruct((3, 64, 128), F32),
+            jax.ShapeDtypeStruct((1024, 128), F32),
         ),
-        in_specs=[vmem(), pl.BlockSpec(memory_space=pltpu.SMEM)] + [vmem()] * 12,
-        out_specs=(vmem(), vmem(), vmem()),
+        in_specs=[vmem(), pl.BlockSpec(memory_space=pltpu.SMEM)] + [vmem()] * 4,
+        out_specs=(vmem(), vmem(), anywhere, vmem()),
         scratch_shapes=[
             pltpu.VMEM((3, 64, 128), F32),
             pltpu.VMEM((4, 64, 128), F32),
             pltpu.VMEM((1024, 1024), BF16),
             pltpu.VMEM((192, 1024), BF16),
             pltpu.VMEM((1024, 256), F32),
-            pltpu.VMEM((64, 128), F32),
             pltpu.VMEM((1024, 128), F32),
             pltpu.VMEM((1024, 128), F32),
             pltpu.VMEM((4, 48, 128), F32),
             pltpu.VMEM((192, 128), F32),
-            pltpu.VMEM((768, STEP * 128), BF16),
-            pltpu.VMEM((512, STEP * 128), BF16),
-            pltpu.VMEM((768, 512), F32),
+            pltpu.VMEM((1152, STEP * 128), F8),
+            pltpu.VMEM((512, STEP * 128), F8),
+            pltpu.VMEM((1152, 512), F32),
             pltpu.VMEM((3, TALL, BROAD), F32),
             pltpu.VMEM((3, TALL, BROAD), F32),
             pltpu.VMEM((1, TALL, BROAD), F32),
             pltpu.VMEM((3, TALL, BROAD), F32),
-            pltpu.VMEM((384, 1024), BF16),
+            pltpu.VMEM((384, 1536), F8),
             pltpu.VMEM((3, 48, 128), F32),
             pltpu.VMEM((1024, 128), F32),
-            pltpu.VMEM((1024, 128), F32),
-            pltpu.VMEM((384, 384), BF16),
-            *buffers,
-            *buffers,
+            *buffers([96, 96, 128, 128]),
+            *buffers([96, 96, 128, 128]),
+            *buffers([128, 128, 128, 128]),
+            *buffers([128, 128, 128, 128]),
+            dma((8,)),
+            dma((8,)),
             dma((8,)),
             dma((8,)),
             dma,
             dma((GROUPS,)),
+            dma,
             dma,
             dma,
         ],
@@ -698,25 +750,18 @@
             vmem_limit_bytes=VMEM_LIMIT, collective_id=1, has_side_effects=True
         ),
         name="main",
-    )(pad, present, dest, cell, surface, depth, *rims)
+    )(pad, near, dest, cell, surface, depth)
 
 
 def shards(
     offsets, velocity, particle_mass, neighbours, owner_device, target_cell, surface, water_depth
 ):
-    padded, *rims = rims_call(offsets, velocity, particle_mass, surface, water_depth)
-    present = jnp.any(
-        neighbours[..., :, None] == jnp.arange(9, dtype=jnp.int32), axis=-2
-    ).astype(F32)
-    density, water_state, feedback = main_call(
-        padded,
-        present.reshape(-1),
-        owner_device.reshape(64, 128),
-        target_cell.reshape(64, 128),
-        surface,
-        water_depth,
-        rims,
+    padded = rims_call(offsets, velocity, particle_mass)
+    dest = owner_device.reshape(64, 128)
+    density, rank, water_state, back = main_call(
+        padded, jnp.transpose(neighbours, (2, 0, 1)), dest, target_cell.reshape(64, 128), surface, water_depth
     )
+    feedback, water_state, density = finish_call(back, dest, rank, water_state, density)
     return (
         water_state,
         density.reshape(particle_mass.shape),

time: 137 us -> 146 us (1.066)
  Pallas kernels: 131 us -> 145 us
  local copies, waits for them, and re-layouts: 4.19 us -> 0 us
    pallas_call x1 -> x2, Pallas kernels: 15.4 us -> 41.6 us  [the longest x1 27.6 us: finish_call(): pl.pallas_call(finish_kernel, out_shape=(jax.ShapeDtypeStruct((3, 64, 128...]
    pallas_call x1, Pallas kernels: 115 us -> 103 us  [main_call(): pl.pallas_call(main_kernel, out_shape=(jax.ShapeDtypeStruct((64, 128), F3...]
    unnamed x7 -> x0, local copies, waits for them, and re-layouts: 3.36 us -> none
where the time goes in v4:
time: 146 us
  Pallas kernels  145 us (99%)
    pallas_call x1, Pallas kernels, main_call(): pl.pallas_call(main_kernel, out_shape=(jax.ShapeDtypeStruct((64, 128), F3...  103 us
    pallas_call x1, Pallas kernels, finish_call(): pl.pallas_call(finish_kernel, out_shape=(jax.ShapeDtypeStruct((3, 64, 128...  27.6 us
    pallas_call x1, Pallas kernels, rims_call(): pl.pallas_call(rims_kernel, out_shape=jax.ShapeDtypeStruct((5, rows + 2,...  14 us

profile of v4, /device:TPU:1, one launch (start us, length us, event | category | flops | bytes accessed | tf_op | source)
XLA Modules:
  0.0 145.6 jit_solution(11695857863741823904)
XLA Ops:
  0.6 14.0 %rims.1.pad_ref = f32[5,6,18,128]{3,2,1,0:T(8,128)} custom-call(f32[2,4,16,128]{3,2,1,0:T(8,128)} %off_ref.1, f32[2,4,16,128]{3,2,1,0:T(8,128)} %vel_ref.1, f32[4,16,128]{2,1,0:T(8,128)} %mass_ref.1), custom_call_target="tpu_custom_call" | custom-call | tf_op jit(solution)/shard_map/rims/pallas_call | solution.py:277
  14.6 103.2 %main.1 = (f32[64,128]{1,0:T(8,128)}, f32[64,128]{1,0:T(8,128)}, f32[3,128,512]{2,1,0:T(8,128)}, f32[1024,128]{1,0:T(8,128)}) custom-call(f32[5,6,18,128]{3,2,1,0:T(8,128)} %rims.1.pad_ref, s32[9,4,16]{2,1,0:T(4,128)} %bitcast.8, s32[64,128]{1,0:T(8,128)} %bitcast.5, s32[64,128]{1,0:T(8,128)} %bitcast.7, f32[3,128,512]{2,1,0:T(8,128)} %surface_ref.1, ...), custom_call_target="tpu_custom_call" | custom-call | tf_op jit(solution)/shard_map/main/pallas_call | solution.py:705
  117.8 27.6 %finish.1 = (f32[3,64,128]{2,1,0:T(8,128)}, f32[3,128,512]{2,1,0:T(8,128)}, f32[64,128]{1,0:T(8,128)}) custom-call(f32[1024,128]{1,0:T(8,128)} %get-tuple-element.10.back_ref, s32[64,128]{1,0:T(8,128)} %bitcast.6, f32[64,128]{1,0:T(8,128)} %get-tuple-element.11.rank_ref, f32[3,128,512]{2,1,0:T(8,128)} %get-tuple-element.12.state_in, ...), custom_call_target="tpu_custom_call" | custom-call | tf_op jit(solution)/shard_map/finish/pallas_call | solution.py:349

commit v5 on v4

--- a/solution.py
+++ b/solution.py
@@ -40,7 +40,7 @@
 
 
 def window_sums(pad_ref, near_ref, dest_ref, sums_ref, rank_ref):
-    rows, cols = pad_ref.shape[1] - 2, pad_ref.shape[2] - 2
+    cols = pad_ref.shape[2] - 2
     d_iota = iota((128, 128), 0)
     before = jnp.concatenate(
         [
@@ -50,15 +50,13 @@
         1,
     ).astype(BF16)
 
-    def tile(t, running):
-        hit = d_iota == jnp.broadcast_to(dest_ref[pl.ds(t, 1), :], (128, 128))
+    def tile(i, j, row, running):
+        hit = d_iota == jnp.broadcast_to(dest_ref[pl.ds(row, 1), :], (128, 128))
         counts = dot(jnp.where(hit, 1.0, 0.0).astype(BF16), before, NN)
-        rank_ref[pl.ds(t, 1), :] = jnp.sum(
+        rank_ref[pl.ds(row, 1), :] = jnp.sum(
             jnp.where(hit, counts[:, :128] + running, 0.0), axis=0, keepdims=True
         )
         running = running + counts[:, 128:]
-        i = t // cols
-        j = t - i * cols
         x = pad_ref[0, i + 1, pl.ds(j + 1, 1), :] * KAPPA
         y = pad_ref[1, i + 1, pl.ds(j + 1, 1), :] * KAPPA
         x_col = jnp.broadcast_to(x, (128, 128)).T
@@ -82,10 +80,10 @@
             acc = [total + weights * c for total, c in zip(acc, carried)]
         scale = jnp.exp2(-x * x - y * y)
         for k in range(3):
-            sums_ref[k, pl.ds(t, 1), :] = jnp.sum(acc[k].T, axis=0, keepdims=True) * scale
+            sums_ref[k, pl.ds(i * cols + j, 1), :] = jnp.sum(acc[k].T, axis=0, keepdims=True) * scale
         return running
 
-    lax.fori_loop(0, rows * cols, tile, jnp.zeros((128, 128), F32), unroll=4)
+    return tile
 
 
 def pack(dest_ref, vals_ref, rank_ref, send_ref, left_ref, slots_ref, acc_ref):
@@ -200,20 +198,7 @@
         out_refs[6 + right][base[4] : base[4] + 8, :] = strip[120:128]
 
 
-def rims_kernel(
-    off_ref, vel_ref, mass_ref, pad_ref,
-    o0, o1, o2, o3, o4, o5, o6, o7, i0, i1, i2, i3, i4, i5, i6, i7, send_sem, recv_sem,
-):
-    outs = [o0, o1, o2, o3, o4, o5, o6, o7]
-    ins = [i0, i1, i2, i3, i4, i5, i6, i7]
-    rows, cols = mass_ref.shape[0], mass_ref.shape[1]
-    barrier = pltpu.get_barrier_semaphore()
-    for step in AROUND:
-        pl.semaphore_signal(barrier, inc=1, device_id=at_step(step), device_id_type=MESH)
-    particle = [
-        (off_ref, 0), (off_ref, 1), (vel_ref, 0), (vel_ref, 1), (mass_ref, None),
-    ]
-
+def stage_particles(particle, rows, cols, outs, pad_ref):
     def tiles(f, i, j):
         ref, part = particle[f]
         return ref[i, j, :] if part is None else ref[part, i, j, :]
@@ -233,15 +218,12 @@
         )
         outs[4 + side][5:8, :] = jnp.zeros((3, 128), F32)
         outs[6 + side][5:8, :] = jnp.zeros((3, 128), F32)
-    pl.semaphore_wait(barrier, len(AROUND))
-    copies = rim_copies(outs, ins, send_sem, recv_sem)
-    for copy in copies:
-        copy.start()
     for f in range(5):
         for i in range(rows):
             pad_ref[f, i + 1, 1 : cols + 1, :] = tiles(f, i, everything)
-    for copy in copies:
-        copy.wait()
+
+
+def place_particles(ins, rows, cols, pad_ref):
     (a, c), (na, nc) = my_place(), sizes()
     inside = [a > 0, a < na - 1, c > 0, c < nc - 1]
 
@@ -270,37 +252,11 @@
             )
 
 
-def rims_call(offsets, velocity, mass):
-    rows, cols = mass.shape[0], mass.shape[1]
-    heights = [5 * cols] * 2 + [SIDE_PARTICLES] * 2 + [8] * 4
-    buffers = [pltpu.VMEM((h, 128), F32) for h in heights]
-    return pl.pallas_call(
-        rims_kernel,
-        out_shape=jax.ShapeDtypeStruct((5, rows + 2, cols + 2, 128), F32),
-        in_specs=[vmem()] * 3,
-        out_specs=vmem(),
-        scratch_shapes=[
-            *buffers,
-            *buffers,
-            pltpu.SemaphoreType.DMA((8,)),
-            pltpu.SemaphoreType.DMA((8,)),
-        ],
-        compiler_params=pltpu.CompilerParams(
-            vmem_limit_bytes=VMEM_LIMIT, collective_id=0, has_side_effects=True
-        ),
-        name="rims",
-    )(offsets, velocity, mass)
-
-
 def finish_kernel(
-    back_ref, dest_ref, rank_ref, state_in, dens_in, out_ref, state_ref, dens_ref, table_ref, sems
+    back_ref, dest_ref, rank_ref, state_in, dens_in, out_ref, state_ref, dens_ref, table_ref
 ):
-    copies = [
-        pltpu.make_async_copy(state_in, state_ref, sems.at[0]),
-        pltpu.make_async_copy(dens_in, dens_ref, sems.at[1]),
-    ]
-    for copy in copies:
-        copy.start()
+    state_ref[...] = state_in[...]
+    dens_ref[...] = dens_in[...]
     tail = back_ref[pl.ds(3, 128, stride=8), :]
     tails = [tail, pltpu.roll(tail, 64, 1), back_ref[pl.ds(4, 128, stride=8), :]]
     for k in range(3):
@@ -340,12 +296,9 @@
         return carry
 
     lax.fori_loop(0, dest_ref.shape[0] // 8, step, 0, unroll=2)
-    for copy in copies:
-        copy.wait()
 
 
 def finish_call(back, dest, rank, state, density):
-    anywhere = pl.BlockSpec(memory_space=pl.ANY)
     return pl.pallas_call(
         finish_kernel,
         out_shape=(
@@ -353,9 +306,9 @@
             jax.ShapeDtypeStruct(state.shape, F32),
             jax.ShapeDtypeStruct(density.shape, F32),
         ),
-        in_specs=[vmem(), vmem(), vmem(), anywhere, anywhere],
-        out_specs=(vmem(), anywhere, anywhere),
-        scratch_shapes=[pltpu.VMEM((384, 384), BF16), pltpu.SemaphoreType.DMA((2,))],
+        in_specs=[vmem()] * 5,
+        out_specs=(vmem(), vmem(), vmem()),
+        scratch_shapes=[pltpu.VMEM((384, 384), BF16)],
         compiler_params=pltpu.CompilerParams(vmem_limit_bytes=VMEM_LIMIT),
         name="finish",
     )(back, dest, rank, state, density)
@@ -418,15 +371,16 @@
     return 2.0 * (t0 + (1.0 / 16.0) * t1 + (1.0 / 256.0) * t2)
 
 
-def lookup_table(state, k, table_ref):
+def lookup_table(state, k, high_ref, low_ref):
     most = jnp.max(jnp.max(jnp.abs(state), axis=0, keepdims=True), axis=1, keepdims=True)
     most = jnp.maximum(most, 1e-30)
-    for part, term in enumerate(split8(state * (256.0 / most))):
-        table_ref[k * 128 : k * 128 + 128, part * 512 : part * 512 + 512] = term.astype(F8)
-    return most * (1.0 / 256.0)
-
-
-def lookup_group(group, cells_ref, table_ref, undo, found_ref, back_ref):
+    hi, lo = split2(state * (1024.0 / most))
+    high_ref[k * 128 : k * 128 + 128, :] = hi.astype(BF16)
+    low_ref[k * 128 : k * 128 + 128, :] = (lo * 64.0).astype(F8)
+    return most * (1.0 / 1024.0)
+
+
+def lookup_group(group, cells_ref, high_ref, low_ref, undo, found_ref, back_ref):
     r_iota = iota((128, 128), 0).astype(F32)
     c_iota = iota((512, 128), 0).astype(F32)
 
@@ -435,13 +389,14 @@
         row8, col8 = row_and_column(cells_ref[at, :])
         found = [[], [], []]
         for pair in range(4):
-            rights = [[], [], []]
+            high, low = [], []
             for r in (2 * pair, 2 * pair + 1):
                 column = c_iota == jnp.broadcast_to(col8[r : r + 1], (512, 128))
-                for part, share in enumerate((1.0, 1.0 / 16.0, 1.0 / 256.0)):
-                    rights[part].append(jnp.where(column, share, 0.0).astype(F8))
-            right = jnp.concatenate([jnp.concatenate(halves, 1) for halves in rights], 0)
-            got = dot(table_ref[...], right, NN)
+                high.append(jnp.where(column, 1.0, 0.0).astype(BF16))
+                low.append(jnp.where(column, 1.0 / 64.0, 0.0).astype(F8))
+            got = dot(high_ref[...], jnp.concatenate(high, 1), NN) + dot(
+                low_ref[...], jnp.concatenate(low, 1), NN
+            )
             for k in range(3):
                 for h in range(2):
                     r = 2 * pair + h
@@ -546,67 +501,119 @@
 
 
 def main_kernel(
-    pad_ref, near_ref, dest_ref, cell_ref, surface_ref, depth_ref,
+    off_ref, vel_ref, mass_ref, near_ref, dest_ref, cell_ref, surface_ref, depth_ref,
     dens_ref, rank_ref, state_ref, back_got,
+    pad_ref,
     sums_ref, vals_ref, pleft_ref, pslots_ref, pacc_ref, send_ref, got_ref,
     slots_ref, cells_ref, left_ref, right_ref, acc_ref,
     even, odd, deep, wide_source,
-    table_ref, found_ref, back_ref,
+    high_ref, low_ref, found_ref, back_ref,
     o0, o1, o2, o3, o4, o5, o6, o7, i0, i1, i2, i3, i4, i5, i6, i7,
     q0, q1, q2, q3, q4, q5, q6, q7, g0, g1, g2, g3, g4, g5, g6, g7,
-    rim_send, rim_recv, first_send, first_recv,
+    r0, r1, r2, r3, r4, r5, r6, r7, t0, t1, t2, t3, t4, t5, t6, t7,
+    rim_send, rim_recv, first_send, first_recv, tile_send, tile_recv,
     out_sem, in_sem, back_out_sem, back_in_sem, state_sem,
 ):
     (a, c), (na, nc) = my_place(), sizes()
     count = na * nc
     me = a * nc + c
-
-    def device(n):
-        return (lax.div(n, nc), lax.rem(n, nc))
+    rows, cols = mass_ref.shape[0], mass_ref.shape[1]
+    ahead = [lax.rem(c + step, nc) for step in range(nc)]
+    behind = [lax.rem(c - step + nc, nc) for step in range(nc)]
 
     def block(n):
         return pl.ds(pl.multiple_of(n * 8, 8), 8)
 
+    def each_other(first, last, act):
+        if first == 0:
+            for across in range(1, nc):
+                act(0, across)
+
+        def along(step, carry):
+            for across in range(nc):
+                act(step, across)
+            return carry
+
+        lax.fori_loop(max(first, 1), last, along, 0)
+
     barrier = pltpu.get_barrier_semaphore()
 
-    def greet(step, carry):
+    def greet(along, across):
         pl.semaphore_signal(
-            barrier, inc=1, device_id=device(lax.rem(me + step, count)), device_id_type=MESH
+            barrier,
+            inc=1,
+            device_id=(lax.rem(a + along, na), ahead[across]),
+            device_id_type=MESH,
         )
-        return carry
-
-    lax.fori_loop(1, count, greet, 0)
-
-    window_sums(pad_ref, near_ref, dest_ref, sums_ref, rank_ref)
-    rows, cols = pad_ref.shape[1] - 2, pad_ref.shape[2] - 2
+
+    each_other(0, na, greet)
+
+    particle = [
+        (off_ref, 0), (off_ref, 1), (vel_ref, 0), (vel_ref, 1), (mass_ref, None),
+    ]
+    tile_outs = [r0, r1, r2, r3, r4, r5, r6, r7]
+    tile_ins = [t0, t1, t2, t3, t4, t5, t6, t7]
+    stage_particles(particle, rows, cols, tile_outs, pad_ref)
+    tile = window_sums(pad_ref, near_ref, dest_ref, sums_ref, rank_ref)
+    inner = cols - 2
+    half = rows // 2 - 1
+
+    def inner_tiles(base, row0, running):
+        def one(n, running):
+            return tile(row0 + n // inner, 1 + n % inner, base + n, running)
+
+        return lax.fori_loop(0, half * inner, one, running, unroll=2)
+
+    running = inner_tiles(0, 1, jnp.zeros((128, 128), F32))
+    pl.semaphore_wait(barrier, count - 1)
+    copies = rim_copies(tile_outs, tile_ins, tile_send, tile_recv)
+    for copy in copies:
+        copy.start()
+    running = inner_tiles(half * inner, 1 + half, running)
+    for copy in copies:
+        copy.wait()
+    place_particles(tile_ins, rows, cols, pad_ref)
+    done = 2 * half * inner
+
+    def end_rows(n, running):
+        i = (n // cols) * (rows - 1)
+        return tile(i, n % cols, done + n, running)
+
+    running = lax.fori_loop(0, 2 * cols, end_rows, running, unroll=4)
+    done = done + 2 * cols
+
+    def end_columns(n, running):
+        return tile(1 + n // 2, (n % 2) * (cols - 1), done + n, running)
+
+    lax.fori_loop(0, 2 * (rows - 2), end_columns, running, unroll=2)
+
     for i in range(rows):
         at = slice(i * cols, (i + 1) * cols)
         s0 = sums_ref[0, at, :]
         density = s0 / 128.0
         dens_ref[at, :] = density
-        volume = pad_ref[4, i + 1, 1 : cols + 1, :] / density
+        volume = mass_ref[i] / density
         vals_ref[0, at, :] = cell_ref[at, :].astype(F32)
         vals_ref[1, at, :] = volume
         vals_ref[2, at, :] = volume * (sums_ref[1, at, :] / s0)
         vals_ref[3, at, :] = volume * (sums_ref[2, at, :] / s0)
     pack(dest_ref, vals_ref, rank_ref, send_ref, pleft_ref, pslots_ref, pacc_ref)
 
-    pl.semaphore_wait(barrier, count - 1)
+    per_group = na // GROUPS
 
     def send_out(group):
-        def start(step, carry):
-            to = lax.rem(me + step, count)
+        def start(along, across):
+            to = (lax.rem(a + along, na), ahead[across])
             pltpu.make_async_remote_copy(
-                src_ref=send_ref.at[block(to), :],
-                dst_ref=got_ref.at[block(step), :],
+                src_ref=send_ref.at[block(to[0] * nc + to[1]), :],
+                dst_ref=got_ref.at[block(along * nc + across), :],
                 send_sem=out_sem,
                 recv_sem=in_sem.at[group],
-                device_id=device(to),
+                device_id=to,
                 device_id_type=MESH,
             ).start()
-            return carry
-
-        lax.fori_loop(max(1, group * PER_GROUP), (group + 1) * PER_GROUP, start, 0)
+
+        each_other(group * per_group, (group + 1) * per_group, start)
 
     for group in range(GROUPS):
         send_out(group)
@@ -668,23 +675,22 @@
     lax.fori_loop(0, SUBSTEPS // 2, two_steps, 0)
     keep = pltpu.make_async_copy(even.at[:, 0:128, 0:512], state_ref, state_sem)
     keep.start()
-    undo = [lookup_table(even[k, 0:128, 0:512], k, table_ref) for k in range(3)]
+    undo = [lookup_table(even[k, 0:128, 0:512], k, high_ref, low_ref) for k in range(3)]
 
     for group in range(GROUPS):
-        lookup_group(group, cells_ref, table_ref, undo, found_ref, back_ref)
-
-        def start(step, carry):
+        lookup_group(group, cells_ref, high_ref, low_ref, undo, found_ref, back_ref)
+
+        def start(along, across):
             pltpu.make_async_remote_copy(
-                src_ref=back_ref.at[block(step), :],
+                src_ref=back_ref.at[block(along * nc + across), :],
                 dst_ref=back_got.at[block(me), :],
                 send_sem=back_out_sem,
                 recv_sem=back_in_sem,
-                device_id=device(lax.rem(me - step + count, count)),
+                device_id=(lax.rem(a - along + na, na), behind[across]),
                 device_id_type=MESH,
             ).start()
-            return carry
-
-        lax.fori_loop(max(1, group * PER_GROUP), (group + 1) * PER_GROUP, start, 0)
+
+        each_other(group * per_group, (group + 1) * per_group, start)
     back_got[block(me), :] = back_ref[0:8, :]
     others = (count - 1) * 8
     for ref, sem in (
@@ -696,10 +702,11 @@
     keep.wait()
 
 
-def main_call(pad, near, dest, cell, surface, depth):
+def main_call(offsets, velocity, mass, near, dest, cell, surface, depth):
     def buffers(heights):
         return [pltpu.VMEM((h, 128), F32) for h in heights + [8, 8, 8, 8]]
 
+    rows, cols = mass.shape[0], mass.shape[1]
     dma = pltpu.SemaphoreType.DMA
     anywhere = pl.BlockSpec(memory_space=pl.ANY)
     return pl.pallas_call(
@@ -710,9 +717,10 @@
             jax.ShapeDtypeStruct((3, 128, 512), F32),
             jax.ShapeDtypeStruct((1024, 128), F32),
         ),
-        in_specs=[vmem(), pl.BlockSpec(memory_space=pltpu.SMEM)] + [vmem()] * 4,
+        in_specs=[vmem()] * 3 + [pl.BlockSpec(memory_space=pltpu.SMEM)] + [vmem()] * 4,
         out_specs=(vmem(), vmem(), anywhere, vmem()),
         scratch_shapes=[
+            pltpu.VMEM((5, rows + 2, cols + 2, 128), F32),
             pltpu.VMEM((3, 64, 128), F32),
             pltpu.VMEM((4, 64, 128), F32),
             pltpu.VMEM((1024, 1024), BF16),
@@ -729,13 +737,18 @@
             pltpu.VMEM((3, TALL, BROAD), F32),
             pltpu.VMEM((1, TALL, BROAD), F32),
             pltpu.VMEM((3, TALL, BROAD), F32),
-            pltpu.VMEM((384, 1536), F8),
+            pltpu.VMEM((384, 512), BF16),
+            pltpu.VMEM((384, 512), F8),
             pltpu.VMEM((3, 48, 128), F32),
             pltpu.VMEM((1024, 128), F32),
             *buffers([96, 96, 128, 128]),
             *buffers([96, 96, 128, 128]),
             *buffers([128, 128, 128, 128]),
             *buffers([128, 128, 128, 128]),
+            *buffers([5 * cols, 5 * cols, SIDE_PARTICLES, SIDE_PARTICLES]),
+            *buffers([5 * cols, 5 * cols, SIDE_PARTICLES, SIDE_PARTICLES]),
+            dma((8,)),
+            dma((8,)),
             dma((8,)),
             dma((8,)),
             dma((8,)),
@@ -750,16 +763,22 @@
             vmem_limit_bytes=VMEM_LIMIT, collective_id=1, has_side_effects=True
         ),
         name="main",
-    )(pad, near, dest, cell, surface, depth)
+    )(offsets, velocity, mass, near, dest, cell, surface, depth)
 
 
 def shards(
     offsets, velocity, particle_mass, neighbours, owner_device, target_cell, surface, water_depth
 ):
-    padded = rims_call(offsets, velocity, particle_mass)
     dest = owner_device.reshape(64, 128)
     density, rank, water_state, back = main_call(
-        padded, jnp.transpose(neighbours, (2, 0, 1)), dest, target_cell.reshape(64, 128), surface, water_depth
+        offsets,
+        velocity,
+        particle_mass,
+        jnp.transpose(neighbours, (2, 0, 1)),
+        dest,
+        target_cell.reshape(64, 128),
+        surface,
+        water_depth,
     )
     feedback, water_state, density = finish_call(back, dest, rank, water_state, density)
     return (

time: 146 us -> 112 us (0.77)
  Pallas kernels: 145 us -> 111 us
    pallas_call x1, Pallas kernels: 27.6 us -> 6.45 us  [finish_call(): pl.pallas_call(finish_kernel, out_shape=(jax.ShapeDtypeStruct((3, 64, 128...]
    pallas_call x1 -> x0, Pallas kernels: 14 us -> none  [rims_call(): pl.pallas_call(rims_kernel, out_shape=jax.ShapeDtypeStruct((5, rows + 2,...]
    pallas_call x1, Pallas kernels: 103 us -> 105 us  [main_call(): pl.pallas_call(main_kernel, out_shape=(jax.ShapeDtypeStruct((64, 128), F3...]
where the time goes in v5:
time: 112 us
  Pallas kernels  111 us (99%)
    pallas_call x1, Pallas kernels, main_call(): pl.pallas_call(main_kernel, out_shape=(jax.ShapeDtypeStruct((64, 128), F3...  105 us
    pallas_call x1, Pallas kernels, finish_call(): pl.pallas_call(finish_kernel, out_shape=(jax.ShapeDtypeStruct((3, 64, 128...  6.45 us

profile of v5, /device:TPU:1, one launch (start us, length us, event | category | flops | bytes accessed | tf_op | source)
XLA Modules:
  0.0 112.1 jit_solution(10741300647272746378)
XLA Ops:
  0.6 105.0 %main.1 = (f32[64,128]{1,0:T(8,128)}, f32[64,128]{1,0:T(8,128)}, f32[3,128,512]{2,1,0:T(8,128)}, f32[1024,128]{1,0:T(8,128)}) custom-call(f32[2,4,16,128]{3,2,1,0:T(8,128)} %off_ref.1, f32[2,4,16,128]{3,2,1,0:T(8,128)} %vel_ref.1, f32[4,16,128]{2,1,0:T(8,128)} %mass_ref.1, s32[9,4,16]{2,1,0:T(4,128)} %bitcast.8, s32[64,128]{1,0:T(8,128)} %bitcast.5, ...), custom_call_target="tpu_custom_call" | custom-call | tf_op jit(solution)/shard_map/main/pallas_call | solution.py:712
  105.6 6.4 %finish.1 = (f32[3,64,128]{2,1,0:T(8,128)}, f32[3,128,512]{2,1,0:T(8,128)}, f32[64,128]{1,0:T(8,128)}) custom-call(f32[1024,128]{1,0:T(8,128)} %get-tuple-element.10.back_ref, s32[64,128]{1,0:T(8,128)} %bitcast.6, f32[64,128]{1,0:T(8,128)} %get-tuple-element.11.rank_ref, f32[3,128,512]{2,1,0:T(8,128)} %get-tuple-element.12.state_in, ...), custom_call_target="tpu_custom_call" | custom-call | tf_op jit(solution)/shard_map/finish/pallas_call | solution.py:302

commit v6 on v5

--- a/solution.py
+++ b/solution.py
@@ -49,6 +49,9 @@
         ],
         1,
     ).astype(BF16)
+
+    q16 = iota((16, 128), 0)
+    kind = jnp.where(q16 >= 3, q16 - 3, q16)
 
     def tile(i, j, row, running):
         hit = d_iota == jnp.broadcast_to(dest_ref[pl.ds(row, 1), :], (128, 128))
@@ -71,16 +74,25 @@
             by = (pad_ref[1, bi, pl.ds(bj, 1), :] + (w % 3 - 1.0)) * KAPPA
             c0 = pad_ref[4, bi, pl.ds(bj, 1), :] * jnp.exp2(-bx * bx - by * by)
             c0 = c0 * (lax.shift_right_logical(listed, w + 1) & 1).astype(F32)
-            c1 = c0 * pad_ref[2, bi, pl.ds(bj, 1), :]
-            c2 = c0 * pad_ref[3, bi, pl.ds(bj, 1), :]
-            window.append((2.0 * bx, 2.0 * by, c0, c1, c2))
-        acc = [jnp.zeros((128, 128), F32)] * 3
-        for bx, by, *carried in window:
+            vx = pad_ref[2, bi, pl.ds(bj, 1), :]
+            vy = pad_ref[3, bi, pl.ds(bj, 1), :]
+            c_hi, c_lo = split2(
+                jnp.broadcast_to(c0, (16, 128))
+                * jnp.where(kind == 0, 1.0, jnp.where(kind == 1, vx, vy))
+            )
+            carried = jnp.where(q16 < 3, c_hi, jnp.where(q16 < 6, c_lo, 0.0)).astype(BF16)
+            window.append((2.0 * bx, 2.0 * by, carried))
+        left, right = [], []
+        for bx, by, carried in window:
             weights = jnp.exp2(x_col * bx + y_col * by)
-            acc = [total + weights * c for total, c in zip(acc, carried)]
+            hi = weights.astype(BF16)
+            left += [hi, (weights - hi.astype(F32)).astype(BF16)]
+            right += [carried, carried]
+        total = dot(jnp.concatenate(left, 1), jnp.concatenate(right, 1), NT)
+        total = jnp.concatenate([total, jnp.zeros((128, 112), F32)], 1).T
         scale = jnp.exp2(-x * x - y * y)
         for k in range(3):
-            sums_ref[k, pl.ds(i * cols + j, 1), :] = jnp.sum(acc[k].T, axis=0, keepdims=True) * scale
+            sums_ref[k, pl.ds(i * cols + j, 1), :] = (total[k : k + 1] + total[k + 3 : k + 4]) * scale
         return running
 
     return tile
@@ -295,7 +307,7 @@
             out_ref[k, at, :] = jnp.concatenate(found[k], 0)
         return carry
 
-    lax.fori_loop(0, dest_ref.shape[0] // 8, step, 0, unroll=2)
+    lax.fori_loop(0, dest_ref.shape[0] // 8, step, 0, unroll=4)
 
 
 def finish_call(back, dest, rank, state, density):
@@ -463,7 +475,7 @@
     return (cols >= 0) & (cols < nc * 512) & (rows >= 0) & (rows < na * 128)
 
 
-def water_step(old_ref, new_ref, depth_ref, source_ref):
+def water_step(old_ref, new_ref, depth_ref, source_ref=None):
     blocks = TALL // 8
     sub = iota((8, BROAD), 0)
 
@@ -496,7 +508,9 @@
         next_v = 0.25 * (v_e + v_w + right(v) + left(v)) - 0.5 * courant * (h_n - h_s)
         inside = inside_grid(block)
         for f, value in enumerate((next_h, next_u, next_v)):
-            new_ref[f, at, :] = jnp.where(inside, value + source_ref[f, at, :], 0.0)
+            if source_ref is not None:
+                value = value + source_ref[f, at, :]
+            new_ref[f, at, :] = jnp.where(inside, value, 0.0)
         before, here = here, after
 
 
@@ -562,7 +576,7 @@
         def one(n, running):
             return tile(row0 + n // inner, 1 + n % inner, base + n, running)
 
-        return lax.fori_loop(0, half * inner, one, running, unroll=2)
+        return lax.fori_loop(0, half * inner, one, running, unroll=7)
 
     running = inner_tiles(0, 1, jnp.zeros((128, 128), F32))
     pl.semaphore_wait(barrier, count - 1)
@@ -575,17 +589,15 @@
     place_particles(tile_ins, rows, cols, pad_ref)
     done = 2 * half * inner
 
-    def end_rows(n, running):
-        i = (n // cols) * (rows - 1)
-        return tile(i, n % cols, done + n, running)
-
-    running = lax.fori_loop(0, 2 * cols, end_rows, running, unroll=4)
-    done = done + 2 * cols
-
-    def end_columns(n, running):
-        return tile(1 + n // 2, (n % 2) * (cols - 1), done + n, running)
-
-    lax.fori_loop(0, 2 * (rows - 2), end_columns, running, unroll=2)
+    ends = 2 * cols
+
+    def outer_tiles(n, running):
+        late = n // ends
+        i = (1 - late) * (n // cols) * (rows - 1) + late * (1 + (n - ends) // 2)
+        j = (1 - late) * (n % cols) + late * (n % 2) * (cols - 1)
+        return tile(i, j, done + n, running)
+
+    lax.fori_loop(0, ends + 2 * (rows - 2), outer_tiles, running, unroll=6)
 
     for i in range(rows):
         at = slice(i * cols, (i + 1) * cols)
@@ -644,6 +656,7 @@
         for f in range(3):
             even[f, at, :] = jnp.where(inside_grid(b), even[f, at, :], 0.0)
 
+    water_step(even, odd, deep)
     for group in range(GROUPS):
         landed = got_ref.at[max(8, group * PER_GROUP * 8) : (group + 1) * PER_GROUP * 8, :]
         pltpu.make_async_copy(landed, landed, in_sem.at[group]).wait()
@@ -667,12 +680,14 @@
     for f in range(3):
         place_rims(wide_source, f, f, ins, [0, 0, 0])
 
-    def two_steps(n, carry):
+    for b in range(TALL // 8):
+        at = slice(b * 8, b * 8 + 8)
+        for f in range(3):
+            odd[f, at, :] = jnp.where(inside_grid(b), odd[f, at, :] + wide_source[f, at, :], 0.0)
+    water_step(odd, even, deep, wide_source)
+    for _ in range(SUBSTEPS // 2 - 1):
         water_step(even, odd, deep, wide_source)
         water_step(odd, even, deep, wide_source)
-        return carry
-
-    lax.fori_loop(0, SUBSTEPS // 2, two_steps, 0)
     keep = pltpu.make_async_copy(even.at[:, 0:128, 0:512], state_ref, state_sem)
     keep.start()
     undo = [lookup_table(even[k, 0:128, 0:512], k, high_ref, low_ref) for k in range(3)]

time: 112 us -> 109 us (0.973)
  Pallas kernels: 111 us -> 108 us
    pallas_call x1, Pallas kernels: 105 us -> 102 us  [main_call(): pl.pallas_call(main_kernel, out_shape=(jax.ShapeDtypeStruct((64, 128), F3...]
where the time goes in v6:
time: 109 us; the launch traced here: 108 us
  Pallas kernels  108 us (99%)
    pallas_call x1, Pallas kernels, main_call(): pl.pallas_call(main_kernel, out_shape=(jax.ShapeDtypeStruct((64, 128), F3...  102 us
    pallas_call x1, Pallas kernels, finish_call(): pl.pallas_call(finish_kernel, out_shape=(jax.ShapeDtypeStruct((3, 64, 128...  6.09 us

profile of v6, /device:TPU:1, one launch (start us, length us, event | category | flops | bytes accessed | tf_op | source)
XLA Modules:
  0.0 108.4 jit_solution(15086656287605119770)
XLA Ops:
  0.6 101.6 %main.1 = (f32[64,128]{1,0:T(8,128)}, f32[64,128]{1,0:T(8,128)}, f32[3,128,512]{2,1,0:T(8,128)}, f32[1024,128]{1,0:T(8,128)}) custom-call(f32[2,4,16,128]{3,2,1,0:T(8,128)} %off_ref.1, f32[2,4,16,128]{3,2,1,0:T(8,128)} %vel_ref.1, f32[4,16,128]{2,1,0:T(8,128)} %mass_ref.1, s32[9,4,16]{2,1,0:T(4,128)} %bitcast.8, s32[64,128]{1,0:T(8,128)} %bitcast.5, ...), custom_call_target="tpu_custom_call" | custom-call | tf_op jit(solution)/shard_map/main/pallas_call | solution.py:727
  102.3 6.1 %finish.1 = (f32[3,64,128]{2,1,0:T(8,128)}, f32[3,128,512]{2,1,0:T(8,128)}, f32[64,128]{1,0:T(8,128)}) custom-call(f32[1024,128]{1,0:T(8,128)} %get-tuple-element.10.back_ref, s32[64,128]{1,0:T(8,128)} %bitcast.6, f32[64,128]{1,0:T(8,128)} %get-tuple-element.11.rank_ref, f32[3,128,512]{2,1,0:T(8,128)} %get-tuple-element.12.state_in, ...), custom_call_target="tpu_custom_call" | custom-call | tf_op jit(solution)/shard_map/finish/pallas_call | solution.py:314

commit v7 on v6

--- a/solution.py
+++ b/solution.py
@@ -350,13 +350,13 @@
         slots_ref[k, 32:48, :] = full
 
 
-def deposit_group(group, slots_ref, cells_ref, left_ref, right_ref, acc_ref):
+def deposit_group(group, slots_ref, cells_ref, left_refs, right_refs, acc_ref):
     r_iota = iota((128, 128), 0).astype(F32)
     c_iota = iota((512, 128), 0).astype(F32)
     cells_ref[pl.ds(pl.multiple_of(group * 48, 8), 48), :] = slots_ref[0]
-
-    def step(g, carry):
-        at = pl.ds(pl.multiple_of(g * STEP, STEP), STEP)
+    for g in range(48 // STEP):
+        left_ref, right_ref = left_refs[g % 2], right_refs[g % 2]
+        at = slice(g * STEP, g * STEP + STEP)
         row8, col8 = row_and_column(slots_ref[0, at, :])
         vals8 = [split8(slots_ref[1 + k, at, :] * 0.5) for k in range(3)]
         for r in range(STEP):
@@ -371,9 +371,6 @@
                 c_iota == jnp.broadcast_to(col8[r : r + 1], (512, 128)), 1.0, 0.0
             ).astype(F8)
         acc_ref[...] += dot(left_ref[...], right_ref[...], NT)
-        return carry
-
-    lax.fori_loop(0, 48 // STEP, step, 0)
 
 
 def deposit_sum(acc_ref, k):
@@ -519,14 +516,14 @@
     dens_ref, rank_ref, state_ref, back_got,
     pad_ref,
     sums_ref, vals_ref, pleft_ref, pslots_ref, pacc_ref, send_ref, got_ref,
-    slots_ref, cells_ref, left_ref, right_ref, acc_ref,
+    slots_ref, cells_ref, left0, left1, right0, right1, acc_ref,
     even, odd, deep, wide_source,
     high_ref, low_ref, found_ref, back_ref,
     o0, o1, o2, o3, o4, o5, o6, o7, i0, i1, i2, i3, i4, i5, i6, i7,
     q0, q1, q2, q3, q4, q5, q6, q7, g0, g1, g2, g3, g4, g5, g6, g7,
     r0, r1, r2, r3, r4, r5, r6, r7, t0, t1, t2, t3, t4, t5, t6, t7,
     rim_send, rim_recv, first_send, first_recv, tile_send, tile_recv,
-    out_sem, in_sem, back_out_sem, back_in_sem, state_sem,
+    out_sem, in_sem, back_out_sem, back_in_sem, state_sem, fill_sem,
 ):
     (a, c), (na, nc) = my_place(), sizes()
     count = na * nc
@@ -550,6 +547,12 @@
 
         lax.fori_loop(max(first, 1), last, along, 0)
 
+    fill = [
+        pltpu.make_async_copy(surface_ref, even.at[:, 0:128, 0:512], fill_sem.at[0]),
+        pltpu.make_async_copy(depth_ref, deep.at[0, 0:128, 0:512], fill_sem.at[1]),
+    ]
+    for copy in fill:
+        copy.start()
     barrier = pltpu.get_barrier_semaphore()
 
     def greet(along, across):
@@ -629,22 +632,21 @@
 
     for group in range(GROUPS):
         send_out(group)
-    got_ref[0:8, :] = send_ref[block(me), :]
+    pltpu.make_async_copy(send_ref.at[block(me), :], got_ref.at[0:8, :], in_sem.at[0]).start()
 
     first_outs = [q0, q1, q2, q3, q4, q5, q6, q7]
     first_ins = [g0, g1, g2, g3, g4, g5, g6, g7]
+    for copy in fill:
+        copy.wait()
     write_rims(first_outs, [0, 0, 0, 0, 0], [
-        lambda r, c: surface_ref[0, r, c],
-        lambda r, c: surface_ref[1, r, c],
-        lambda r, c: surface_ref[2, r, c],
-        lambda r, c: depth_ref[r, c],
+        lambda r, c: even[0, r, c],
+        lambda r, c: even[1, r, c],
+        lambda r, c: even[2, r, c],
+        lambda r, c: deep[0, r, c],
     ])
     copies = rim_copies(first_outs, first_ins, first_send, first_recv)
     for copy in copies:
         copy.start()
-    for f in range(3):
-        even[f, 0:128, 0:512] = surface_ref[f]
-    deep[0, 0:128, 0:512] = depth_ref[...]
     acc_ref[...] = jnp.zeros_like(acc_ref)
     for copy in copies:
         copy.wait()
@@ -657,11 +659,15 @@
             even[f, at, :] = jnp.where(inside_grid(b), even[f, at, :], 0.0)
 
     water_step(even, odd, deep)
-    for group in range(GROUPS):
-        landed = got_ref.at[max(8, group * PER_GROUP * 8) : (group + 1) * PER_GROUP * 8, :]
+    def take_group(group, carry):
+        span = PER_GROUP * 8
+        landed = got_ref.at[pl.ds(pl.multiple_of(group * span, span), span), :]
         pltpu.make_async_copy(landed, landed, in_sem.at[group]).wait()
         unfold(got_ref, slots_ref, group)
-        deposit_group(group, slots_ref, cells_ref, left_ref, right_ref, acc_ref)
+        deposit_group(group, slots_ref, cells_ref, [left0, left1], [right0, right1], acc_ref)
+        return carry
+
+    lax.fori_loop(0, GROUPS, take_group, 0)
     for k in range(3):
         wide_source[k, 0:128, 0:512] = deposit_sum(acc_ref, k)
 
@@ -732,7 +738,10 @@
             jax.ShapeDtypeStruct((3, 128, 512), F32),
             jax.ShapeDtypeStruct((1024, 128), F32),
         ),
-        in_specs=[vmem()] * 3 + [pl.BlockSpec(memory_space=pltpu.SMEM)] + [vmem()] * 4,
+        in_specs=[vmem()] * 3
+        + [pl.BlockSpec(memory_space=pltpu.SMEM)]
+        + [vmem()] * 2
+        + [anywhere] * 2,
         out_specs=(vmem(), vmem(), anywhere, vmem()),
         scratch_shapes=[
             pltpu.VMEM((5, rows + 2, cols + 2, 128), F32),
@@ -746,6 +755,8 @@
             pltpu.VMEM((4, 48, 128), F32),
             pltpu.VMEM((192, 128), F32),
             pltpu.VMEM((1152, STEP * 128), F8),
+            pltpu.VMEM((1152, STEP * 128), F8),
+            pltpu.VMEM((512, STEP * 128), F8),
             pltpu.VMEM((512, STEP * 128), F8),
             pltpu.VMEM((1152, 512), F32),
             pltpu.VMEM((3, TALL, BROAD), F32),
@@ -773,6 +784,7 @@
             dma,
             dma,
             dma,
+            dma((2,)),
         ],
         compiler_params=pltpu.CompilerParams(
             vmem_limit_bytes=VMEM_LIMIT, collective_id=1, has_side_effects=True

time: 109 us -> 107 us (0.982)
  Pallas kernels: 108 us -> 106 us
    pallas_call x1, Pallas kernels: 102 us -> 99.8 us  [main_call(): pl.pallas_call(main_kernel, out_shape=(jax.ShapeDtypeStruct((64, 128), F3...]
where the time goes in v7:
time: 107 us; the launch traced here: 106 us
  Pallas kernels  106 us (99%)
    pallas_call x1, Pallas kernels, main_call(): pl.pallas_call(main_kernel, out_shape=(jax.ShapeDtypeStruct((64, 128), F3...  99.8 us
    pallas_call x1, Pallas kernels, finish_call(): pl.pallas_call(finish_kernel, out_shape=(jax.ShapeDtypeStruct((3, 64, 128...  6.09 us

profile of v7, /device:TPU:1, one launch (start us, length us, event | category | flops | bytes accessed | tf_op | source)
XLA Modules:
  0.0 106.5 jit_solution(7981726719866488497)
XLA Ops:
  0.6 99.8 %main.1 = (f32[64,128]{1,0:T(8,128)}, f32[64,128]{1,0:T(8,128)}, f32[3,128,512]{2,1,0:T(8,128)}, f32[1024,128]{1,0:T(8,128)}) custom-call(f32[2,4,16,128]{3,2,1,0:T(8,128)} %off_ref.1, f32[2,4,16,128]{3,2,1,0:T(8,128)} %vel_ref.1, f32[4,16,128]{2,1,0:T(8,128)} %mass_ref.1, s32[9,4,16]{2,1,0:T(4,128)} %bitcast.8, s32[64,128]{1,0:T(8,128)} %bitcast.5, ...), custom_call_target="tpu_custom_call" | custom-call | tf_op jit(solution)/shard_map/main/pallas_call | solution.py:733
  100.4 6.1 %finish.1 = (f32[3,64,128]{2,1,0:T(8,128)}, f32[3,128,512]{2,1,0:T(8,128)}, f32[64,128]{1,0:T(8,128)}) custom-call(f32[1024,128]{1,0:T(8,128)} %get-tuple-element.10.back_ref, s32[64,128]{1,0:T(8,128)} %bitcast.6, f32[64,128]{1,0:T(8,128)} %get-tuple-element.11.rank_ref, f32[3,128,512]{2,1,0:T(8,128)} %get-tuple-element.12.state_in, ...), custom_call_target="tpu_custom_call" | custom-call | tf_op jit(solution)/shard_map/finish/pallas_call | solution.py:314

commit v8 on v7

--- a/solution.py
+++ b/solution.py
@@ -307,7 +307,7 @@
             out_ref[k, at, :] = jnp.concatenate(found[k], 0)
         return carry
 
-    lax.fori_loop(0, dest_ref.shape[0] // 8, step, 0, unroll=4)
+    lax.fori_loop(0, dest_ref.shape[0] // 8, step, 0, unroll=8)
 
 
 def finish_call(back, dest, rank, state, density):
@@ -389,7 +389,7 @@
     return most * (1.0 / 1024.0)
 
 
-def lookup_group(group, cells_ref, high_ref, low_ref, undo, found_ref, back_ref):
+def lookup_group(group, cells_ref, high_ref, low_ref, undo, found_ref, back_ref, beside, steps):
     r_iota = iota((128, 128), 0).astype(F32)
     c_iota = iota((512, 128), 0).astype(F32)
 
@@ -418,7 +418,13 @@
             )
         return carry
 
-    lax.fori_loop(0, 6, step, 0)
+    def step_beside(g, carry):
+        beside(g)
+        return step(g, carry)
+
+    if steps:
+        lax.fori_loop(0, steps, step_beside, 0)
+    lax.fori_loop(steps, 6, step, 0)
     low_half = iota((16, 128), 1) < 64
     first_row = group * PER_GROUP * 8
     tails = [found_ref[k, 32:48, :] for k in range(3)]
@@ -698,20 +704,31 @@
     keep.start()
     undo = [lookup_table(even[k, 0:128, 0:512], k, high_ref, low_ref) for k in range(3)]
 
+    def send_back(along, across):
+        pltpu.make_async_remote_copy(
+            src_ref=back_ref.at[block(along * nc + across), :],
+            dst_ref=back_got.at[block(me), :],
+            send_sem=back_out_sem,
+            recv_sem=back_in_sem,
+            device_id=(lax.rem(a - along + na, na), behind[across]),
+            device_id_type=MESH,
+        ).start()
+
     for group in range(GROUPS):
-        lookup_group(group, cells_ref, high_ref, low_ref, undo, found_ref, back_ref)
-
-        def start(along, across):
-            pltpu.make_async_remote_copy(
-                src_ref=back_ref.at[block(along * nc + across), :],
-                dst_ref=back_got.at[block(me), :],
-                send_sem=back_out_sem,
-                recv_sem=back_in_sem,
-                device_id=(lax.rem(a - along + na, na), behind[across]),
-                device_id_type=MESH,
-            ).start()
-
-        each_other(group * per_group, (group + 1) * per_group, start)
+        ready = (group - 1) * per_group
+        if group == 1:
+            each_other(0, 1, send_back)
+            ready = 1
+
+        def beside(step):
+            for across in range(nc):
+                send_back(ready + step, across)
+
+        lookup_group(
+            group, cells_ref, high_ref, low_ref, undo, found_ref, back_ref,
+            beside, max(0, group * per_group - ready) if group else 0,
+        )
+    each_other((GROUPS - 1) * per_group, na, send_back)
     back_got[block(me), :] = back_ref[0:8, :]
     others = (count - 1) * 8
     for ref, sem in (

time: 107 us -> 107 us (level)
  no operation moved by 1% of the time
where the time goes in v8:
time: 107 us
  Pallas kernels  106 us (99%)
    pallas_call x1, Pallas kernels, main_call(): pl.pallas_call(main_kernel, out_shape=(jax.ShapeDtypeStruct((64, 128), F3...  99.9 us
    pallas_call x1, Pallas kernels, finish_call(): pl.pallas_call(finish_kernel, out_shape=(jax.ShapeDtypeStruct((3, 64, 128...  6.14 us

profile of v8, /device:TPU:1, one launch (start us, length us, event | category | flops | bytes accessed | tf_op | source)
XLA Modules:
  0.0 106.7 jit_solution(9970472733525404880)
XLA Ops:
  0.6 99.9 %main.1 = (f32[64,128]{1,0:T(8,128)}, f32[64,128]{1,0:T(8,128)}, f32[3,128,512]{2,1,0:T(8,128)}, f32[1024,128]{1,0:T(8,128)}) custom-call(f32[2,4,16,128]{3,2,1,0:T(8,128)} %off_ref.1, f32[2,4,16,128]{3,2,1,0:T(8,128)} %vel_ref.1, f32[4,16,128]{2,1,0:T(8,128)} %mass_ref.1, s32[9,4,16]{2,1,0:T(4,128)} %bitcast.8, s32[64,128]{1,0:T(8,128)} %bitcast.5, ...), custom_call_target="tpu_custom_call" | custom-call | tf_op jit(solution)/shard_map/main/pallas_call | solution.py:750
  100.6 6.1 %finish.1 = (f32[3,64,128]{2,1,0:T(8,128)}, f32[3,128,512]{2,1,0:T(8,128)}, f32[64,128]{1,0:T(8,128)}) custom-call(f32[1024,128]{1,0:T(8,128)} %get-tuple-element.10.back_ref, s32[64,128]{1,0:T(8,128)} %bitcast.6, f32[64,128]{1,0:T(8,128)} %get-tuple-element.11.rank_ref, f32[3,128,512]{2,1,0:T(8,128)} %get-tuple-element.12.state_in, ...), custom_call_target="tpu_custom_call" | custom-call | tf_op jit(solution)/shard_map/finish/pallas_call | solution.py:314
